TPU v7x, 32 devices: a whole 2x2x4 slice. The times are simulated.
32 devices in a mesh: mem: 8 (over y, x, core), head: 4 (over z).
Axes of the slice: x: 2, y: 2, z: 4, core: 2. Of those that a mesh axis runs over, the one named last changes fastest.
Arguments:
- queries: bfloat16 [4096, 6144], P(('mem', 'head')), may hold values from -18 to 18
- keys_local: bfloat16 [4096, 6144], P(('mem', 'head')), may hold values from -15 to 15
- values_local: bfloat16 [4096, 6144], P(('mem', 'head')), may hold values from -6 to 6
- cache_keys: bfloat16 [4096, 6144], P('mem', 'head'), may hold values from -6 to 6
- cache_values: bfloat16 [4096, 6144], P('mem', 'head'), may hold values from -6 to 6
- block_map: int32 [64], replicated, may hold values from 0 to 63, as said below
- retrieved: int32 [64, 16, 4], P('mem', 'head'), may hold values from 0 to 63, as said below
- out_grad: bfloat16 [4096, 6144], P(('mem', 'head')), may hold values from -24 to 24
Outputs:
- grad_queries: bfloat16 [4096, 6144], P(('mem', 'head'))
- grad_keys_local: bfloat16 [4096, 6144], P(('mem', 'head'))
- grad_values_local: bfloat16 [4096, 6144], P(('mem', 'head'))
- grad_cache_keys: bfloat16 [4096, 6144], P('mem', 'head')
- grad_cache_values: bfloat16 [4096, 6144], P('mem', 'head')
Inputs may be any that keep to these rules, and one draw needn't show every extreme that they name: block_map is a permutation of the block ids; block b is stored as block block_map[b] % 8 of index block_map[b] // 8 of mem. `retrieved`: for each head group and each aligned run of 8 query blocks, the 32 ids are distinct and at most 5 of them are stored on one index of mem; in every draw some index of mem stores exactly 5 of them for every run and every group.
All inputs are finite; a program needn't handle non-finite values.
Results may differ from a plain program's by a relative error of at most 0.012.
The roundings to bfloat16 on the way count: a program that leaves them out, or rounds other values in their place, can miss the bound.
Values may be sent and summed in bfloat16 or wider, within the bound.
No kernel may reach another device: no remote copies, remote signals or barrier semaphores. Data moves between devices by JAX's collectives and lax.ppermute only.
A program may use at most 256 MiB of HBM per device.

v0:
```python
import math

import jax
import jax.numpy as jnp
from jax import lax
from jax.sharding import PartitionSpec as P

HEAD_DIM = 128
GROUP_HEADS = 3
BLOCK = 64
READS = 4
WINDOW = 512


def from_behind(array, axis, by):
    size = lax.axis_size(axis)
    pairs = [(i, i + by) for i in range(size) if 0 <= i + by < size]
    return lax.ppermute(array, axis, pairs)


def lookup_storage(block_map, retrieved):
    all_ids = jnp.arange(block_map.shape[0], dtype=jnp.int32)
    matches = retrieved[..., None] == all_ids
    return jnp.sum(jnp.where(matches, block_map, 0), axis=-1)


def serve_blocks(cache, slot_table, groups, group_width):
    blocks = cache.reshape(cache.shape[0] // BLOCK, BLOCK, groups, group_width)
    return jnp.einsum("sgcl,ltgw->sgctw", slot_table, blocks, preferred_element_type=jnp.bfloat16)


def per_device(
    queries, keys_local, values_local, cache_keys, cache_values, block_map, retrieved, out_grad
):
    q_all, k_all, v_all, dout_all = (
        lax.all_to_all(queries, "head", split_axis=1, concat_axis=0, tiled=True),
        lax.all_to_all(keys_local, "head", split_axis=1, concat_axis=0, tiled=True),
        lax.all_to_all(values_local, "head", split_axis=1, concat_axis=0, tiled=True),
        lax.all_to_all(out_grad, "head", split_axis=1, concat_axis=0, tiled=True),
    )
    group_width = GROUP_HEADS * HEAD_DIM
    features = q_all.shape[1]
    groups = features // group_width
    tok_rows = q_all.shape[0]
    num_blocks = tok_rows // BLOCK
    mem_span = READS * BLOCK
    mem_count = lax.axis_size("mem")
    mem_index = lax.axis_index("mem")
    req_count = num_blocks * READS
    capacity = max(2, (5 * req_count + 4 * mem_count - 1) // (4 * mem_count))
    seq_len = tok_rows * min(8, mem_count)
    scaling = 1.0 / math.sqrt(HEAD_DIM)
    blk_dev = cache_keys.shape[0] // BLOCK
    key_count = WINDOW + tok_rows
    storage = lookup_storage(block_map, retrieved)
    wanted = jnp.transpose(storage, (1, 0, 2)).reshape(groups, req_count)
    owners = wanted // blk_dev
    local_block = wanted % blk_dev
    positions = jnp.arange(req_count)
    same_owner = (owners[:, :, None] == owners[:, None, :]) & (
        positions[None, None, :] < positions[None, :, None]
    )
    copy_rank = jnp.sum(same_owner.astype(jnp.int32), axis=-1)
    slot_hit = (owners[:, :, None, None] == jnp.arange(mem_count)[:, None]) & (
        copy_rank[:, :, None, None] == jnp.arange(capacity)
    )
    slot_select = slot_hit.astype(jnp.bfloat16)
    requests = jnp.sum(jnp.where(slot_hit, local_block[:, :, None, None] + 1, 0), axis=1) - 1
    requests = jnp.transpose(requests, (1, 0, 2))
    asked_slots = lax.all_to_all(requests, "mem", split_axis=0, concat_axis=0, tiled=True)
    one_hot = (asked_slots[..., None] == jnp.arange(blk_dev)).astype(jnp.bfloat16)
    served_k = serve_blocks(cache_keys, one_hot, groups, group_width)
    served_v = serve_blocks(cache_values, one_hot, groups, group_width)
    fetched_k, fetched_v = (
        lax.all_to_all(served_k, "mem", split_axis=0, concat_axis=0, tiled=True),
        lax.all_to_all(served_v, "mem", split_axis=0, concat_axis=0, tiled=True),
    )

    def unpack(fetched):
        picked = jnp.einsum(
            "grsc,sgctw->grtw", slot_select, fetched, preferred_element_type=jnp.bfloat16
        )
        return picked.reshape(groups, num_blocks, mem_span, GROUP_HEADS, HEAD_DIM)

    mem_k = unpack(fetched_k)
    tail_rows = (k_all, v_all)
    before_k, before_v = from_behind((tail_rows[0], tail_rows[1]), "mem", 1)
    head_four = (tok_rows, groups, GROUP_HEADS, HEAD_DIM)
    ext_k = jnp.concatenate([before_k, k_all], 0).reshape(key_count, groups, GROUP_HEADS, HEAD_DIM)
    ext_v = jnp.concatenate([before_v, v_all], 0).reshape(key_count, groups, GROUP_HEADS, HEAD_DIM)
    query_four = q_all.reshape(head_four)
    grad_four = dout_all.reshape(head_four)
    shape_five = (num_blocks, BLOCK, groups, GROUP_HEADS, HEAD_DIM)
    query_heads = q_all.reshape(shape_five)
    grad_heads = dout_all.reshape(shape_five)
    split = (groups, GROUP_HEADS, num_blocks, BLOCK)
    flat = (groups, GROUP_HEADS, tok_rows)
    query_pos = mem_index * tok_rows + jnp.arange(tok_rows)
    key_pos = mem_index * tok_rows - WINDOW + jnp.arange(key_count)
    allowed = (
        (key_pos[None, :] <= query_pos[:, None])
        & (key_pos[None, :] >= query_pos[:, None] - WINDOW)
        & (key_pos[None, :] >= (query_pos // seq_len * seq_len)[:, None])
    )
    score_loc = (
        jnp.einsum("igkd,jgkd->gkij", query_four, ext_k, preferred_element_type=jnp.float32)
        * scaling
    )
    score_loc = jnp.where(allowed[None, None], score_loc, -jnp.inf)
    score_mem = (
        jnp.einsum("bigkd,gbjkd->gkbij", query_heads, mem_k, preferred_element_type=jnp.float32)
        * scaling
    )
    row_max = jnp.maximum(jnp.max(score_loc, -1).reshape(split), jnp.max(score_mem, -1))
    exp_loc = jnp.exp(score_loc - row_max.reshape(flat)[..., None])
    exp_mem = jnp.exp(score_mem - row_max[..., None])
    totals = jnp.sum(exp_loc, -1).reshape(split) + jnp.sum(exp_mem, -1)
    prob_loc = exp_loc / totals.reshape(flat)[..., None]
    prob_mem = exp_mem / totals[..., None]
    weight_loc = prob_loc.astype(jnp.bfloat16)
    weight_mem = prob_mem.astype(jnp.bfloat16)
    mem_v = unpack(fetched_v)
    attended = jnp.einsum(
        "gkij,jgkd->igkd", weight_loc, ext_v, preferred_element_type=jnp.float32
    ) + jnp.einsum(
        "gkbij,gbjkd->bigkd", weight_mem, mem_v, preferred_element_type=jnp.float32
    ).reshape(
        head_four
    )
    deltas = jnp.transpose(jnp.sum(grad_four.astype(jnp.float32) * attended, -1), (1, 2, 0))
    delta_loc = deltas[..., None]
    delta_mem = deltas.reshape(split)[..., None]

    def place_slots(grads):
        return jnp.einsum(
            "grsc,grtw->sgctw", slot_select, grads, preferred_element_type=jnp.bfloat16
        )

    read_dv = (
        jnp.einsum("gkbij,bigkd->gbjkd", weight_mem, grad_heads, preferred_element_type=jnp.float32)
        .astype(jnp.bfloat16)
        .reshape(groups, req_count, BLOCK, group_width)
    )
    slots_v = place_slots(read_dv)
    dprob_loc = jnp.einsum("igkd,jgkd->gkij", grad_four, ext_v, preferred_element_type=jnp.float32)
    dprob_mem = jnp.einsum(
        "bigkd,gbjkd->gkbij", grad_heads, mem_v, preferred_element_type=jnp.float32
    )
    dscore_loc = (prob_loc * (dprob_loc - delta_loc)).astype(jnp.bfloat16)
    dscore_mem = (prob_mem * (dprob_mem - delta_mem)).astype(jnp.bfloat16)
    grad_q = (
        (
            scaling
            * (
                jnp.einsum("gkij,jgkd->igkd", dscore_loc, ext_k, preferred_element_type=jnp.float32)
                + jnp.einsum(
                    "gkbij,gbjkd->bigkd", dscore_mem, mem_k, preferred_element_type=jnp.float32
                ).reshape(head_four)
            )
        )
        .astype(jnp.bfloat16)
        .reshape(tok_rows, features)
    )
    key_grads = (
        scaling
        * jnp.einsum("gkij,igkd->jgkd", dscore_loc, query_four, preferred_element_type=jnp.float32)
    ).reshape(key_count, features)
    value_grads = jnp.einsum(
        "gkij,igkd->jgkd", weight_loc, grad_four, preferred_element_type=jnp.float32
    ).reshape(key_count, features)
    back_k, back_v = from_behind((key_grads[:WINDOW], value_grads[:WINDOW]), "mem", -1)
    tail_start = tok_rows - WINDOW
    grad_k = key_grads[WINDOW:].at[tail_start:].add(back_k).astype(jnp.bfloat16)
    grad_v = value_grads[WINDOW:].at[tail_start:].add(back_v).astype(jnp.bfloat16)
    read_dk = (
        (
            scaling
            * jnp.einsum(
                "gkbij,bigkd->gbjkd", dscore_mem, query_heads, preferred_element_type=jnp.float32
            )
        )
        .astype(jnp.bfloat16)
        .reshape(groups, req_count, BLOCK, group_width)
    )
    slots_k = place_slots(read_dk)
    returned_k, returned_v = (
        lax.all_to_all(slots_k, "mem", split_axis=0, concat_axis=0, tiled=True),
        lax.all_to_all(slots_v, "mem", split_axis=0, concat_axis=0, tiled=True),
    )

    def stored_sum(returned):
        summed = jnp.einsum(
            "sgcl,sgctw->ltgw", one_hot, returned, preferred_element_type=jnp.float32
        )
        return summed.reshape(blk_dev * BLOCK, groups * group_width).astype(jnp.bfloat16)

    grad_cache_k = stored_sum(returned_k)
    grad_cache_v = stored_sum(returned_v)
    tok_q, tok_k, tok_v = (
        lax.all_to_all(grad_q, "head", split_axis=0, concat_axis=1, tiled=True),
        lax.all_to_all(grad_k, "head", split_axis=0, concat_axis=1, tiled=True),
        lax.all_to_all(grad_v, "head", split_axis=0, concat_axis=1, tiled=True),
    )
    return (tok_q, tok_k, tok_v, grad_cache_k, grad_cache_v)


def solution(mesh):
    placed = (
        P(("mem", "head"), None),
        P(("mem", "head"), None),
        P(("mem", "head"), None),
        P("mem", "head"),
        P("mem", "head"),
        P(),
        P("mem", "head", None),
        P(("mem", "head"), None),
    )
    return jax.shard_map(
        per_device,
        mesh=mesh,
        in_specs=placed,
        out_specs=(
            P(("mem", "head"), None),
            P(("mem", "head"), None),
            P(("mem", "head"), None),
            P("mem", "head"),
            P("mem", "head"),
        ),
        check_vma=False,
    )
```

profile of v0, /device:TPU:0, one launch (start us, length us, event | category | flops | bytes accessed | tf_op | source)
XLA Modules:
  0.0 924.0 jit_solution(12761290820925803016)
XLA Ops:
  3.4 5.2 all-to-all-start.2
  13.3 4.9 all-to-all-start.1
  20.8 34.3 %all-to-all-done.1 = bf16[128,4,1536]{2,0,1:T(8,128)(2,1)S(1)} async-done(((bf16[128,4,1536]{2,0,1:T(8,128)(2,1)}), bf16[128,4,1536]{2,0,1:T(8,128)(2,1)S(1)}, u32[]{:S(2)}, u32[]{:S(2)}) %all-to-all-start.1) | async-done | bytes 1572896 | tf_op jit(solution)/shard_map/all_to_all | solution.py:36
  55.1 4.4 all-to-all-start
  62.2 33.8 %all-to-all-done = bf16[128,4,1536]{0,2,1:T(8,128)(2,1)} async-done(((bf16[128,4,1536]{0,2,1:T(8,128)(2,1)}), bf16[128,4,1536]{0,2,1:T(8,128)(2,1)}, u32[]{:S(2)}, u32[]{:S(2)}) %all-to-all-start) | async-done | bytes 1572896 | tf_op jit(solution)/shard_map/all_to_all | solution.py:37
  96.0 4.4 all-to-all-start.5
  102.9 33.9 %all-to-all-done.5 = bf16[128,4,1536]{2,0,1:T(8,128)(2,1)} async-done(((bf16[128,4,1536]{2,0,1:T(8,128)(2,1)}), bf16[128,4,1536]{2,0,1:T(8,128)(2,1)}, u32[]{:S(2)}, u32[]{:S(2)}) %all-to-all-start.5) | async-done | bytes 1572896 | tf_op jit(solution)/shard_map/all_to_all | solution.py:39
  136.9 4.3 all-to-all-start.4
  141.2 3.9 reshape.442
  146.1 3.8 convolution_bitcast_fusion.1
  149.9 4.7 copy.404
  154.6 23.2 %all-to-all-done.4 = bf16[128,4,1536]{0,2,1:T(8,128)(2,1)} async-done(((bf16[128,4,1536]{0,2,1:T(8,128)(2,1)}), bf16[128,4,1536]{0,2,1:T(8,128)(2,1)}, u32[]{:S(2)}, u32[]{:S(2)}) %all-to-all-start.4) | async-done | bytes 1572896 | tf_op jit(solution)/shard_map/all_to_all | solution.py:38
  177.7 4.9 all-to-all-start.3
  182.6 3.9 reshape.447
  190.4 4.7 copy.428
  195.0 76.0 %all-to-all-done.3 = bf16[8,4,5,64,384]{4,3,2,1,0:T(8,128)(2,1)} async-done(((bf16[8,4,5,64,384]{4,3,2,1,0:T(8,128)(2,1)}), bf16[8,4,5,64,384]{4,3,2,1,0:T(8,128)(2,1)}, u32[]{:S(2)}, u32[]{:S(2)}) %all-to-all-start.3) | async-done | bytes 7864352 | tf_op jit(solution)/shard_map/all_to_all | solution.py:75
  271.1 5.1 all-to-all-start.6
  289.9 8.5 copy.393
  303.0 8.6 copy.418
  315.3 5.7 reshape.451
  327.7 3.9 reshape.446
  342.9 12.1 %fusion.3 = (f32[4,3,512]{2,1,0:T(4,128)S(1)}, f32[4,3,1024,512]{3,2,1,0:T(8,128)}) fusion(pred[512,1024]{0,1:T(8,128)(4,1)} %compare_and_fusion, bf16[512,4,3,128]{0,3,2,1:T(8,128)(2,1)S(1)} %reshape.440, bf16[512,4,3,128]{3,0,2,1:T(8,128)(2,1)S(1)} %copy.395, bf16[512,4,3,128]{3,0,2,1:T(8,128)(2,1)} %copy.394), kind=kOutput, calls=%fused_computation.6 | convolution fusion | flops 1635772416 | bytes 30433280 | tf_op jit(solution)/shard_map/igkd,jgkd->gkij/dot_general | solution.py:106
  358.4 8.6 fusion.52
  367.1 5.0 copy.406
  372.1 16.8 %reshape.443 = bf16[4,8,256,3,128]{4,3,2,1,0:T(4,128)(2,1)} reshape(bf16[4,32,64,384]{3,2,1,0:T(8,128)(2,1)} %copy.406) | data formatting | bytes 12582912 | tf_op jit(solution)/shard_map/reshape | solution.py:83
  388.9 8.6 fusion.55
  397.5 5.1 copy.430
  402.6 16.8 %reshape.448 = bf16[4,8,256,3,128]{4,3,2,1,0:T(4,128)(2,1)} reshape(bf16[4,32,64,384]{3,2,1,0:T(8,128)(2,1)} %copy.430) | data formatting | bytes 12582912 | tf_op jit(solution)/shard_map/reshape | solution.py:83
  419.4 8.5 bitcast_reduce_fusion
  428.0 11.2 %fusion.2 = f32[4,3,512]{2,1,0:T(4,128)S(1)} fusion(f32[4,3,1024,512]{3,2,1,0:T(8,128)} %get-tuple-element.72, f32[4,3,512]{2,1,0:T(4,128)S(1)} %max.13, pred[512,1024]{0,1:T(8,128)(4,1)S(1)} %copy-done.9), kind=kLoop, calls=%fused_computation.5 | loop fusion | flops 25159680 | bytes 25739264 | tf_op jit(solution)/shard_map/reduce_sum | solution.py:117
  439.3 4.0 fusion.32
  443.4 4.4 fusion.86
  447.9 5.7 fusion.60
  456.4 14.6 %fusion.42 = f32[512,4,3]{0,2,1:T(4,128)S(1)} fusion(f32[512,4,3,128]{0,3,2,1:T(8,128)} %copy.436, bf16[512,4,3,128]{0,3,2,1:T(8,128)(2,1)} %reshape.446, bf16[512,4,3,128]{3,0,2,1:T(8,128)(2,1)} %copy.420, bf16[512,4,3,128]{3,0,2,1:T(8,128)(2,1)} %copy.419, f32[4,3,1024,512]{3,2,1,0:T(8,128)} %get-tuple-element.72, f32[4,3,512]{2,1,0:T(4,128)S(1)} %add.118, ...), kind=kOutput, calls=%fused_computation.55 | convolution fusion | flops 1651501056 | bytes 33628160 | tf_op jit(solution)/shard_map/gkij,jgkd->igkd/dot_general | solution.py:123
  471.1 18.3 %fusion = bf16[4,3,512,1024]{2,3,1,0:T(8,128)(2,1)} fusion(f32[4,3,512]{2,1,0:T(4,128)S(1)} %bitcast.215, bf16[512,4,3,128]{0,3,2,1:T(8,128)(2,1)} %reshape.446, bf16[512,4,3,128]{3,0,2,1:T(8,128)(2,1)} %copy.420, bf16[512,4,3,128]{3,0,2,1:T(8,128)(2,1)} %copy.419, f32[4,3,512]{2,1,0:T(4,128)S(1)} %add.118, f32[4,3,512]{2,1,0:T(4,128)S(1)} %max.13, ...), kind=kOutput, calls=%fused_computation.1 | convolution fusion | flops 1660944384 | bytes 43065344 | tf_op jit(solution)/shard_map/igkd,jgkd->gkij/dot_general | solution.py:145
  489.4 7.6 fusion.17
  497.0 5.7 fusion.65
  507.1 11.8 %multiply_bitcast_fusion = f32[1024,4,3,128]{0,3,2,1:T(8,128)} fusion(bf16[4,3,512,1024]{2,3,1,0:T(8,128)(2,1)} %fusion, bf16[512,4,3,128]{0,3,2,1:T(8,128)(2,1)} %copy-done.6), kind=kOutput, calls=%fused_computation.35 | convolution fusion | flops 1612185600 | bytes 20447232 | tf_op jit(solution)/shard_map/gkij,igkd->jgkd/dot_general | solution.py:166
  518.9 8.7 fusion.40
  531.3 4.4 all-to-all-start.7
  535.7 5.5 fusion.110
  544.9 14.1 %fusion.47 = f32[1024,4,3,128]{0,3,2,1:T(8,128)} fusion(bf16[512,4,3,128]{0,3,2,1:T(8,128)(2,1)} %reshape.446, f32[4,3,1024,512]{3,2,1,0:T(8,128)} %get-tuple-element.72, f32[4,3,512]{2,1,0:T(4,128)S(1)} %add.118, f32[4,3,512]{2,1,0:T(4,128)S(1)} %max.13, pred[512,1024]{0,1:T(8,128)(4,1)} %compare_and_fusion), kind=kOutput, calls=%fused_computation.62 | convolution fusion | flops 1642070016 | bytes 33603584 | tf_op jit(solution)/shard_map/gkij,igkd->jgkd/dot_general | solution.py:168
  559.0 5.5 fusion.109
  574.5 17.4 %collective-permute-done.2 = f32[512,1536]{1,0:T(8,128)} collective-permute-done((f32[512,1536]{1,0:T(8,128)}, f32[512,1536]{1,0:T(8,128)}, u32[]{:S(2)}, u32[]{:S(2)}) %collective-permute-start.2) | collective-permute-done | bytes 3145760 | tf_op jit(solution)/shard_map/ppermute | solution.py:18
  596.7 4.8 all-to-all-start.8
  607.6 8.2 collective-permute-done.3
  615.8 4.4 add_convert_fusion
  623.1 4.6 all-to-all-start.9
  627.7 7.1 fusion.12
  634.8 12.0 %copy.458 = bf16[4,8,256,3,128]{4,3,2,1,0:T(4,128)(2,1)} copy(bf16[4,8,256,3,128]{4,2,3,1,0:T(8,128)(2,1)} %fusion.12) | data formatting | bytes 12582912 | tf_op jit(solution)/shard_map/convert_element_type | solution.py:182
  646.8 17.0 %reshape.455 = bf16[4,32,64,384]{3,2,1,0:T(8,128)(2,1)} reshape(bf16[4,8,256,3,128]{4,3,2,1,0:T(4,128)(2,1)} %copy.458) | data formatting | bytes 12582912 | tf_op jit(solution)/shard_map/reshape | solution.py:183
  663.8 7.0 fusion.33
  670.8 4.7 copy.460
  675.5 51.4 %all-to-all-start.10 = ((bf16[8,4,5,64,384]{4,3,2,1,0:T(8,128)(2,1)}), bf16[8,4,5,64,384]{4,3,2,1,0:T(8,128)(2,1)}, u32[]{:S(2)}, u32[]{:S(2)}) async-start(bf16[8,4,5,64,384]{4,3,2,1,0:T(8,128)(2,1)} %copy.460), calls=%async_computation.10 | async-start | bytes 15728640 | tf_op jit(solution)/shard_map/all_to_all | solution.py:187
  727.0 5.4 convert_bitcast_fusion
  732.4 12.0 %copy.465 = bf16[4,8,256,3,128]{4,3,2,1,0:T(4,128)(2,1)} copy(bf16[4,8,256,3,128]{4,2,3,1,0:T(8,128)(2,1)} %convert_bitcast_fusion) | data formatting | bytes 12582912 | tf_op jit(solution)/shard_map/convert_element_type | solution.py:141
  744.4 16.8 %reshape.456 = bf16[4,32,64,384]{3,2,1,0:T(8,128)(2,1)} reshape(bf16[4,8,256,3,128]{4,3,2,1,0:T(4,128)(2,1)} %copy.465) | data formatting | bytes 12582912 | tf_op jit(solution)/shard_map/reshape | solution.py:142
  761.3 7.0 fusion.36
  768.2 4.7 copy.467
  772.9 42.8 %all-to-all-done.10 = bf16[8,4,5,64,384]{4,3,2,1,0:T(8,128)(2,1)} async-done(((bf16[8,4,5,64,384]{4,3,2,1,0:T(8,128)(2,1)}), bf16[8,4,5,64,384]{4,3,2,1,0:T(8,128)(2,1)}, u32[]{:S(2)}, u32[]{:S(2)}) %all-to-all-start.10) | async-done | bytes 7864352 | tf_op jit(solution)/shard_map/all_to_all | solution.py:187
  815.7 4.9 all-to-all-start.11
  828.6 11.5 %fusion.80 = bf16[8,64,4,384]{3,0,1,2:T(8,128)(2,1)S(1)} fusion(bf16[8,4,5,64,384]{4,3,2,1,0:T(8,128)(2,1)} %all-to-all-done.10, s32[8,4,5]{2,0,1:T(8,128)S(1)} %copy-done.16), kind=kOutput, calls=%fused_computation.78 | convolution fusion | flops 63702272 | bytes 9437824 | tf_op jit(solution)/shard_map/sgcl,sgctw->ltgw/dot_general | solution.py:192
  842.7 66.3 %all-to-all-done.11 = bf16[8,4,5,64,384]{4,3,2,1,0:T(8,128)(2,1)} async-done(((bf16[8,4,5,64,384]{4,3,2,1,0:T(8,128)(2,1)}), bf16[8,4,5,64,384]{4,3,2,1,0:T(8,128)(2,1)}, u32[]{:S(2)}, u32[]{:S(2)}) %all-to-all-start.11) | async-done | bytes 7864352 | tf_op jit(solution)/shard_map/all_to_all | solution.py:188
  909.1 11.8 %fusion.83 = bf16[8,64,4,384]{3,0,1,2:T(8,128)(2,1)S(1)} fusion(bf16[8,4,5,64,384]{4,3,2,1,0:T(8,128)(2,1)} %all-to-all-done.11, s32[8,4,5]{2,0,1:T(8,128)S(1)} %copy-done.16), kind=kOutput, calls=%fused_computation.79 | convolution fusion | flops 63702272 | bytes 9437824 | tf_op jit(solution)/shard_map/sgcl,sgctw->ltgw/dot_general | solution.py:192
  (113 shorter events, 115.3 us)
Async XLA Ops:
  2.0 386.9 %copy-start.11 = (pred[4,32,8]{1,2,0:T(8,128)(4,1)}, pred[4,32,8]{1,2,0:T(8,128)(4,1)S(1)}, u32[]{:S(2)}) copy-start(pred[4,32,8]{1,2,0:T(8,128)(4,1)S(1)} %iota_compare_fusion.4) | copy-start | bytes 3076
  2.2 386.6 %copy-start.13 = (pred[4,32,5]{1,2,0:T(8,128)(4,1)}, pred[4,32,5]{1,2,0:T(8,128)(4,1)S(1)}, u32[]{:S(2)}) copy-start(pred[4,32,5]{1,2,0:T(8,128)(4,1)S(1)} %iota_compare_fusion.2) | copy-start | bytes 1924
  3.4 9.9 %all-to-all-start.2 = ((s32[8,4,5]{2,1,0:T(4,128)}), s32[8,4,5]{2,1,0:T(4,128)S(1)}, u32[]{:S(2)}, u32[]{:S(2)}) async-start(s32[8,4,5]{2,1,0:T(4,128)} %copy.400), calls=%async_computation.2 | async-start | bytes 32768 | tf_op jit(solution)/shard_map/all_to_all | solution.py:70
  13.3 41.8 %all-to-all-start.1 = ((bf16[128,4,1536]{2,0,1:T(8,128)(2,1)}), bf16[128,4,1536]{2,0,1:T(8,128)(2,1)S(1)}, u32[]{:S(2)}, u32[]{:S(2)}) async-start(bf16[128,4,1536]{2,0,1:T(8,128)(2,1)} %bitcast.200), calls=%async_computation.1 | async-start | bytes 3145728 | tf_op jit(solution)/shard_map/all_to_all | solution.py:36
  55.1 40.9 %all-to-all-start = ((bf16[128,4,1536]{0,2,1:T(8,128)(2,1)}), bf16[128,4,1536]{0,2,1:T(8,128)(2,1)}, u32[]{:S(2)}, u32[]{:S(2)}) async-start(bf16[128,4,1536]{0,2,1:T(8,128)(2,1)} %bitcast.201), calls=%async_computation | async-start | bytes 3145728 | tf_op jit(solution)/shard_map/all_to_all | solution.py:37
  96.0 40.9 %all-to-all-start.5 = ((bf16[128,4,1536]{2,0,1:T(8,128)(2,1)}), bf16[128,4,1536]{2,0,1:T(8,128)(2,1)}, u32[]{:S(2)}, u32[]{:S(2)}) async-start(bf16[128,4,1536]{2,0,1:T(8,128)(2,1)} %bitcast.202), calls=%async_computation.5 | async-start | bytes 3145728 | tf_op jit(solution)/shard_map/all_to_all | solution.py:39
  136.9 40.9 %all-to-all-start.4 = ((bf16[128,4,1536]{0,2,1:T(8,128)(2,1)}), bf16[128,4,1536]{0,2,1:T(8,128)(2,1)}, u32[]{:S(2)}, u32[]{:S(2)}) async-start(bf16[128,4,1536]{0,2,1:T(8,128)(2,1)} %bitcast.199), calls=%async_computation.4 | async-start | bytes 3145728 | tf_op jit(solution)/shard_map/all_to_all | solution.py:38
  145.2 0.6 copy-start.15
  177.7 93.3 %all-to-all-start.3 = ((bf16[8,4,5,64,384]{4,3,2,1,0:T(8,128)(2,1)}), bf16[8,4,5,64,384]{4,3,2,1,0:T(8,128)(2,1)}, u32[]{:S(2)}, u32[]{:S(2)}) async-start(bf16[8,4,5,64,384]{4,3,2,1,0:T(8,128)(2,1)} %copy.404), calls=%async_computation.3 | async-start | bytes 15728640 | tf_op jit(solution)/shard_map/all_to_all | solution.py:75
  271.1 117.8 %all-to-all-start.6 = ((bf16[8,4,5,64,384]{4,3,2,1,0:T(8,128)(2,1)}), bf16[8,4,5,64,384]{4,3,2,1,0:T(8,128)(2,1)}, u32[]{:S(2)}, u32[]{:S(2)}) async-start(bf16[8,4,5,64,384]{4,3,2,1,0:T(8,128)(2,1)} %copy.428), calls=%async_computation.6 | async-start | bytes 15728640 | tf_op jit(solution)/shard_map/all_to_all | solution.py:76
  278.8 59.0 %collective-permute-start = (bf16[512,1536]{1,0:T(8,128)(2,1)}, bf16[512,1536]{1,0:T(8,128)(2,1)}, u32[]{:S(2)}, u32[]{:S(2)}) collective-permute-start(bf16[512,1536]{1,0:T(8,128)(2,1)} %bitcast.209), channel_id=1, source_target_pairs={{0,4},{4,8},{8,12},{12,16},{16,20},{20,24},{24,28},{1,5},{5,9},{9,... | collective-permute-start | bytes 4718600 | tf_op jit(solution)/shard_map/ppermute | solution.py:18
  284.9 70.2 %collective-permute-start.1 = (bf16[512,1536]{1,0:T(8,128)(2,1)}, bf16[512,1536]{1,0:T(8,128)(2,1)}, u32[]{:S(2)}, u32[]{:S(2)}) collective-permute-start(bf16[512,1536]{1,0:T(8,128)(2,1)} %bitcast.210), channel_id=1, source_target_pairs={{0,4},{4,8},{8,12},{12,16},{16,20},{20,24},{24,28},{1,5},{5,9},{9,... | collective-permute-start | bytes 4718600 | tf_op jit(solution)/shard_map/ppermute | solution.py:18
  315.3 8.2 copy-start.8
  323.5 19.4 %copy-start.6 = (bf16[512,4,3,128]{0,3,2,1:T(8,128)(2,1)}, bf16[512,4,3,128]{0,3,2,1:T(8,128)(2,1)S(1)}, u32[]{:S(2)}) copy-start(bf16[512,4,3,128]{0,3,2,1:T(8,128)(2,1)S(1)} %reshape.440) | copy-start | bytes 4718596
  327.6 15.3 %copy-start.7 = (bf16[512,4,3,128]{3,0,2,1:T(8,128)(2,1)}, bf16[512,4,3,128]{3,0,2,1:T(8,128)(2,1)S(1)}, u32[]{:S(2)}) copy-start(bf16[512,4,3,128]{3,0,2,1:T(8,128)(2,1)S(1)} %copy.395) | copy-start | bytes 4718596
  402.6 16.8 %copy-start.2 = (bf16[8,64,4,3,128]{4,3,2,1,0:T(4,128)(2,1)S(1)}, bf16[8,64,4,3,128]{4,3,2,1,0:T(4,128)(2,1)}, u32[]{:S(2)}) copy-start(bf16[8,64,4,3,128]{4,3,2,1,0:T(4,128)(2,1)} %reshape.444) | copy-start | bytes 4718596
  419.4 8.6 copy-start.9
  447.9 5.7 copy-start
  456.4 14.7 %copy-start.10 = (pred[512,1024]{0,1:T(8,128)(4,1)S(1)}, pred[512,1024]{0,1:T(8,128)(4,1)}, u32[]{:S(2)}) copy-start(pred[512,1024]{0,1:T(8,128)(4,1)} %compare_and_fusion) | copy-start | bytes 1572868
  471.1 18.3 %copy-start.5 = (bf16[8,64,4,3,128]{4,3,2,1,0:T(4,128)(2,1)S(1)}, bf16[8,64,4,3,128]{4,3,2,1,0:T(4,128)(2,1)}, u32[]{:S(2)}) copy-start(bf16[8,64,4,3,128]{4,3,2,1,0:T(4,128)(2,1)} %reshape.451) | copy-start | bytes 4718596
  497.0 5.7 copy-start.4
  531.3 65.4 %all-to-all-start.7 = ((bf16[4,128,1536]{1,2,0:T(8,128)(2,1)}), bf16[4,128,1536]{1,2,0:T(8,128)(2,1)}, u32[]{:S(2)}, u32[]{:S(2)}) async-start(bf16[4,128,1536]{1,2,0:T(8,128)(2,1)} %copy.447), calls=%async_computation.7 | async-start | bytes 3145728 | tf_op jit(solution)/shard_map/all_to_all | solution.py:200
  543.6 48.3 %collective-permute-start.2 = (f32[512,1536]{1,0:T(8,128)}, f32[512,1536]{1,0:T(8,128)}, u32[]{:S(2)}, u32[]{:S(2)}) collective-permute-start(f32[512,1536]{1,0:T(8,128)} %copy.449), channel_id=1, source_target_pairs={{4,0},{8,4},{12,8},{16,12},{20,16},{24,20},{28,24},{5,1},{9,5},{13... | collective-permute-start | bytes 9437192 | tf_op jit(solution)/shard_map/ppermute | solution.py:18
  566.9 48.9 %collective-permute-start.3 = (f32[512,1536]{1,0:T(8,128)}, f32[512,1536]{1,0:T(8,128)}, u32[]{:S(2)}, u32[]{:S(2)}) collective-permute-start(f32[512,1536]{1,0:T(8,128)} %copy.453), channel_id=1, source_target_pairs={{4,0},{8,4},{12,8},{16,12},{20,16},{24,20},{28,24},{5,1},{9,5},{13... | collective-permute-start | bytes 9437192 | tf_op jit(solution)/shard_map/ppermute | solution.py:18
  596.7 26.4 %all-to-all-start.8 = ((bf16[4,128,1536]{1,2,0:T(8,128)(2,1)}), bf16[4,128,1536]{1,2,0:T(8,128)(2,1)}, u32[]{:S(2)}, u32[]{:S(2)}) async-start(bf16[4,128,1536]{1,2,0:T(8,128)(2,1)} %copy.451), calls=%async_computation.8 | async-start | bytes 3145728 | tf_op jit(solution)/shard_map/all_to_all | solution.py:201
  620.2 7.5 copy-start.3
  623.1 52.4 %all-to-all-start.9 = ((bf16[4,128,1536]{1,2,0:T(8,128)(2,1)}), bf16[4,128,1536]{1,2,0:T(8,128)(2,1)}, u32[]{:S(2)}, u32[]{:S(2)}) async-start(bf16[4,128,1536]{1,2,0:T(8,128)(2,1)} %copy.455), calls=%async_computation.9 | async-start | bytes 3145728 | tf_op jit(solution)/shard_map/all_to_all | solution.py:202
  646.8 17.1 %copy-start.12 = (pred[4,32,8]{1,2,0:T(8,128)(4,1)S(1)}, pred[4,32,8]{1,2,0:T(8,128)(4,1)}, u32[]{:S(2)}) copy-start(pred[4,32,8]{1,2,0:T(8,128)(4,1)} %copy-done.11) | copy-start | bytes 3076
  646.8 17.1 %copy-start.14 = (pred[4,32,5]{1,2,0:T(8,128)(4,1)S(1)}, pred[4,32,5]{1,2,0:T(8,128)(4,1)}, u32[]{:S(2)}) copy-start(pred[4,32,5]{1,2,0:T(8,128)(4,1)} %copy-done.13) | copy-start | bytes 1924
  675.5 51.5 %copy-start.1 = (bf16[4,3,8,64,256]{4,3,2,1,0:T(8,128)(2,1)S(1)}, bf16[4,3,8,64,256]{4,3,2,1,0:T(8,128)(2,1)}, u32[]{:S(2)}) copy-start(bf16[4,3,8,64,256]{4,3,2,1,0:T(8,128)(2,1)} %copy-done) | copy-start | bytes 9437188
  675.5 140.2 %all-to-all-start.10 = ((bf16[8,4,5,64,384]{4,3,2,1,0:T(8,128)(2,1)}), bf16[8,4,5,64,384]{4,3,2,1,0:T(8,128)(2,1)}, u32[]{:S(2)}, u32[]{:S(2)}) async-start(bf16[8,4,5,64,384]{4,3,2,1,0:T(8,128)(2,1)} %copy.460), calls=%async_computation.10 | async-start | bytes 15728640 | tf_op jit(solution)/shard_map/all_to_all | solution.py:187
  815.7 93.4 %all-to-all-start.11 = ((bf16[8,4,5,64,384]{4,3,2,1,0:T(8,128)(2,1)}), bf16[8,4,5,64,384]{4,3,2,1,0:T(8,128)(2,1)}, u32[]{:S(2)}, u32[]{:S(2)}) async-start(bf16[8,4,5,64,384]{4,3,2,1,0:T(8,128)(2,1)} %copy.467), calls=%async_computation.11 | async-start | bytes 15728640 | tf_op jit(solution)/shard_map/all_to_all | solution.py:188
  823.2 5.4 copy-start.16
where the time goes:
time: 937 us; the launch traced here: 924 us
  waiting for transfers between devices  338 us (36%)
  local copies, waits for them, and re-layouts  259 us (28%)
  matrix products  182 us (19%)
  starting transfers between devices  113 us (12%)
  other arithmetic  30.6 us (3%)
    all_to_all x1, waiting for transfers between devices, per_device(): lax.all_to_all(served_k, 'mem', split_axis=0, concat_axis=0, tiled=True)  76 us
    all_to_all x1, waiting for transfers between devices, per_device(): lax.all_to_all(slots_v, 'mem', split_axis=0, concat_axis=0, tiled=True)  66.3 us
    all_to_all x1, starting transfers between devices, per_device(): lax.all_to_all(slots_k, 'mem', split_axis=0, concat_axis=0, tiled=True)  51.4 us
    all_to_all x1, waiting for transfers between devices, per_device(): lax.all_to_all(slots_k, 'mem', split_axis=0, concat_axis=0, tiled=True)  42.8 us
    all_to_all x1, waiting for transfers between devices, per_device(): lax.all_to_all(queries, 'head', split_axis=1, concat_axis=0, tiled=True)  34.3 us
    all_to_all x1, waiting for transfers between devices, per_device(): lax.all_to_all(out_grad, 'head', split_axis=1, concat_axis=0, tiled=True)  33.9 us
    all_to_all x1, waiting for transfers between devices, per_device(): lax.all_to_all(keys_local, 'head', split_axis=1, concat_axis=0, tiled=True)  33.8 us
    reshape x2, local copies, waits for them, and re-layouts, unpack(): return picked.reshape(groups, num_blocks, mem_span, GROUP_HEADS, HEAD_DIM)  33.6 us
  transfers between devices with their start and end apart: 16, of which 11 were waited for; matrix products, arithmetic and copies ran while one was open for 34% of the time, Pallas kernels for 0%

commit v1 on v0

v1 whole, which is shorter than its diff:
```python
import functools
import math

import jax
import jax.numpy as jnp
from jax import lax
from jax.experimental import pallas as pl
from jax.experimental.pallas import tpu as pltpu
from jax.sharding import Mesh
from jax.sharding import PartitionSpec as P

HEAD_DIM = 128
GROUP_HEADS = 3
BLOCK = 64
READS = 4
WINDOW = 512
TILE = 128
MASKED = -1e30
SCALE = 1.0 / math.sqrt(HEAD_DIM)


def dot(a, b, contract):
    return lax.dot_general(a, b, ((contract[:1], contract[1:]), ((), ())), preferred_element_type=jnp.float32)


def attention_kernel(parts, slots_ref, reads_ref, start_ref, *refs):
    q_ref, do_ref, k_ref, v_ref, kt_ref, vt_ref = refs[:6]
    refs = refs[6:]
    ck_refs, cv_refs, refs = refs[:parts], refs[parts : 2 * parts], refs[2 * parts :]
    dq_ref, dk_ref, dv_ref, dkt_ref, dvt_ref = refs[:5]
    refs = refs[5:]
    gk_refs, gv_refs, refs = refs[:parts], refs[parts : 2 * parts], refs[2 * parts :]
    kx, vx, dkx, dvx = refs[:4]
    if parts > 1:
        ckx, cvx, gkx, gvx = refs[4:]
    else:
        ckx, cvx, gkx, gvx = ck_refs[0], cv_refs[0], gk_refs[0], gv_refs[0]
    rows = q_ref.shape[0]
    span = WINDOW + TILE
    group = pl.program_id(0) // GROUP_HEADS

    kx[:WINDOW] = kt_ref[...]
    kx[WINDOW:] = k_ref[...]
    vx[:WINDOW] = vt_ref[...]
    vx[WINDOW:] = v_ref[...]
    dkx[...] = jnp.zeros_like(dkx)
    dvx[...] = jnp.zeros_like(dvx)
    gkx[...] = jnp.zeros_like(gkx)
    gvx[...] = jnp.zeros_like(gvx)
    if parts > 1:
        part_rows = ck_refs[0].shape[0]
        for p in range(parts):
            ckx[p * part_rows : (p + 1) * part_rows] = ck_refs[p][...]
            cvx[p * part_rows : (p + 1) * part_rows] = cv_refs[p][...]

    key_at = lax.broadcasted_iota(jnp.int32, (TILE, TILE), 0)
    query_at = lax.broadcasted_iota(jnp.int32, (TILE, TILE), 1)
    first_half = lax.broadcasted_iota(jnp.int32, (1, TILE), 1) < BLOCK
    first_rows = lax.broadcasted_iota(jnp.int32, (TILE, 1), 0) < BLOCK
    at_start = start_ref[0]

    def tile(t, carry):
        at = pl.multiple_of(t * TILE, TILE)
        q = q_ref[pl.ds(at, TILE)]
        do = do_ref[pl.ds(at, TILE)]
        k_loc = kx[pl.ds(at, span)]
        v_loc = vx[pl.ds(at, span)]
        places = []
        k_mem, v_mem = [], []
        for b in range(TILE // BLOCK):
            block = (group * (rows // BLOCK) + t * (TILE // BLOCK) + b) * READS
            where = [pl.multiple_of(slots_ref[reads_ref[block + r]] * BLOCK, BLOCK) for r in range(READS)]
            places.append(where)
            k_mem.append(jnp.concatenate([ckx[pl.ds(w, BLOCK)] for w in where], 0))
            v_mem.append(jnp.concatenate([cvx[pl.ds(w, BLOCK)] for w in where], 0))

        s_loc = dot(k_loc, q, (1, 1))
        s_mem = jnp.where(first_half, dot(k_mem[0], q, (1, 1)), dot(k_mem[1], q, (1, 1)))
        pieces = []
        for c in range(span // TILE):
            piece = s_loc[c * TILE : (c + 1) * TILE]
            if c < span // TILE - 1:
                before = (at_start > 0) & (at + c * TILE < WINDOW)
                piece = piece + jnp.where(before, MASKED, 0.0)
            else:
                piece = jnp.where(key_at <= query_at, piece, MASKED)
            if c == 0:
                piece = jnp.where(key_at >= query_at, piece, MASKED)
            pieces.append(piece)
        s_loc = jnp.concatenate(pieces, 0)
        top = jnp.maximum(jnp.max(s_loc, 0, keepdims=True), jnp.max(s_mem, 0, keepdims=True))
        unit = SCALE * math.log2(math.e)
        e_loc = jnp.exp2((s_loc - top) * unit)
        e_mem = jnp.exp2((s_mem - top) * unit)
        total = jnp.sum(e_loc, 0, keepdims=True) + jnp.sum(e_mem, 0, keepdims=True)
        inverse = 1.0 / total
        p_loc = e_loc * inverse
        p_mem = e_mem * inverse
        w_loc = p_loc.astype(jnp.bfloat16)
        w_mem = p_mem.astype(jnp.bfloat16)
        dp_loc = dot(v_loc, do, (1, 1))
        dp_mem = jnp.where(first_half, dot(v_mem[0], do, (1, 1)), dot(v_mem[1], do, (1, 1)))
        delta = jnp.sum(w_loc.astype(jnp.float32) * dp_loc, 0, keepdims=True) + jnp.sum(
            w_mem.astype(jnp.float32) * dp_mem, 0, keepdims=True
        )
        ds_loc = (p_loc * (dp_loc - delta)).astype(jnp.bfloat16)
        ds_mem = (p_mem * (dp_mem - delta)).astype(jnp.bfloat16)

        dq_mem = jnp.where(first_rows, dot(ds_mem, k_mem[0], (0, 0)), dot(ds_mem, k_mem[1], (0, 0)))
        dq_ref[pl.ds(at, TILE)] = ((dot(ds_loc, k_loc, (0, 0)) + dq_mem) * SCALE).astype(dq_ref.dtype)
        dkx[pl.ds(at, span)] += dot(ds_loc, q, (1, 0))
        dvx[pl.ds(at, span)] += dot(w_loc, do, (1, 0))
        zero = jnp.zeros_like(q)
        q_two = jnp.concatenate([jnp.where(first_rows, q, zero), jnp.where(first_rows, zero, q)], 1)
        do_two = jnp.concatenate([jnp.where(first_rows, do, zero), jnp.where(first_rows, zero, do)], 1)
        read_k = (dot(ds_mem, q_two, (1, 0)) * SCALE).astype(jnp.bfloat16).astype(jnp.float32)
        read_v = dot(w_mem, do_two, (1, 0)).astype(jnp.bfloat16).astype(jnp.float32)
        for b in range(TILE // BLOCK):
            for r in range(READS):
                here = (slice(r * BLOCK, (r + 1) * BLOCK), slice(b * HEAD_DIM, (b + 1) * HEAD_DIM))
                gkx[pl.ds(places[b][r], BLOCK)] += read_k[here]
                gvx[pl.ds(places[b][r], BLOCK)] += read_v[here]
        return carry

    lax.fori_loop(0, rows // TILE, tile, 0)
    dkt_ref[...] = (dkx[:WINDOW] * SCALE).astype(dkt_ref.dtype)
    dvt_ref[...] = dvx[:WINDOW].astype(dvt_ref.dtype)
    dk_ref[...] = dkx[WINDOW:] * SCALE
    dv_ref[...] = dvx[WINDOW:]
    if parts > 1:
        for p in range(parts):
            gk_refs[p][...] = gkx[p * part_rows : (p + 1) * part_rows].astype(gk_refs[p].dtype)
            gv_refs[p][...] = gvx[p * part_rows : (p + 1) * part_rows].astype(gv_refs[p].dtype)


def attention(slots, reads, start, qd, kv, tails, cache_k, cache_v):
    rows, width = qd.shape[0], qd.shape[1] // 2
    heads = width // HEAD_DIM
    parts = len(cache_k)
    part_rows = cache_k[0].shape[0]

    def column(height, offset=0):
        return pl.BlockSpec((height, HEAD_DIM), lambda h, *_: (0, h + offset))

    bf16, f32 = jnp.bfloat16, jnp.float32
    kinds = [f32] + [bf16] * (parts - 1)
    shape = jax.ShapeDtypeStruct
    scratch = [
        pltpu.VMEM((WINDOW + rows, HEAD_DIM), bf16),
        pltpu.VMEM((WINDOW + rows, HEAD_DIM), bf16),
        pltpu.VMEM((WINDOW + rows, HEAD_DIM), f32),
        pltpu.VMEM((WINDOW + rows, HEAD_DIM), f32),
    ]
    if parts > 1:
        scratch += [pltpu.VMEM((parts * part_rows, HEAD_DIM), kind) for kind in (bf16, bf16, f32, f32)]
    pairs = heads * rows * (WINDOW + TILE + 2 * READS * BLOCK)
    outs = pl.pallas_call(
        functools.partial(attention_kernel, parts),
        grid_spec=pltpu.PrefetchScalarGridSpec(
            num_scalar_prefetch=3,
            grid=(heads,),
            in_specs=[
                column(rows),
                column(rows, heads),
                column(rows),
                column(rows, heads),
                column(WINDOW),
                column(WINDOW, heads),
            ]
            + [column(part_rows)] * (2 * parts),
            out_specs=[column(rows)] * 3 + [column(WINDOW)] * 2 + [column(part_rows)] * (2 * parts),
            scratch_shapes=scratch,
        ),
        out_shape=[shape((rows, width), bf16), shape((rows, width), f32), shape((rows, width), f32)]
        + [shape((WINDOW, width), bf16)] * 2
        + [shape((part_rows, width), kind) for kind in kinds] * 2,
        compiler_params=pltpu.CompilerParams(vmem_limit_bytes=56 * 2**20),
        cost_estimate=pl.CostEstimate(
            flops=10 * pairs * HEAD_DIM, bytes_accessed=heads * part_rows * parts * 1400, transcendentals=pairs
        ),
        name="attention",
    )(slots, reads, start, qd, qd, kv, kv, tails, tails, *cache_k, *cache_v)
    return outs[:5], outs[5 : 5 + parts], outs[5 + parts :]


def per_device(queries, keys_local, values_local, cache_keys, cache_values, block_map, retrieved, out_grad):
    chips, zs = lax.axis_size("chip"), lax.axis_size("head")
    chip, core = lax.axis_index("chip"), lax.axis_index("core")
    rows, features = queries.shape
    blk_dev = cache_keys.shape[0] // BLOCK
    groups = retrieved.shape[1]
    split = 2 if groups % 2 == 0 else 1
    head_axes = ("core", "head") if split == 2 else ("head",)
    token_axes = ("chip",) if split == 2 else ("chip", "core")
    peers = split * zs
    width = features // peers
    tokens = rows * peers
    token_parts = chips if split == 2 else 2 * chips
    token_index = lax.axis_index(token_axes)
    relay = split == 2 and chips == 4
    seq_parts = min(8, 2 * chips) * cache_keys.shape[0] // tokens

    def to_heads(arrays):
        packed = [
            a.reshape(rows, zs, split, width).transpose(2, 1, 0, 3).reshape(peers, rows, width) for a in arrays
        ]
        packed = jnp.concatenate(packed, 2)
        moved = lax.all_to_all(packed, head_axes, split_axis=0, concat_axis=0, tiled=True)
        return moved.reshape(tokens, len(arrays) * width)

    def to_tokens(array):
        moved = lax.all_to_all(
            array.reshape(peers, rows, width), head_axes, split_axis=0, concat_axis=0, tiled=True
        )
        return moved.reshape(split, zs, rows, width).transpose(2, 1, 0, 3).reshape(rows, features)

    def other_core(array):
        return lax.ppermute(array, "core", [(0, 1), (1, 0)])

    def other_chip(array, by):
        return lax.ppermute(array, "chip", [(i, i ^ by) for i in range(chips)])

    def half(array, which):
        return lax.dynamic_slice_in_dim(array, which * width, width, 1)

    if split == 2:
        cache_k, cache_v = (
            jnp.concatenate([half(a, core), other_core(half(a, 1 - core))], 0) for a in (cache_keys, cache_values)
        )
        theirs = other_core(retrieved)
        ids = jnp.where(core == 0, jnp.stack([retrieved, theirs]), jnp.stack([theirs, retrieved]))
        ids = ids.reshape((-1,) + retrieved.shape[1:])
        ids = lax.dynamic_slice_in_dim(ids, core * (groups // 2), groups // 2, 1)
    else:
        cache_k, cache_v, ids = cache_keys, cache_values, retrieved
    reads = jnp.transpose(ids, (1, 0, 2)).reshape(-1)
    owner, local = block_map // blk_dev, block_map % blk_dev
    owner_chip, owner_core = owner // 2, owner % 2
    if relay:
        owner_chip = owner_chip ^ chip
    if split == 2:
        owner_core = owner_core ^ core
    slots = ((owner_chip * 2 + owner_core) * blk_dev + local).astype(jnp.int32)
    start = (token_index % seq_parts == 0).astype(jnp.int32).reshape(1)

    if relay:
        k_y = other_chip(cache_k, 2)
        v_x = other_chip(cache_v, 1)
        k_x = other_chip(cache_k, 1)
        v_y = other_chip(cache_v, 2)
        all_k = [cache_k, k_x, k_y, other_chip(k_y, 1)]
        all_v = [cache_v, v_x, v_y, other_chip(v_x, 2)]
    else:
        all_k, all_v = ([lax.all_gather(a, token_axes, tiled=True)] for a in (cache_k, cache_v))

    kv = to_heads([keys_local, values_local])
    tails = lax.ppermute(kv[tokens - WINDOW :], token_axes, [(i, i + 1) for i in range(token_parts - 1)])
    qd = to_heads([queries, out_grad])
    (dq, dk, dv, dkt, dvt), gk, gv = attention(slots, reads, start, qd, kv, tails, all_k, all_v)

    back = [(i + 1, i) for i in range(token_parts - 1)]
    dkt, dvt = lax.ppermute((dkt, dvt), token_axes, back)

    def with_tail(own, tail):
        own = jnp.concatenate([own[: tokens - WINDOW], own[tokens - WINDOW :] + tail.astype(jnp.float32)], 0)
        return own.astype(jnp.bfloat16)

    if relay:
        bf16, f32 = jnp.bfloat16, jnp.float32
        k_far = other_chip(gk[3], 1)
        v_far = other_chip(gv[3], 2)
        k_x = other_chip(gk[1], 1)
        v_y = other_chip(gv[2], 2)
        k_y = other_chip((gk[2].astype(f32) + k_far.astype(f32)).astype(bf16), 2)
        v_x = other_chip((gv[1].astype(f32) + v_far.astype(f32)).astype(bf16), 1)
        sum_k = (gk[0] + k_x.astype(f32) + k_y.astype(f32)).astype(bf16)
        sum_v = (gv[0] + v_x.astype(f32) + v_y.astype(f32)).astype(bf16)
    else:
        sum_k, sum_v = (
            lax.psum_scatter(g[0], token_axes, scatter_dimension=0, tiled=True).astype(jnp.bfloat16) for g in (gk, gv)
        )
    if split == 2:
        own_rows = sum_k.shape[0] // 2

        def to_owner(total):
            mine, recv = total[:own_rows], other_core(total[own_rows:])
            return jnp.where(core == 0, jnp.concatenate([mine, recv], 1), jnp.concatenate([recv, mine], 1))

        sum_k, sum_v = to_owner(sum_k), to_owner(sum_v)

    out_q = to_tokens(dq)
    out_k = to_tokens(with_tail(dk, dkt))
    out_v = to_tokens(with_tail(dv, dvt))
    return out_q, out_k, out_v, sum_k, sum_v


def solution(mesh):
    shape = mesh.shape
    fine = Mesh(mesh.devices.reshape(shape["mem"] // 2, 2, shape["head"]), ("chip", "core", "head"))
    by_token = P(("chip", "core", "head"), None)
    by_block = P(("chip", "core"), "head")
    return jax.shard_map(
        per_device,
        mesh=fine,
        in_specs=(
            by_token,
            by_token,
            by_token,
            by_block,
            by_block,
            P(),
            P(("chip", "core"), "head", None),
            by_token,
        ),
        out_specs=(by_token, by_token, by_token, by_block, by_block),
        check_vma=False,
    )
```

time: 937 us -> 495 us (0.53)
  local copies, waits for them, and re-layouts: 259 us -> 50 us
  matrix products: 182 us -> 0 us
  starting transfers between devices: 113 us -> 48.8 us
  Pallas kernels: 0 us -> 55.8 us
  waiting for transfers between devices: 338 us -> 307 us
    all_to_all x12 -> x5, waiting for transfers between devices: 313 us -> 67.4 us  [the longest x2 54.7 us: to_heads(): lax.all_to_all(packed, head_axes, split_axis=0, concat_axis=0, tiled=True)]
    ppermute x4 -> x20, waiting for transfers between devices: 25.6 us -> 239 us  [the longest x12 206 us: other_chip(): return lax.ppermute(array, 'chip', [(i, i ^ by) for i in range(chips)])]
    dot_general x20 -> x0, matrix products: 182 us -> none  [the longest x2 23.3 us: stored_sum(): jnp.einsum('sgcl,sgctw->ltgw', one_hot, returned, preferred_element_type=...]
    all_to_all x12 -> x5, starting transfers between devices: 103 us -> 24.2 us  [the longest x3 13.4 us: to_tokens(): lax.all_to_all(array.reshape(peers, rows, width), head_axes, split_axis=0...]
    reshape x15 -> x11, local copies, waits for them, and re-layouts: 95 us -> 34.9 us  [the longest x4 17.9 us: to_heads(): a.reshape(rows, zs, split, width).transpose(2, 1, 0, 3)]
    pallas_call x0 -> x1, Pallas kernels: none -> 55.8 us  [attention(): pl.pallas_call(functools.partial(attention_kernel, parts), grid_spec=pltp...]
    all_to_all x11 -> x0, local copies, waits for them, and re-layouts: 37.3 us -> none  [the longest x2 11.2 us: per_device(): lax.all_to_all(values_local, 'head', split_axis=1, concat_axis=0, tiled=T...]
    convert_element_type x6 -> x0, local copies, waits for them, and re-layouts: 30.7 us -> none  [the longest x1 12 us: per_device(): read_dk = (scaling * jnp.einsum('gkbij,bigkd->gbjkd', dscore_mem, query_h...]
  transfers between devices with their start and end apart: 16 -> 25, of which waited for: 11 -> 13; matrix products, arithmetic and copies ran while one was open for 34% -> 13% of each run, Pallas kernels for 0% -> 0%
where the time goes in v1:
time: 495 us; the launch traced here: 488 us
  waiting for transfers between devices  307 us (62%)
  Pallas kernels  55.8 us (11%)
  local copies, waits for them, and re-layouts  50 us (10%)
  starting transfers between devices  48.8 us (10%)
  other arithmetic  25.9 us (5%)
    ppermute x12, waiting for transfers between devices, other_chip(): return lax.ppermute(array, 'chip', [(i, i ^ by) for i in range(chips)])  206 us
    pallas_call x1, Pallas kernels, attention(): pl.pallas_call(functools.partial(attention_kernel, parts), grid_spec=pltp...  55.8 us
    all_to_all x2, waiting for transfers between devices, to_heads(): lax.all_to_all(packed, head_axes, split_axis=0, concat_axis=0, tiled=True)  54.7 us
    ppermute x2, waiting for transfers between devices, per_device(): dkt, dvt = lax.ppermute((dkt, dvt), token_axes, back)  31.8 us
    reshape x4, local copies, waits for them, and re-layouts, to_heads(): a.reshape(rows, zs, split, width).transpose(2, 1, 0, 3)  17.9 us
    ppermute x12, starting transfers between devices, other_chip(): return lax.ppermute(array, 'chip', [(i, i ^ by) for i in range(chips)])  17.7 us
    reshape x6, local copies, waits for them, and re-layouts, to_tokens(): moved.reshape(split, zs, rows, width).transpose(2, 1, 0, 3)  16.3 us
    all_to_all x3, starting transfers between devices, to_tokens(): lax.all_to_all(array.reshape(peers, rows, width), head_axes, split_axis=0...  13.4 us
  transfers between devices with their start and end apart: 25, of which 13 were waited for; matrix products, arithmetic and copies ran while one was open for 13% of the time, Pallas kernels for 0%

profile of v1, /device:TPU:0, one launch (start us, length us, event | category | flops | bytes accessed | tf_op | source)
XLA Modules:
  0.0 487.8 jit_solution(4153730740161842550)
XLA Ops:
  0.6 4.1 reshape.89
  5.0 4.1 reshape.91
  9.4 1.9 pad_maximum_fusion.1
  11.3 6.3 %all-to-all-start.1 = ((bf16[8,128,1536]{2,1,0:T(8,128)(2,1)}), bf16[8,128,1536]{2,1,0:T(8,128)(2,1)S(1)}, u32[]{:S(2)}, u32[]{:S(2)}) async-start(bf16[8,128,1536]{2,1,0:T(8,128)(2,1)} %pad_maximum_fusion.1), calls=%async_computation.1 | async-start | bytes 6291456 | tf_op jit(solution)/shard_map/all_to_all | solution.py:208
  17.6 4.9 reshape.84
  22.5 2.8 copy.22
  25.4 4.9 reshape.86
  30.2 1.8 copy.23
  32.1 1.9 pad_maximum_fusion
  34.0 54.7 %all-to-all-done.1 = bf16[8,128,1536]{2,1,0:T(8,128)(2,1)S(1)} async-done(((bf16[8,128,1536]{2,1,0:T(8,128)(2,1)}), bf16[8,128,1536]{2,1,0:T(8,128)(2,1)S(1)}, u32[]{:S(2)}, u32[]{:S(2)}) %all-to-all-start.1) | async-done | bytes 3145760 | tf_op jit(solution)/shard_map/all_to_all | solution.py:208
  88.7 4.4 all-to-all-start
  93.2 1.6 constant_dynamic-slice_fusion.1
  95.6 1.5 collective-permute-done.6
  97.1 1.2 pad_maximum_fusion.3.refs_10_
  98.4 1.5 collective-permute-start.7
  99.9 1.2 pad_maximum_fusion.2.refs_6_
  101.1 1.5 collective-permute-start.4
  103.7 32.2 %collective-permute-done.7.refs_11_ = bf16[1024,768]{1,0:T(8,128)(2,1)} collective-permute-done((bf16[1024,768]{1,0:T(8,128)(2,1)}, bf16[1024,768]{1,0:T(8,128)(2,1)}, u32[]{:S(2)}, u32[]{:S(2)}) %collective-permute-start.7) | collective-permute-done | bytes 1572896 | tf_op jit(solution)/shard_map/ppermute | solution.py:221
  135.9 1.5 collective-permute-start.9
  137.4 1.3 collective-permute-done.4.refs_8_
  139.2 1.2 slice.42
  140.5 3.7 collective-permute-start.1
  144.2 0.5 fusion.slots_ref
  144.9 0.7 reshape.81.reads_ref
  145.6 26.8 %collective-permute-done.8.refs_12_ = bf16[1024,768]{1,0:T(8,128)(2,1)} collective-permute-done((bf16[1024,768]{1,0:T(8,128)(2,1)}, bf16[1024,768]{1,0:T(8,128)(2,1)}, u32[]{:S(2)}, u32[]{:S(2)}) %collective-permute-start.8) | collective-permute-done | bytes 1572896 | tf_op jit(solution)/shard_map/ppermute | solution.py:221
  172.4 65.6 %collective-permute-done.9.refs_13_ = bf16[1024,768]{1,0:T(8,128)(2,1)} collective-permute-done((bf16[1024,768]{1,0:T(8,128)(2,1)}, bf16[1024,768]{1,0:T(8,128)(2,1)}, u32[]{:S(2)}, u32[]{:S(2)}) %collective-permute-start.9) | collective-permute-done | bytes 1572896 | tf_op jit(solution)/shard_map/ppermute | solution.py:221
  238.0 1.1 copy-done.11
  239.1 55.8 %attention.1 = (bf16[1024,768]{1,0:T(8,128)(2,1)}, f32[1024,768]{1,0:T(8,128)}, f32[1024,768]{1,0:T(8,128)}, bf16[512,768]{1,0:T(8,128)(2,1)}, bf16[512,768]{1,0...) custom-call(s32[64]{0:T(128)} %fusion.slots_ref, ...), custom_call_target="tpu_custom_call" | custom-call | flops 9059696640 | bytes 34406400 | tf_op jit(solution)/shard_map/attention/pallas_call | solution.py:157
  294.9 4.9 %all-to-all-start.2 = ((bf16[8,128,768]{2,1,0:T(8,128)(2,1)}), bf16[8,128,768]{2,1,0:T(8,128)(2,1)S(1)}, u32[]{:S(2)}, u32[]{:S(2)}) async-start(bf16[8,128,768]{2,1,0:T(8,128)(2,1)} %bitcast.50), calls=%async_computation.2 | async-start | bytes 3145728 | tf_op jit(solution)/shard_map/all_to_all | solution.py:212
  299.8 1.3 collective-permute-start.10
  301.1 1.5 slice.54
  302.6 19.0 %collective-permute-done.10 = bf16[512,768]{1,0:T(8,128)(2,1)S(1)} collective-permute-done((bf16[512,768]{1,0:T(8,128)(2,1)S(1)}, bf16[512,768]{1,0:T(8,128)(2,1)S(1)}, u32[]{:S(2)}, u32[]{:S(2)}) %collective-permute-start.10) | collective-permute-done | bytes 786464 | tf_op jit(solution)/shard_map/ppermute | solution.py:262
  321.6 1.6 add_convert_fusion.5
  323.2 1.2 pad_maximum_fusion.4
  324.5 12.7 %all-to-all-done.2 = bf16[8,128,768]{2,1,0:T(8,128)(2,1)S(1)} async-done(((bf16[8,128,768]{2,1,0:T(8,128)(2,1)}), bf16[8,128,768]{2,1,0:T(8,128)(2,1)S(1)}, u32[]{:S(2)}, u32[]{:S(2)}) %all-to-all-start.2) | async-done | bytes 1572896 | tf_op jit(solution)/shard_map/all_to_all | solution.py:212
  337.1 3.6 all-to-all-start.3
  340.8 2.5 collective-permute-start.16
  343.4 1.3 collective-permute-start.11
  344.6 1.5 slice.53
  346.1 2.7 collective-permute-start.12
  348.8 1.5 collective-permute-start.18
  350.3 27.9 %collective-permute-done.13 = bf16[1024,768]{1,0:T(8,128)(2,1)S(1)} collective-permute-done((bf16[1024,768]{1,0:T(8,128)(2,1)}, bf16[1024,768]{1,0:T(8,128)(2,1)S(1)}, u32[]{:S(2)}, u32[]{:S(2)}) %collective-permute-start.13) | collective-permute-done | bytes 1572896 | tf_op jit(solution)/shard_map/ppermute | solution.py:221
  378.2 1.6 add_convert_fusion.3
  379.8 2.5 collective-permute-start.14
  382.3 12.8 %collective-permute-done.11 = bf16[512,768]{1,0:T(8,128)(2,1)S(1)} collective-permute-done((bf16[512,768]{1,0:T(8,128)(2,1)}, bf16[512,768]{1,0:T(8,128)(2,1)S(1)}, u32[]{:S(2)}, u32[]{:S(2)}) %collective-permute-start.11) | collective-permute-done | bytes 786464 | tf_op jit(solution)/shard_map/ppermute | solution.py:262
  395.3 1.6 add_convert_fusion.1
  396.9 2.3 collective-permute-start.17
  399.2 1.2 pad_maximum_fusion.5
  400.4 5.0 %all-to-all-start.4 = ((bf16[8,128,768]{2,1,0:T(8,128)(2,1)}), bf16[8,128,768]{2,1,0:T(8,128)(2,1)}, u32[]{:S(2)}, u32[]{:S(2)}) async-start(bf16[8,128,768]{2,1,0:T(8,128)(2,1)} %bitcast.38), calls=%async_computation.4 | async-start | bytes 3145728 | tf_op jit(solution)/shard_map/all_to_all | solution.py:212
  405.4 23.5 %collective-permute-done.12 = bf16[1024,768]{1,0:T(8,128)(2,1)} collective-permute-done((bf16[1024,768]{1,0:T(8,128)(2,1)}, bf16[1024,768]{1,0:T(8,128)(2,1)}, u32[]{:S(2)}, u32[]{:S(2)}) %collective-permute-start.12) | collective-permute-done | bytes 1572896 | tf_op jit(solution)/shard_map/ppermute | solution.py:221
  428.9 17.1 %collective-permute-done.14 = bf16[1024,768]{1,0:T(8,128)(2,1)} collective-permute-done((bf16[1024,768]{1,0:T(8,128)(2,1)}, bf16[1024,768]{1,0:T(8,128)(2,1)}, u32[]{:S(2)}, u32[]{:S(2)}) %collective-permute-start.14) | collective-permute-done | bytes 1572896 | tf_op jit(solution)/shard_map/ppermute | solution.py:221
  446.0 3.3 add_convert_fusion.2
  449.3 1.3 fusion.4
  450.6 11.5 %collective-permute-done.17 = bf16[1024,768]{1,0:T(8,128)(2,1)} collective-permute-done((bf16[1024,768]{1,0:T(8,128)(2,1)}, bf16[1024,768]{1,0:T(8,128)(2,1)}, u32[]{:S(2)}, u32[]{:S(2)}) %collective-permute-start.17) | collective-permute-done | bytes 1572896 | tf_op jit(solution)/shard_map/ppermute | solution.py:221
  462.0 2.3 add_convert_fusion
  464.4 1.2 fusion.3
  465.6 2.8 copy.34
  468.4 4.7 reshape.96
  473.1 1.6 copy.33
  474.7 2.1 reshape.98
  476.8 3.0 copy.32
  479.8 2.1 reshape.100
  481.9 3.0 maximum_select_fusion
  484.9 2.9 maximum_select_fusion.1
  (55 shorter events, 3.6 us)
Async XLA Ops:
  11.3 77.4 %all-to-all-start.1 = ((bf16[8,128,1536]{2,1,0:T(8,128)(2,1)}), bf16[8,128,1536]{2,1,0:T(8,128)(2,1)S(1)}, u32[]{:S(2)}, u32[]{:S(2)}) async-start(bf16[8,128,1536]{2,1,0:T(8,128)(2,1)} %pad_maximum_fusion.1), calls=%async_computation.1 | async-start | bytes 6291456 | tf_op jit(solution)/shard_map/all_to_all | solution.py:208
  30.2 1.9 copy-start.1
  88.7 50.5 %copy-start = (bf16[8,128,1536]{2,1,0:T(8,128)(2,1)}, bf16[8,128,1536]{2,1,0:T(8,128)(2,1)S(1)}, u32[]{:S(2)}) copy-start(bf16[8,128,1536]{2,1,0:T(8,128)(2,1)S(1)} %all-to-all-done.1) | copy-start | bytes 9437188
  88.7 149.3 %all-to-all-start = ((bf16[8,128,1536]{2,1,0:T(8,128)(2,1)}), bf16[8,128,1536]{2,1,0:T(8,128)(2,1)}, u32[]{:S(2)}, u32[]{:S(2)}) async-start(bf16[8,128,1536]{2,1,0:T(8,128)(2,1)} %pad_maximum_fusion), calls=%async_computation | async-start | bytes 6291456 | tf_op jit(solution)/shard_map/all_to_all | solution.py:208
  93.2 2.1 copy-start.6
  94.8 2.4 collective-permute-start.6
  95.3 4.6 collective-permute-start.2
  98.4 37.5 %collective-permute-start.7 = (bf16[1024,768]{1,0:T(8,128)(2,1)}, bf16[1024,768]{1,0:T(8,128)(2,1)}, u32[]{:S(2)}, u32[]{:S(2)}) collective-permute-start(bf16[1024,768]{1,0:T(8,128)(2,1)} %pad_maximum_fusion.3.refs_10_), channel_id=1, source_target_pairs={{0,8},{8,0},{16,24},{24,16},{1,9},{9,1},{17,25},{25,17},{2,10},{10... | collective-permute-start | bytes 4718600 | tf_op jit(solution)/shard_map/ppermute | solution.py:221
  99.9 2.8 copy-start.9
  101.1 43.0 %copy-start.10 = (s32[64]{0:T(128)S(1)}, s32[64]{0:T(128)}, u32[]{:S(2)}) copy-start(s32[64]{0:T(128)} %param.13) | copy-start | bytes 772
  101.1 37.6 %collective-permute-start.4 = (bf16[1024,768]{1,0:T(8,128)(2,1)}, bf16[1024,768]{1,0:T(8,128)(2,1)}, u32[]{:S(2)}, u32[]{:S(2)}) collective-permute-start(bf16[1024,768]{1,0:T(8,128)(2,1)} %pad_maximum_fusion.2.refs_6_), channel_id=1, source_target_pairs={{0,16},{8,24},{16,0},{24,8},{1,17},{9,25},{17,1},{25,9},{2,18},{10... | collective-permute-start | bytes 4718600 | tf_op jit(solution)/shard_map/ppermute | solution.py:221
  102.6 37.8 %collective-permute-start = (s32[8,4,4]{0,2,1:T(4,128)S(1)}, s32[8,4,4]{0,2,1:T(4,128)S(1)}, u32[]{:S(2)}, u32[]{:S(2)}) collective-permute-start(s32[8,4,4]{0,2,1:T(4,128)S(1)} %copy-done.9), channel_id=1, source_target_pairs={{0,4},{4,0},{1,5},{5,1},{2,6},{6,2},{3,7},{7,3},{8,12},{12,8},{9,1... | collective-permute-start | bytes 1544 | tf_op jit(solution)/shard_map/ppermute | solution.py:218
  102.6 69.7 %collective-permute-start.8 = (bf16[1024,768]{1,0:T(8,128)(2,1)}, bf16[1024,768]{1,0:T(8,128)(2,1)}, u32[]{:S(2)}, u32[]{:S(2)}) collective-permute-start(bf16[1024,768]{1,0:T(8,128)(2,1)} %pad_maximum_fusion.3.refs_10_), channel_id=1, source_target_pairs={{0,16},{8,24},{16,0},{24,8},{1,17},{9,25},{17,1},{25,9},{2,18},{10... | collective-permute-start | bytes 4718600 | tf_op jit(solution)/shard_map/ppermute | solution.py:221
  103.2 69.2 %collective-permute-start.3 = (bf16[1024,768]{1,0:T(8,128)(2,1)}, bf16[1024,768]{1,0:T(8,128)(2,1)}, u32[]{:S(2)}, u32[]{:S(2)}) collective-permute-start(bf16[1024,768]{1,0:T(8,128)(2,1)} %pad_maximum_fusion.2.refs_6_), channel_id=1, source_target_pairs={{0,8},{8,0},{16,24},{24,16},{1,9},{9,1},{17,25},{25,17},{2,10},{10... | collective-permute-start | bytes 4718600 | tf_op jit(solution)/shard_map/ppermute | solution.py:221
  135.9 102.1 %collective-permute-start.9 = (bf16[1024,768]{1,0:T(8,128)(2,1)}, bf16[1024,768]{1,0:T(8,128)(2,1)}, u32[]{:S(2)}, u32[]{:S(2)}) collective-permute-start(bf16[1024,768]{1,0:T(8,128)(2,1)} %collective-permute-done.7.refs_11_), channel_id=1, source_target_pairs={{0,16},{8,24},{16,0},{24,8},{1,17},{9,25},{17,1},{25,9},{2,18},{10... | collective-permute-start | bytes 4718600 | tf_op jit(solution)/shard_map/ppermute | solution.py:221
  138.7 99.3 %collective-permute-start.5 = (bf16[1024,768]{1,0:T(8,128)(2,1)}, bf16[1024,768]{1,0:T(8,128)(2,1)}, u32[]{:S(2)}, u32[]{:S(2)}) collective-permute-start(bf16[1024,768]{1,0:T(8,128)(2,1)} %collective-permute-done.4.refs_8_), channel_id=1, source_target_pairs={{0,8},{8,0},{16,24},{24,16},{1,9},{9,1},{17,25},{25,17},{2,10},{10... | collective-permute-start | bytes 4718600 | tf_op jit(solution)/shard_map/ppermute | solution.py:221
  140.5 97.5 %collective-permute-start.1 = (bf16[512,1536]{1,0:T(8,128)(2,1)}, bf16[512,1536]{1,0:T(8,128)(2,1)S(1)}, u32[]{:S(2)}, u32[]{:S(2)}) collective-permute-start(bf16[512,1536]{1,0:T(8,128)(2,1)} %bitcast.14), channel_id=1, source_target_pairs={{0,8},{8,16},{16,24},{1,9},{9,17},{17,25},{2,10},{10,18},{18,26},{... | collective-permute-start | bytes 4718600 | tf_op jit(solution)/shard_map/ppermute | solution.py:257
  238.0 1.1 copy-start.11
  294.9 4.9 %copy-start.12 = (bf16[512,768]{1,0:T(8,128)(2,1)S(1)}, bf16[512,768]{1,0:T(8,128)(2,1)}, u32[]{:S(2)}) copy-start(bf16[512,768]{1,0:T(8,128)(2,1)} %get-tuple-element.20) | copy-start | bytes 2359300
  294.9 42.2 %all-to-all-start.2 = ((bf16[8,128,768]{2,1,0:T(8,128)(2,1)}), bf16[8,128,768]{2,1,0:T(8,128)(2,1)S(1)}, u32[]{:S(2)}, u32[]{:S(2)}) async-start(bf16[8,128,768]{2,1,0:T(8,128)(2,1)} %bitcast.50), calls=%async_computation.2 | async-start | bytes 3145728 | tf_op jit(solution)/shard_map/all_to_all | solution.py:212
  299.8 21.8 %collective-permute-start.10 = (bf16[512,768]{1,0:T(8,128)(2,1)S(1)}, bf16[512,768]{1,0:T(8,128)(2,1)S(1)}, u32[]{:S(2)}, u32[]{:S(2)}) collective-permute-start(bf16[512,768]{1,0:T(8,128)(2,1)S(1)} %copy-done.12), channel_id=1, source_target_pairs={{8,0},{16,8},{24,16},{9,1},{17,9},{25,17},{10,2},{18,10},{26,18},{... | collective-permute-start | bytes 2359304 | tf_op jit(solution)/shard_map/ppermute | solution.py:262
  337.1 63.3 %all-to-all-start.3 = ((bf16[8,128,768]{2,1,0:T(8,128)(2,1)}), bf16[8,128,768]{2,1,0:T(8,128)(2,1)S(1)}, u32[]{:S(2)}, u32[]{:S(2)}) async-start(bf16[8,128,768]{2,1,0:T(8,128)(2,1)} %bitcast.37), calls=%async_computation.3 | async-start | bytes 3145728 | tf_op jit(solution)/shard_map/all_to_all | solution.py:212
  340.7 37.5 %copy-start.8 = (bf16[1024,768]{1,0:T(8,128)(2,1)S(1)}, bf16[1024,768]{1,0:T(8,128)(2,1)}, u32[]{:S(2)}) copy-start(bf16[1024,768]{1,0:T(8,128)(2,1)} %get-tuple-element.25) | copy-start | bytes 4718596
  340.7 37.5 %collective-permute-start.13 = (bf16[1024,768]{1,0:T(8,128)(2,1)}, bf16[1024,768]{1,0:T(8,128)(2,1)S(1)}, u32[]{:S(2)}, u32[]{:S(2)}) collective-permute-start(bf16[1024,768]{1,0:T(8,128)(2,1)} %get-tuple-element.26), channel_id=1, source_target_pairs={{0,8},{8,0},{16,24},{24,16},{1,9},{9,1},{17,25},{25,17},{2,10},{10... | collective-permute-start | bytes 4718600 | tf_op jit(solution)/shard_map/ppermute | solution.py:221
  340.8 54.4 %collective-permute-start.16 = (bf16[1024,768]{1,0:T(8,128)(2,1)}, bf16[1024,768]{1,0:T(8,128)(2,1)S(1)}, u32[]{:S(2)}, u32[]{:S(2)}) collective-permute-start(bf16[1024,768]{1,0:T(8,128)(2,1)} %get-tuple-element.29), channel_id=1, source_target_pairs={{0,16},{8,24},{16,0},{24,8},{1,17},{9,25},{17,1},{25,9},{2,18},{10... | collective-permute-start | bytes 4718600 | tf_op jit(solution)/shard_map/ppermute | solution.py:221
  343.4 51.7 %collective-permute-start.11 = (bf16[512,768]{1,0:T(8,128)(2,1)}, bf16[512,768]{1,0:T(8,128)(2,1)S(1)}, u32[]{:S(2)}, u32[]{:S(2)}) collective-permute-start(bf16[512,768]{1,0:T(8,128)(2,1)} %get-tuple-element.22), channel_id=1, source_target_pairs={{8,0},{16,8},{24,16},{9,1},{17,9},{25,17},{10,2},{18,10},{26,18},{... | collective-permute-start | bytes 2359304 | tf_op jit(solution)/shard_map/ppermute | solution.py:262
  346.1 82.8 %collective-permute-start.12 = (bf16[1024,768]{1,0:T(8,128)(2,1)}, bf16[1024,768]{1,0:T(8,128)(2,1)}, u32[]{:S(2)}, u32[]{:S(2)}) collective-permute-start(bf16[1024,768]{1,0:T(8,128)(2,1)} %get-tuple-element.24), channel_id=1, source_target_pairs={{0,8},{8,0},{16,24},{24,16},{1,9},{9,1},{17,25},{25,17},{2,10},{10... | collective-permute-start | bytes 4718600 | tf_op jit(solution)/shard_map/ppermute | solution.py:221
  348.8 101.7 %collective-permute-start.18 = (bf16[1024,768]{1,0:T(8,128)(2,1)}, bf16[1024,768]{1,0:T(8,128)(2,1)}, u32[]{:S(2)}, u32[]{:S(2)}) collective-permute-start(bf16[1024,768]{1,0:T(8,128)(2,1)} %get-tuple-element.30), channel_id=1, source_target_pairs={{0,16},{8,24},{16,0},{24,8},{1,17},{9,25},{17,1},{25,9},{2,18},{10... | collective-permute-start | bytes 4718600 | tf_op jit(solution)/shard_map/ppermute | solution.py:221
  378.2 16.9 %copy-start.5 = (f32[1024,768]{1,0:T(8,128)S(1)}, f32[1024,768]{1,0:T(8,128)}, u32[]{:S(2)}) copy-start(f32[1024,768]{1,0:T(8,128)} %get-tuple-element.21) | copy-start | bytes 9437188
  379.8 15.4 %copy-start.7 = (bf16[1024,768]{1,0:T(8,128)(2,1)S(1)}, bf16[1024,768]{1,0:T(8,128)(2,1)}, u32[]{:S(2)}) copy-start(bf16[1024,768]{1,0:T(8,128)(2,1)} %get-tuple-element.28) | copy-start | bytes 4718596
  379.8 66.2 %collective-permute-start.14 = (bf16[1024,768]{1,0:T(8,128)(2,1)}, bf16[1024,768]{1,0:T(8,128)(2,1)}, u32[]{:S(2)}, u32[]{:S(2)}) collective-permute-start(bf16[1024,768]{1,0:T(8,128)(2,1)} %add_convert_fusion.3), channel_id=1, source_target_pairs={{0,16},{8,24},{16,0},{24,8},{1,17},{9,25},{17,1},{25,9},{2,18},{10... | collective-permute-start | bytes 4718600 | tf_op jit(solution)/shard_map/ppermute | solution.py:221
  396.9 65.2 %collective-permute-start.17 = (bf16[1024,768]{1,0:T(8,128)(2,1)}, bf16[1024,768]{1,0:T(8,128)(2,1)}, u32[]{:S(2)}, u32[]{:S(2)}) collective-permute-start(bf16[1024,768]{1,0:T(8,128)(2,1)} %add_convert_fusion.1), channel_id=1, source_target_pairs={{0,8},{8,0},{16,24},{24,16},{1,9},{9,1},{17,25},{25,17},{2,10},{10... | collective-permute-start | bytes 4718600 | tf_op jit(solution)/shard_map/ppermute | solution.py:221
  400.4 76.4 %all-to-all-start.4 = ((bf16[8,128,768]{2,1,0:T(8,128)(2,1)}), bf16[8,128,768]{2,1,0:T(8,128)(2,1)}, u32[]{:S(2)}, u32[]{:S(2)}) async-start(bf16[8,128,768]{2,1,0:T(8,128)(2,1)} %bitcast.38), calls=%async_computation.4 | async-start | bytes 3145728 | tf_op jit(solution)/shard_map/all_to_all | solution.py:212
  449.3 12.8 %copy-start.2 = (f32[1024,768]{1,0:T(8,128)S(1)}, f32[1024,768]{1,0:T(8,128)}, u32[]{:S(2)}) copy-start(f32[1024,768]{1,0:T(8,128)} %get-tuple-element.27) | copy-start | bytes 9437188
  450.6 31.4 %collective-permute-start.15 = (bf16[512,768]{1,0:T(8,128)(2,1)}, bf16[512,768]{1,0:T(8,128)(2,1)}, u32[]{:S(2)}, u32[]{:S(2)}) collective-permute-start(bf16[512,768]{1,0:T(8,128)(2,1)} %get-tuple-element.34), channel_id=1, source_target_pairs={{0,4},{4,0},{1,5},{5,1},{2,6},{6,2},{3,7},{7,3},{8,12},{12,8},{9,1... | collective-permute-start | bytes 2359304 | tf_op jit(solution)/shard_map/ppermute | solution.py:218
  465.6 19.3 %collective-permute-start.19 = (bf16[512,768]{1,0:T(8,128)(2,1)}, bf16[512,768]{1,0:T(8,128)(2,1)}, u32[]{:S(2)}, u32[]{:S(2)}) collective-permute-start(bf16[512,768]{1,0:T(8,128)(2,1)} %get-tuple-element.32), channel_id=1, source_target_pairs={{0,4},{4,0},{1,5},{5,1},{2,6},{6,2},{3,7},{7,3},{8,12},{12,8},{9,1... | collective-permute-start | bytes 2359304 | tf_op jit(solution)/shard_map/ppermute | solution.py:218
  479.8 2.1 copy-start.3
  481.9 3.0 copy-start.4

commit v2 on v1

--- a/solution.py
+++ b/solution.py
@@ -23,12 +23,80 @@
     return lax.dot_general(a, b, ((contract[:1], contract[1:]), ((), ())), preferred_element_type=jnp.float32)
 
 
+def after(values, others):
+    return lax.optimization_barrier((values, others))[0]
+
+
+def pack(first, second, peers, split, stages):
+    rows, features = first.shape
+    width = features // (peers * stages)
+    zs = peers // split
+
+    def body(a_ref, b_ref, *outs):
+        for s in range(stages):
+            for c in range(split):
+                at = (c * stages + s) * width
+                outs[s][c, 0, :, :width] = a_ref[:, at : at + width]
+                outs[s][c, 0, :, width:] = b_ref[:, at : at + width]
+
+    return pl.pallas_call(
+        body,
+        grid=(zs,),
+        in_specs=[pl.BlockSpec((rows, features // zs), lambda z: (0, z))] * 2,
+        out_specs=[pl.BlockSpec((split, 1, rows, 2 * width), lambda z: (0, z, 0, 0))] * stages,
+        out_shape=[jax.ShapeDtypeStruct((split, zs, rows, 2 * width), first.dtype)] * stages,
+        cost_estimate=pl.CostEstimate(flops=0, bytes_accessed=8 * rows * features, transcendentals=0),
+        name="pack",
+    )(first, second)
+
+
+def unpack(moved, width, offset):
+    stages = len(moved)
+    split, zs, rows, _ = moved[0].shape
+
+    def body(*refs):
+        for s in range(stages):
+            for c in range(split):
+                at = (c * stages + s) * width
+                refs[-1][:, at : at + width] = refs[s][c, 0]
+
+    return pl.pallas_call(
+        body,
+        grid=(zs,),
+        in_specs=[pl.BlockSpec((split, 1, rows, width), lambda z: (0, z, 0, offset))] * stages,
+        out_specs=pl.BlockSpec((rows, split * stages * width), lambda z: (0, z)),
+        out_shape=jax.ShapeDtypeStruct((rows, zs * split * stages * width), moved[0].dtype),
+        cost_estimate=pl.CostEstimate(flops=0, bytes_accessed=4 * rows * zs * split * stages * width, transcendentals=0),
+        name="unpack",
+    )(*moved)
+
+
+def finish_late(dk, dv, dk_late, dv_late, back_k, back_v):
+    tokens, width = dk.shape
+    early = tokens - WINDOW
+
+    def body(k_ref, v_ref, k_late_ref, v_late_ref, back_k_ref, back_v_ref, out_ref):
+        if early:
+            out_ref[:early, :width] = k_ref[:early]
+            out_ref[:early, width:] = v_ref[:early]
+        out_ref[early:, :width] = (k_late_ref[...] + back_k_ref[...].astype(jnp.float32)).astype(out_ref.dtype)
+        out_ref[early:, width:] = (v_late_ref[...] + back_v_ref[...].astype(jnp.float32)).astype(out_ref.dtype)
+
+    return pl.pallas_call(
+        body,
+        out_shape=jax.ShapeDtypeStruct((tokens, 2 * width), dk.dtype),
+        compiler_params=pltpu.CompilerParams(vmem_limit_bytes=32 * 2**20),
+        cost_estimate=pl.CostEstimate(flops=0, bytes_accessed=12 * tokens * width, transcendentals=0),
+        name="finish_late",
+    )(dk, dv, dk_late, dv_late, back_k, back_v)
+
+
 def attention_kernel(parts, slots_ref, reads_ref, start_ref, *refs):
     q_ref, do_ref, k_ref, v_ref, kt_ref, vt_ref = refs[:6]
     refs = refs[6:]
     ck_refs, cv_refs, refs = refs[:parts], refs[parts : 2 * parts], refs[2 * parts :]
-    dq_ref, dk_ref, dv_ref, dkt_ref, dvt_ref = refs[:5]
-    refs = refs[5:]
+    dq_ref, dk_ref, dv_ref, dk_late_ref, dv_late_ref, dkt_ref, dvt_ref = refs[:7]
+    refs = refs[7:]
     gk_refs, gv_refs, refs = refs[:parts], refs[parts : 2 * parts], refs[2 * parts :]
     kx, vx, dkx, dvx = refs[:4]
     if parts > 1:
@@ -125,8 +193,10 @@
     lax.fori_loop(0, rows // TILE, tile, 0)
     dkt_ref[...] = (dkx[:WINDOW] * SCALE).astype(dkt_ref.dtype)
     dvt_ref[...] = dvx[:WINDOW].astype(dvt_ref.dtype)
-    dk_ref[...] = dkx[WINDOW:] * SCALE
-    dv_ref[...] = dvx[WINDOW:]
+    dk_ref[...] = (dkx[WINDOW:] * SCALE).astype(dk_ref.dtype)
+    dv_ref[...] = dvx[WINDOW:].astype(dv_ref.dtype)
+    dk_late_ref[...] = dkx[rows:] * SCALE
+    dv_late_ref[...] = dvx[rows:]
     if parts > 1:
         for p in range(parts):
             gk_refs[p][...] = gkx[p * part_rows : (p + 1) * part_rows].astype(gk_refs[p].dtype)
@@ -168,10 +238,11 @@
                 column(WINDOW, heads),
             ]
             + [column(part_rows)] * (2 * parts),
-            out_specs=[column(rows)] * 3 + [column(WINDOW)] * 2 + [column(part_rows)] * (2 * parts),
+            out_specs=[column(rows)] * 3 + [column(WINDOW)] * 4 + [column(part_rows)] * (2 * parts),
             scratch_shapes=scratch,
         ),
-        out_shape=[shape((rows, width), bf16), shape((rows, width), f32), shape((rows, width), f32)]
+        out_shape=[shape((rows, width), bf16)] * 3
+        + [shape((WINDOW, width), f32)] * 2
         + [shape((WINDOW, width), bf16)] * 2
         + [shape((part_rows, width), kind) for kind in kinds] * 2,
         compiler_params=pltpu.CompilerParams(vmem_limit_bytes=56 * 2**20),
@@ -180,7 +251,7 @@
         ),
         name="attention",
     )(slots, reads, start, qd, qd, kv, kv, tails, tails, *cache_k, *cache_v)
-    return outs[:5], outs[5 : 5 + parts], outs[5 + parts :]
+    return outs[:7], outs[7 : 7 + parts], outs[7 + parts :]
 
 
 def per_device(queries, keys_local, values_local, cache_keys, cache_values, block_map, retrieved, out_grad):
@@ -193,26 +264,25 @@
     head_axes = ("core", "head") if split == 2 else ("head",)
     token_axes = ("chip",) if split == 2 else ("chip", "core")
     peers = split * zs
-    width = features // peers
+    stages = groups // split
+    width = features // (peers * stages)
     tokens = rows * peers
     token_parts = chips if split == 2 else 2 * chips
     token_index = lax.axis_index(token_axes)
     relay = split == 2 and chips == 4
     seq_parts = min(8, 2 * chips) * cache_keys.shape[0] // tokens
-
-    def to_heads(arrays):
-        packed = [
-            a.reshape(rows, zs, split, width).transpose(2, 1, 0, 3).reshape(peers, rows, width) for a in arrays
-        ]
-        packed = jnp.concatenate(packed, 2)
-        moved = lax.all_to_all(packed, head_axes, split_axis=0, concat_axis=0, tiled=True)
-        return moved.reshape(tokens, len(arrays) * width)
+    bf16, f32 = jnp.bfloat16, jnp.float32
+
+    def exchange(array):
+        return lax.all_to_all(array, head_axes, split_axis=0, concat_axis=0, tiled=True)
+
+    def to_heads(packed):
+        moved = exchange(packed.reshape(peers, rows, 2 * width))
+        return moved.reshape(tokens, 2 * width)
 
     def to_tokens(array):
-        moved = lax.all_to_all(
-            array.reshape(peers, rows, width), head_axes, split_axis=0, concat_axis=0, tiled=True
-        )
-        return moved.reshape(split, zs, rows, width).transpose(2, 1, 0, 3).reshape(rows, features)
+        moved = exchange(array.reshape(peers, rows, array.shape[1]))
+        return moved.reshape(split, zs, rows, array.shape[1])
 
     def other_core(array):
         return lax.ppermute(array, "core", [(0, 1), (1, 0)])
@@ -220,20 +290,21 @@
     def other_chip(array, by):
         return lax.ppermute(array, "chip", [(i, i ^ by) for i in range(chips)])
 
-    def half(array, which):
-        return lax.dynamic_slice_in_dim(array, which * width, width, 1)
-
+    def columns(array, which, stage):
+        return lax.dynamic_slice_in_dim(array, (which * stages + stage) * width, width, 1)
+
+    def own_cache(array, stage):
+        if split == 1:
+            return array
+        return jnp.concatenate([columns(array, core, stage), other_core(columns(array, 1 - core, stage))], 0)
+
+    ids = retrieved
     if split == 2:
-        cache_k, cache_v = (
-            jnp.concatenate([half(a, core), other_core(half(a, 1 - core))], 0) for a in (cache_keys, cache_values)
-        )
         theirs = other_core(retrieved)
         ids = jnp.where(core == 0, jnp.stack([retrieved, theirs]), jnp.stack([theirs, retrieved]))
         ids = ids.reshape((-1,) + retrieved.shape[1:])
-        ids = lax.dynamic_slice_in_dim(ids, core * (groups // 2), groups // 2, 1)
-    else:
-        cache_k, cache_v, ids = cache_keys, cache_values, retrieved
-    reads = jnp.transpose(ids, (1, 0, 2)).reshape(-1)
+        ids = lax.dynamic_slice_in_dim(ids, core * stages, stages, 1)
+    reads = jnp.transpose(ids, (1, 0, 2)).reshape(stages, -1)
     owner, local = block_map // blk_dev, block_map % blk_dev
     owner_chip, owner_core = owner // 2, owner % 2
     if relay:
@@ -242,56 +313,79 @@
         owner_core = owner_core ^ core
     slots = ((owner_chip * 2 + owner_core) * blk_dev + local).astype(jnp.int32)
     start = (token_index % seq_parts == 0).astype(jnp.int32).reshape(1)
-
-    if relay:
-        k_y = other_chip(cache_k, 2)
-        v_x = other_chip(cache_v, 1)
-        k_x = other_chip(cache_k, 1)
-        v_y = other_chip(cache_v, 2)
-        all_k = [cache_k, k_x, k_y, other_chip(k_y, 1)]
-        all_v = [cache_v, v_x, v_y, other_chip(v_x, 2)]
-    else:
-        all_k, all_v = ([lax.all_gather(a, token_axes, tiled=True)] for a in (cache_k, cache_v))
-
-    kv = to_heads([keys_local, values_local])
-    tails = lax.ppermute(kv[tokens - WINDOW :], token_axes, [(i, i + 1) for i in range(token_parts - 1)])
-    qd = to_heads([queries, out_grad])
-    (dq, dk, dv, dkt, dvt), gk, gv = attention(slots, reads, start, qd, kv, tails, all_k, all_v)
-
+    forth = [(i, i + 1) for i in range(token_parts - 1)]
     back = [(i + 1, i) for i in range(token_parts - 1)]
-    dkt, dvt = lax.ppermute((dkt, dvt), token_axes, back)
-
-    def with_tail(own, tail):
-        own = jnp.concatenate([own[: tokens - WINDOW], own[tokens - WINDOW :] + tail.astype(jnp.float32)], 0)
-        return own.astype(jnp.bfloat16)
-
-    if relay:
-        bf16, f32 = jnp.bfloat16, jnp.float32
-        k_far = other_chip(gk[3], 1)
-        v_far = other_chip(gv[3], 2)
+
+    def gather_near(k, v):
+        if not relay:
+            return ()
+        return other_chip(k, 1), other_chip(k, 2), other_chip(v, 1), other_chip(v, 2)
+
+    def gather_far(k, v, near):
+        if not relay:
+            return [lax.all_gather(k, token_axes, tiled=True)], [lax.all_gather(v, token_axes, tiled=True)]
+        k_x, k_y, v_x, v_y = near
+        return [k, k_x, k_y, other_chip(k_y, 1)], [v, v_x, v_y, other_chip(v_x, 2)]
+
+    def reduce_far(gk, gv):
+        return (other_chip(gk[3], 1), other_chip(gv[3], 2)) if relay else ()
+
+    def reduce_near(gk, gv, far):
+        if not relay:
+            return [lax.psum_scatter(g[0], token_axes, scatter_dimension=0, tiled=True).astype(bf16) for g in (gk, gv)]
+        k_y = other_chip((gk[2].astype(f32) + far[0].astype(f32)).astype(bf16), 2)
+        v_x = other_chip((gv[1].astype(f32) + far[1].astype(f32)).astype(bf16), 1)
         k_x = other_chip(gk[1], 1)
         v_y = other_chip(gv[2], 2)
-        k_y = other_chip((gk[2].astype(f32) + k_far.astype(f32)).astype(bf16), 2)
-        v_x = other_chip((gv[1].astype(f32) + v_far.astype(f32)).astype(bf16), 1)
-        sum_k = (gk[0] + k_x.astype(f32) + k_y.astype(f32)).astype(bf16)
-        sum_v = (gv[0] + v_x.astype(f32) + v_y.astype(f32)).astype(bf16)
-    else:
-        sum_k, sum_v = (
-            lax.psum_scatter(g[0], token_axes, scatter_dimension=0, tiled=True).astype(jnp.bfloat16) for g in (gk, gv)
-        )
-    if split == 2:
-        own_rows = sum_k.shape[0] // 2
-
-        def to_owner(total):
-            mine, recv = total[:own_rows], other_core(total[own_rows:])
-            return jnp.where(core == 0, jnp.concatenate([mine, recv], 1), jnp.concatenate([recv, mine], 1))
-
-        sum_k, sum_v = to_owner(sum_k), to_owner(sum_v)
-
-    out_q = to_tokens(dq)
-    out_k = to_tokens(with_tail(dk, dkt))
-    out_v = to_tokens(with_tail(dv, dvt))
-    return out_q, out_k, out_v, sum_k, sum_v
+        return [(own[0] + x.astype(f32) + y.astype(f32)).astype(bf16) for own, x, y in ((gk, k_x, k_y), (gv, v_x, v_y))]
+
+    def to_owner(totals):
+        if split == 1:
+            return totals[0]
+        own_rows = totals[0].shape[0] // 2
+        mine = jnp.concatenate([t[:own_rows] for t in totals], 1)
+        recv = jnp.concatenate([other_core(t[own_rows:]) for t in totals], 1)
+        return jnp.where(core == 0, jnp.concatenate([mine, recv], 1), jnp.concatenate([recv, mine], 1))
+
+    kv = pack(keys_local, values_local, peers, split, stages)
+    qd = pack(queries, out_grad, peers, split, stages)
+    done = ()
+    ready = []
+    for s in range(stages):
+        k, v, kv_s = after((own_cache(cache_keys, s), own_cache(cache_values, s), kv[s]), done)
+        near = gather_near(k, v)
+        kv_s = to_heads(kv_s)
+        qd_s, kv_s, near = after((qd[s], kv_s, near), ())
+        far = gather_far(k, v, near)
+        tails = lax.ppermute(kv_s[tokens - WINDOW :], token_axes, forth)
+        qd_s = to_heads(qd_s)
+        done = (tails, qd_s, far)
+        ready.append((qd_s, kv_s, tails, *far))
+    grads = []
+    moved_q, moved_kv, totals_k, totals_v = [], [], [], []
+    for s in range(stages):
+        grads.append(attention(slots, reads[s], start, *ready[s]))
+    done = ready[-1]
+    for s in range(stages):
+        (dq, dk, dv, dk_late, dv_late, dkt, dvt), gk, gv = after(grads[s], done)
+        back_k, back_v = lax.ppermute((dkt, dvt), token_axes, back)
+        far = reduce_far(gk, gv)
+        dq = to_tokens(dq)
+        far, dq, dkv = after((far, dq, finish_late(dk, dv, dk_late, dv_late, back_k, back_v)), ())
+        dkv = to_tokens(dkv)
+        total_k, total_v = reduce_near(gk, gv, far)
+        done = (dkv, total_k, total_v)
+        moved_q.append(dq)
+        moved_kv.append(dkv)
+        totals_k.append(total_k)
+        totals_v.append(total_v)
+    return (
+        unpack(moved_q, width, 0),
+        unpack(moved_kv, width, 0),
+        unpack(moved_kv, width, 1),
+        to_owner(totals_k),
+        to_owner(totals_v),
+    )
 
 
 def solution(mesh):

time: 495 us -> 385 us (0.78); the launches traced: 488 us -> 383 us
  waiting for transfers between devices: 307 us -> 187 us
  local copies, waits for them, and re-layouts: 50 us -> 14.5 us
  starting transfers between devices: 48.8 us -> 79.3 us
  Pallas kernels: 55.8 us -> 82.4 us
  other arithmetic: 25.9 us -> 18.9 us
    ppermute x12 -> x24, waiting for transfers between devices: 206 us -> 110 us  [other_chip(): return lax.ppermute(array, 'chip', [(i, i ^ by) for i in range(chips)])]
    all_to_all x5 -> x8, waiting for transfers between devices: 67.4 us -> 0.02 us  [exchange(): lax.all_to_all(array, head_axes, split_axis=0, concat_axis=0, tiled=True)]
    ppermute x3 -> x6, waiting for transfers between devices: 31.8 us -> 75.6 us  [the longest x4 62.7 us: per_device(): back_k, back_v = lax.ppermute((dkt, dvt), token_axes, back)]
    reshape x11 -> x0, local copies, waits for them, and re-layouts: 34.9 us -> none  [the longest x4 17.9 us: to_heads(): a.reshape(rows, zs, split, width).transpose(2, 1, 0, 3)]
    pallas_call x0 -> x7, Pallas kernels: none -> 22.1 us  [the longest x3 11.1 us: unpack(): pl.pallas_call(body, grid=(zs,), in_specs=[pl.BlockSpec((split, 1, rows,...]
    all_to_all x5 -> x8, starting transfers between devices: 24.2 us -> 41 us  [exchange(): lax.all_to_all(array, head_axes, split_axis=0, concat_axis=0, tiled=True)]
    concatenate x6 -> x4, other arithmetic: 8.82 us -> 1.31 us  [own_cache(): jnp.concatenate([columns(array, core, stage), other_core(columns(array, 1...]
    ppermute x12 -> x24, starting transfers between devices: 17.7 us -> 24.8 us  [other_chip(): return lax.ppermute(array, 'chip', [(i, i ^ by) for i in range(chips)])]
  transfers between devices with their start and end apart: 25 -> 47, of which waited for: 13 -> 18; matrix products, arithmetic and copies ran while one was open for 13% -> 6% of each run, Pallas kernels for 0% -> 20%
where the time goes in v2:
time: 385 us; the launch traced here: 383 us
  waiting for transfers between devices  187 us (49%)
  Pallas kernels  82.4 us (21%)
  starting transfers between devices  79.3 us (21%)
  other arithmetic  18.9 us (5%)
  local copies, waits for them, and re-layouts  14.5 us (4%)
    ppermute x24, waiting for transfers between devices, other_chip(): return lax.ppermute(array, 'chip', [(i, i ^ by) for i in range(chips)])  110 us
    ppermute x4, waiting for transfers between devices, per_device(): back_k, back_v = lax.ppermute((dkt, dvt), token_axes, back)  62.7 us
    pallas_call x2, Pallas kernels, attention(): pl.pallas_call(functools.partial(attention_kernel, parts), grid_spec=pltp...  60.3 us
    all_to_all x8, starting transfers between devices, exchange(): lax.all_to_all(array, head_axes, split_axis=0, concat_axis=0, tiled=True)  41 us
    ppermute x24, starting transfers between devices, other_chip(): return lax.ppermute(array, 'chip', [(i, i ^ by) for i in range(chips)])  24.8 us
    ppermute x2, waiting for transfers between devices, per_device(): tails = lax.ppermute(kv_s[tokens - WINDOW:], token_axes, forth)  12.9 us
    pallas_call x3, Pallas kernels, unpack(): pl.pallas_call(body, grid=(zs,), in_specs=[pl.BlockSpec((split, 1, rows,...  11.1 us
    pallas_call x2, Pallas kernels, pack(): pl.pallas_call(body, grid=(zs,), in_specs=[pl.BlockSpec((rows, features /...  8.35 us
  transfers between devices with their start and end apart: 47, of which 18 were waited for; matrix products, arithmetic and copies ran while one was open for 6% of the time, Pallas kernels for 20%

profile of v2, /device:TPU:0, one launch (start us, length us, event | category | flops | bytes accessed | tf_op | source)
XLA Modules:
  0.0 383.1 jit_solution(9886745751302654783)
XLA Ops:
  0.7 2.4 constant_dynamic-slice_fusion.3
  4.6 4.2 %pack.3 = (bf16[2,4,128,768]{3,2,1,0:T(8,128)(2,1)}, bf16[2,4,128,768]{3,2,1,0:T(8,128)(2,1)}) custom-call(bf16[128,6144]{1,0:T(8,128)(2,1)} %a_ref.3, bf16[128,6144]{1,0:T(8,128)(2,1)} %b_ref.3), custom_call_target="tpu_custom_call" | custom-call | bytes 6291456 | tf_op jit(solution)/shard_map/pack/pallas_call | solution.py:42
  10.0 6.5 %all-to-all-start = ((bf16[8,128,768]{2,1,0:T(8,128)(2,1)}), bf16[8,128,768]{2,1,0:T(8,128)(2,1)S(1)}, u32[]{:S(2)}, u32[]{:S(2)}) async-start(bf16[8,128,768]{2,1,0:T(8,128)(2,1)} %bitcast.4), calls=%async_computation | async-start | bytes 3145728 | tf_op jit(solution)/shard_map/all_to_all | solution.py:277
  16.4 1.5 collective-permute-start.3
  17.9 1.5 collective-permute-start.4
  20.5 4.2 %pack.2 = (bf16[2,4,128,768]{3,2,1,0:T(8,128)(2,1)}, bf16[2,4,128,768]{3,2,1,0:T(8,128)(2,1)}) custom-call(bf16[128,6144]{1,0:T(8,128)(2,1)} %a_ref.2, bf16[128,6144]{1,0:T(8,128)(2,1)} %b_ref.2), custom_call_target="tpu_custom_call" | custom-call | bytes 6291456 | tf_op jit(solution)/shard_map/pack/pallas_call | solution.py:42
  24.7 12.2 %collective-permute-done.3.refs_7_ = bf16[1024,384]{1,0:T(8,128)(2,1)} collective-permute-done((bf16[1024,384]{1,0:T(8,128)(2,1)S(1)}, bf16[1024,384]{1,0:T(8,128)(2,1)}, u32[]{:S(2)}, u32[]{:S(2)}) %collective-permute-start.3) | collective-permute-done | bytes 786464 | tf_op jit(solution)/shard_map/ppermute | solution.py:291
  36.9 1.5 collective-permute-done.4.refs_8_
  38.4 14.9 %collective-permute-done.5.refs_11_ = bf16[1024,384]{1,0:T(8,128)(2,1)} collective-permute-done((bf16[1024,384]{1,0:T(8,128)(2,1)S(1)}, bf16[1024,384]{1,0:T(8,128)(2,1)}, u32[]{:S(2)}, u32[]{:S(2)}) %collective-permute-start.5) | collective-permute-done | bytes 786464 | tf_op jit(solution)/shard_map/ppermute | solution.py:291
  53.4 1.2 collective-permute-done.6.refs_12_
  54.6 4.7 %all-to-all-start.1 = ((bf16[8,128,768]{2,1,0:T(8,128)(2,1)}), bf16[8,128,768]{2,1,0:T(8,128)(2,1)S(1)}, u32[]{:S(2)}, u32[]{:S(2)}) async-start(bf16[8,128,768]{2,1,0:T(8,128)(2,1)} %bitcast.34), calls=%async_computation.1 | async-start | bytes 3145728 | tf_op jit(solution)/shard_map/all_to_all | solution.py:277
  59.4 2.6 collective-permute-start.7
  62.0 2.5 collective-permute-start.8
  65.0 1.2 collective-permute-done.10
  66.9 12.9 %collective-permute-done.7.refs_4_.refs_5_ = bf16[512,768]{1,0:T(8,128)(2,1)S(1)} collective-permute-done((bf16[512,768]{1,0:T(8,128)(2,1)S(1)}, bf16[512,768]{1,0:T(8,128)(2,1)S(1)}, u32[]{:S(2)}, u32[]{:S(2)}) %collective-permute-start.7) | collective-permute-done | bytes 786464 | tf_op jit(solution)/shard_map/ppermute | solution.py:360
  79.8 19.4 %collective-permute-done.8.refs_9_ = bf16[1024,384]{1,0:T(8,128)(2,1)S(1)} collective-permute-done((bf16[1024,384]{1,0:T(8,128)(2,1)}, bf16[1024,384]{1,0:T(8,128)(2,1)S(1)}, u32[]{:S(2)}, u32[]{:S(2)}) %collective-permute-start.8) | collective-permute-done | bytes 786464 | tf_op jit(solution)/shard_map/ppermute | solution.py:291
  100.1 1.1 copy-done.14
  101.3 4.7 %all-to-all-start.2 = ((bf16[8,128,768]{2,1,0:T(8,128)(2,1)}), bf16[8,128,768]{2,1,0:T(8,128)(2,1)S(1)}, u32[]{:S(2)}, u32[]{:S(2)}) async-start(bf16[8,128,768]{2,1,0:T(8,128)(2,1)} %bitcast.8), calls=%async_computation.2 | async-start | bytes 3145728 | tf_op jit(solution)/shard_map/all_to_all | solution.py:277
  107.1 1.6 collective-permute-start.14
  108.7 1.4 collective-permute-start.15
  110.1 16.3 %collective-permute-done.12.refs_7_ = bf16[1024,384]{1,0:T(8,128)(2,1)S(1)} collective-permute-done((bf16[1024,384]{1,0:T(8,128)(2,1)S(1)}, bf16[1024,384]{1,0:T(8,128)(2,1)S(1)}, u32[]{:S(2)}, u32[]{:S(2)}) %collective-permute-start.12) | collective-permute-done | bytes 786464 | tf_op jit(solution)/shard_map/ppermute | solution.py:291
  126.4 16.4 %collective-permute-done.14.refs_11_ = bf16[1024,384]{1,0:T(8,128)(2,1)S(1)} collective-permute-done((bf16[1024,384]{1,0:T(8,128)(2,1)S(1)}, bf16[1024,384]{1,0:T(8,128)(2,1)S(1)}, u32[]{:S(2)}, u32[]{:S(2)}) %collective-permute-start.14) | collective-permute-done | bytes 786464 | tf_op jit(solution)/shard_map/ppermute | solution.py:291
  143.8 4.9 %all-to-all-start.3 = ((bf16[8,128,768]{2,1,0:T(8,128)(2,1)}), bf16[8,128,768]{2,1,0:T(8,128)(2,1)}, u32[]{:S(2)}, u32[]{:S(2)}) async-start(bf16[8,128,768]{2,1,0:T(8,128)(2,1)} %bitcast.10), calls=%async_computation.3 | async-start | bytes 3145728 | tf_op jit(solution)/shard_map/all_to_all | solution.py:277
  149.8 3.8 collective-permute-start.16
  154.8 30.1 %attention.2 = (bf16[1024,384]{1,0:T(8,128)(2,1)}, bf16[1024,384]{1,0:T(8,128)(2,1)}, bf16[1024,384]{1,0:T(8,128)(2,1)}, f32[512,384]{1,0:T(8,128)}, f32[512,384...) custom-call(s32[64]{0:T(128)} %fusion.slots_ref, ...), custom_call_target="tpu_custom_call" | custom-call | flops 4529848320 | bytes 17203200 | tf_op jit(solution)/shard_map/attention/pallas_call | solution.py:227
  184.9 3.4 collective-permute-done.17.refs_9_
  188.3 5.0 %all-to-all-start.4 = ((bf16[8,128,384]{2,1,0:T(8,128)(2,1)}), bf16[8,128,384]{2,1,0:T(8,128)(2,1)S(1)}, u32[]{:S(2)}, u32[]{:S(2)}) async-start(bf16[8,128,384]{2,1,0:T(8,128)(2,1)} %bitcast.36), calls=%async_computation.4 | async-start | bytes 1572864 | tf_op jit(solution)/shard_map/all_to_all | solution.py:277
  194.8 1.3 collective-permute-start.21
  196.1 1.3 collective-permute-start.22
  197.4 24.9 %collective-permute-done.21.back_k_ref = bf16[512,384]{1,0:T(8,128)(2,1)S(1)} collective-permute-done((bf16[512,384]{1,0:T(8,128)(2,1)}, bf16[512,384]{1,0:T(8,128)(2,1)S(1)}, u32[]{:S(2)}, u32[]{:S(2)}) %collective-permute-start.21) | collective-permute-done | bytes 393248 | tf_op jit(solution)/shard_map/ppermute | solution.py:371
  222.3 8.0 %collective-permute-done.22.back_v_ref = bf16[512,384]{1,0:T(8,128)(2,1)S(1)} collective-permute-done((bf16[512,384]{1,0:T(8,128)(2,1)}, bf16[512,384]{1,0:T(8,128)(2,1)S(1)}, u32[]{:S(2)}, u32[]{:S(2)}) %collective-permute-start.22) | collective-permute-done | bytes 393248 | tf_op jit(solution)/shard_map/ppermute | solution.py:371
  230.3 1.1 copy-done.6
  231.5 1.1 copy-done.7
  232.6 1.3 finish_late.2
  234.8 4.7 %all-to-all-start.5 = ((bf16[8,128,768]{2,1,0:T(8,128)(2,1)}), bf16[8,128,768]{2,1,0:T(8,128)(2,1)}, u32[]{:S(2)}, u32[]{:S(2)}) async-start(bf16[8,128,768]{2,1,0:T(8,128)(2,1)} %bitcast.14), calls=%async_computation.5 | async-start | bytes 3145728 | tf_op jit(solution)/shard_map/all_to_all | solution.py:277
  239.6 1.3 collective-permute-start.23
  240.9 1.3 add_convert_fusion.7
  242.5 1.8 collective-permute-start.26
  246.1 30.2 %attention.3 = (bf16[1024,384]{1,0:T(8,128)(2,1)}, bf16[1024,384]{1,0:T(8,128)(2,1)}, bf16[1024,384]{1,0:T(8,128)(2,1)}, f32[512,384]{1,0:T(8,128)}, f32[512,384...) custom-call(s32[64]{0:T(128)} %fusion.slots_ref, ...), custom_call_target="tpu_custom_call" | custom-call | flops 4529848320 | bytes 17203200 | tf_op jit(solution)/shard_map/attention/pallas_call | solution.py:227
  276.3 2.6 add_convert_fusion.6
  279.0 1.2 add_convert_fusion.4
  280.2 5.2 %all-to-all-start.6 = ((bf16[8,128,384]{2,1,0:T(8,128)(2,1)}), bf16[8,128,384]{2,1,0:T(8,128)(2,1)}, u32[]{:S(2)}, u32[]{:S(2)}) async-start(bf16[8,128,384]{2,1,0:T(8,128)(2,1)} %bitcast.35), calls=%async_computation.6 | async-start | bytes 1572864 | tf_op jit(solution)/shard_map/all_to_all | solution.py:277
  285.4 1.2 collective-permute-start.27
  287.1 1.3 collective-permute-start.29
  288.4 1.3 collective-permute-start.30
  289.7 3.3 collective-permute-start.31
  293.0 21.3 %collective-permute-done.29.back_k_ref = bf16[512,384]{1,0:T(8,128)(2,1)S(1)} collective-permute-done((bf16[512,384]{1,0:T(8,128)(2,1)}, bf16[512,384]{1,0:T(8,128)(2,1)S(1)}, u32[]{:S(2)}, u32[]{:S(2)}) %collective-permute-start.29) | collective-permute-done | bytes 393248 | tf_op jit(solution)/shard_map/ppermute | solution.py:371
  314.3 8.4 %collective-permute-done.30.back_v_ref = bf16[512,384]{1,0:T(8,128)(2,1)S(1)} collective-permute-done((bf16[512,384]{1,0:T(8,128)(2,1)S(1)}, bf16[512,384]{1,0:T(8,128)(2,1)S(1)}, u32[]{:S(2)}, u32[]{:S(2)}) %collective-permute-start.30) | collective-permute-done | bytes 393248 | tf_op jit(solution)/shard_map/ppermute | solution.py:371
  322.8 1.4 finish_late.3
  324.1 5.3 %all-to-all-start.7 = ((bf16[8,128,768]{2,1,0:T(8,128)(2,1)}), bf16[8,128,768]{2,1,0:T(8,128)(2,1)S(1)}, u32[]{:S(2)}, u32[]{:S(2)}) async-start(bf16[8,128,768]{2,1,0:T(8,128)(2,1)} %bitcast.18), calls=%async_computation.7 | async-start | bytes 3145728 | tf_op jit(solution)/shard_map/all_to_all | solution.py:277
  329.5 2.3 add_convert_fusion.3
  331.8 1.4 collective-permute-start.32
  334.9 2.2 add_convert_fusion.1
  337.1 1.2 collective-permute-start.35
  339.2 3.8 unpack.3
  343.0 9.4 %collective-permute-done.32 = bf16[1024,384]{1,0:T(8,128)(2,1)} collective-permute-done((bf16[1024,384]{1,0:T(8,128)(2,1)}, bf16[1024,384]{1,0:T(8,128)(2,1)}, u32[]{:S(2)}, u32[]{:S(2)}) %collective-permute-start.32) | collective-permute-done | bytes 786464 | tf_op jit(solution)/shard_map/ppermute | solution.py:291
  352.4 1.6 add_convert_fusion.2
  354.2 14.7 %collective-permute-done.36 = bf16[1024,384]{1,0:T(8,128)(2,1)} collective-permute-done((bf16[1024,384]{1,0:T(8,128)(2,1)}, bf16[1024,384]{1,0:T(8,128)(2,1)}, u32[]{:S(2)}, u32[]{:S(2)}) %collective-permute-start.36) | collective-permute-done | bytes 786464 | tf_op jit(solution)/shard_map/ppermute | solution.py:291
  368.9 1.7 add_convert_fusion
  370.8 2.4 maximum_select_fusion
  373.2 1.4 maximum_select_fusion.1
  374.6 1.2 copy-done.8
  375.8 3.7 unpack.4
  379.4 3.7 unpack.5
  (151 shorter events, 18.2 us)
Async XLA Ops:
  3.0 5.8 %collective-permute-start.1 = (bf16[512,384]{1,0:T(8,128)(2,1)S(1)}, bf16[512,384]{1,0:T(8,128)(2,1)S(1)}, u32[]{:S(2)}, u32[]{:S(2)}) collective-permute-start(bf16[512,384]{1,0:T(8,128)(2,1)S(1)} %get-tuple-element.190), channel_id=1, source_target_pairs={{0,4},{4,0},{1,5},{5,1},{2,6},{6,2},{3,7},{7,3},{8,12},{12,8},{9,1... | collective-permute-start | bytes 1179656 | tf_op jit(solution)/shard_map/ppermute | solution.py:288
  4.6 4.3 %collective-permute-start.2 = (bf16[512,384]{1,0:T(8,128)(2,1)S(1)}, bf16[512,384]{1,0:T(8,128)(2,1)S(1)}, u32[]{:S(2)}, u32[]{:S(2)}) collective-permute-start(bf16[512,384]{1,0:T(8,128)(2,1)S(1)} %get-tuple-element.186), channel_id=1, source_target_pairs={{0,4},{4,0},{1,5},{5,1},{2,6},{6,2},{3,7},{7,3},{8,12},{12,8},{9,1... | collective-permute-start | bytes 1179656 | tf_op jit(solution)/shard_map/ppermute | solution.py:288
  8.9 9.1 %copy-start.24 = (bf16[1024,384]{1,0:T(8,128)(2,1)}, bf16[1024,384]{1,0:T(8,128)(2,1)S(1)}, u32[]{:S(2)}) copy-start(bf16[1024,384]{1,0:T(8,128)(2,1)S(1)} %pad_maximum_fusion.refs_6_) | copy-start | bytes 2359300
  10.0 9.5 %copy-start.25 = (bf16[1024,384]{1,0:T(8,128)(2,1)S(1)}, bf16[1024,384]{1,0:T(8,128)(2,1)}, u32[]{:S(2)}) copy-start(bf16[1024,384]{1,0:T(8,128)(2,1)} %pad_maximum_fusion.1.refs_10_) | copy-start | bytes 2359300
  10.0 44.6 %all-to-all-start = ((bf16[8,128,768]{2,1,0:T(8,128)(2,1)}), bf16[8,128,768]{2,1,0:T(8,128)(2,1)S(1)}, u32[]{:S(2)}, u32[]{:S(2)}) async-start(bf16[8,128,768]{2,1,0:T(8,128)(2,1)} %bitcast.4), calls=%async_computation | async-start | bytes 3145728 | tf_op jit(solution)/shard_map/all_to_all | solution.py:277
  16.4 20.4 %collective-permute-start.3 = (bf16[1024,384]{1,0:T(8,128)(2,1)S(1)}, bf16[1024,384]{1,0:T(8,128)(2,1)}, u32[]{:S(2)}, u32[]{:S(2)}) collective-permute-start(bf16[1024,384]{1,0:T(8,128)(2,1)S(1)} %pad_maximum_fusion.refs_6_), channel_id=1, source_target_pairs={{0,8},{8,0},{16,24},{24,16},{1,9},{9,1},{17,25},{25,17},{2,10},{10... | collective-permute-start | bytes 2359304 | tf_op jit(solution)/shard_map/ppermute | solution.py:291
  17.9 20.5 %collective-permute-start.4 = (bf16[1024,384]{1,0:T(8,128)(2,1)S(1)}, bf16[1024,384]{1,0:T(8,128)(2,1)}, u32[]{:S(2)}, u32[]{:S(2)}) collective-permute-start(bf16[1024,384]{1,0:T(8,128)(2,1)S(1)} %pad_maximum_fusion.refs_6_), channel_id=1, source_target_pairs={{0,16},{8,24},{16,0},{24,8},{1,17},{9,25},{17,1},{25,9},{2,18},{10... | collective-permute-start | bytes 2359304 | tf_op jit(solution)/shard_map/ppermute | solution.py:291
  19.5 33.9 %collective-permute-start.5 = (bf16[1024,384]{1,0:T(8,128)(2,1)S(1)}, bf16[1024,384]{1,0:T(8,128)(2,1)}, u32[]{:S(2)}, u32[]{:S(2)}) collective-permute-start(bf16[1024,384]{1,0:T(8,128)(2,1)S(1)} %copy-done.25), channel_id=1, source_target_pairs={{0,8},{8,0},{16,24},{24,16},{1,9},{9,1},{17,25},{25,17},{2,10},{10... | collective-permute-start | bytes 2359304 | tf_op jit(solution)/shard_map/ppermute | solution.py:291
  20.0 34.6 %collective-permute-start.6 = (bf16[1024,384]{1,0:T(8,128)(2,1)S(1)}, bf16[1024,384]{1,0:T(8,128)(2,1)}, u32[]{:S(2)}, u32[]{:S(2)}) collective-permute-start(bf16[1024,384]{1,0:T(8,128)(2,1)S(1)} %copy-done.25), channel_id=1, source_target_pairs={{0,16},{8,24},{16,0},{24,8},{1,17},{9,25},{17,1},{25,9},{2,18},{10... | collective-permute-start | bytes 2359304 | tf_op jit(solution)/shard_map/ppermute | solution.py:291
  54.6 45.6 %all-to-all-start.1 = ((bf16[8,128,768]{2,1,0:T(8,128)(2,1)}), bf16[8,128,768]{2,1,0:T(8,128)(2,1)S(1)}, u32[]{:S(2)}, u32[]{:S(2)}) async-start(bf16[8,128,768]{2,1,0:T(8,128)(2,1)} %bitcast.34), calls=%async_computation.1 | async-start | bytes 3145728 | tf_op jit(solution)/shard_map/all_to_all | solution.py:277
  59.4 20.4 %collective-permute-start.7 = (bf16[512,768]{1,0:T(8,128)(2,1)S(1)}, bf16[512,768]{1,0:T(8,128)(2,1)S(1)}, u32[]{:S(2)}, u32[]{:S(2)}) collective-permute-start(bf16[512,768]{1,0:T(8,128)(2,1)S(1)} %slice.39), channel_id=1, source_target_pairs={{0,8},{8,16},{16,24},{1,9},{9,17},{17,25},{2,10},{10,18},{18,26},{... | collective-permute-start | bytes 2359304 | tf_op jit(solution)/shard_map/ppermute | solution.py:360
  62.0 37.2 %collective-permute-start.8 = (bf16[1024,384]{1,0:T(8,128)(2,1)}, bf16[1024,384]{1,0:T(8,128)(2,1)S(1)}, u32[]{:S(2)}, u32[]{:S(2)}) collective-permute-start(bf16[1024,384]{1,0:T(8,128)(2,1)} %collective-permute-done.4.refs_8_), channel_id=1, source_target_pairs={{0,8},{8,0},{16,24},{24,16},{1,9},{9,1},{17,25},{25,17},{2,10},{10... | collective-permute-start | bytes 2359304 | tf_op jit(solution)/shard_map/ppermute | solution.py:291
  64.5 35.6 %collective-permute-start.9 = (bf16[1024,384]{1,0:T(8,128)(2,1)}, bf16[1024,384]{1,0:T(8,128)(2,1)}, u32[]{:S(2)}, u32[]{:S(2)}) collective-permute-start(bf16[1024,384]{1,0:T(8,128)(2,1)} %collective-permute-done.5.refs_11_), channel_id=1, source_target_pairs={{0,16},{8,24},{16,0},{24,8},{1,17},{9,25},{17,1},{25,9},{2,18},{10... | collective-permute-start | bytes 2359304 | tf_op jit(solution)/shard_map/ppermute | solution.py:291
  64.5 1.7 collective-permute-start.10
  64.5 2.3 collective-permute-start.11
  66.3 39.7 %copy-start.22 = (bf16[1024,384]{1,0:T(8,128)(2,1)}, bf16[1024,384]{1,0:T(8,128)(2,1)S(1)}, u32[]{:S(2)}) copy-start(bf16[1024,384]{1,0:T(8,128)(2,1)S(1)} %pad_maximum_fusion.2.refs_6_) | copy-start | bytes 2359300
  66.9 117.9 %copy-start.23 = (bf16[1024,384]{1,0:T(8,128)(2,1)}, bf16[1024,384]{1,0:T(8,128)(2,1)S(1)}, u32[]{:S(2)}) copy-start(bf16[1024,384]{1,0:T(8,128)(2,1)S(1)} %pad_maximum_fusion.3.refs_10_) | copy-start | bytes 2359300
  79.8 19.4 %copy-start.37 = (bf16[512,768]{1,0:T(8,128)(2,1)}, bf16[512,768]{1,0:T(8,128)(2,1)S(1)}, u32[]{:S(2)}) copy-start(bf16[512,768]{1,0:T(8,128)(2,1)S(1)} %collective-permute-done.7.refs_4_.refs_5_) | copy-start | bytes 2359300
  101.3 42.4 %all-to-all-start.2 = ((bf16[8,128,768]{2,1,0:T(8,128)(2,1)}), bf16[8,128,768]{2,1,0:T(8,128)(2,1)S(1)}, u32[]{:S(2)}, u32[]{:S(2)}) async-start(bf16[8,128,768]{2,1,0:T(8,128)(2,1)} %bitcast.8), calls=%async_computation.2 | async-start | bytes 3145728 | tf_op jit(solution)/shard_map/all_to_all | solution.py:277
  106.0 20.3 %collective-permute-start.12 = (bf16[1024,384]{1,0:T(8,128)(2,1)S(1)}, bf16[1024,384]{1,0:T(8,128)(2,1)S(1)}, u32[]{:S(2)}, u32[]{:S(2)}) collective-permute-start(bf16[1024,384]{1,0:T(8,128)(2,1)S(1)} %pad_maximum_fusion.2.refs_6_), channel_id=1, source_target_pairs={{0,8},{8,0},{16,24},{24,16},{1,9},{9,1},{17,25},{25,17},{2,10},{10... | collective-permute-start | bytes 2359304 | tf_op jit(solution)/shard_map/ppermute | solution.py:291
  106.0 20.4 %collective-permute-start.13 = (bf16[1024,384]{1,0:T(8,128)(2,1)S(1)}, bf16[1024,384]{1,0:T(8,128)(2,1)S(1)}, u32[]{:S(2)}, u32[]{:S(2)}) collective-permute-start(bf16[1024,384]{1,0:T(8,128)(2,1)S(1)} %pad_maximum_fusion.2.refs_6_), channel_id=1, source_target_pairs={{0,16},{8,24},{16,0},{24,8},{1,17},{9,25},{17,1},{25,9},{2,18},{10... | collective-permute-start | bytes 2359304 | tf_op jit(solution)/shard_map/ppermute | solution.py:291
  107.1 35.7 %collective-permute-start.14 = (bf16[1024,384]{1,0:T(8,128)(2,1)S(1)}, bf16[1024,384]{1,0:T(8,128)(2,1)S(1)}, u32[]{:S(2)}, u32[]{:S(2)}) collective-permute-start(bf16[1024,384]{1,0:T(8,128)(2,1)S(1)} %pad_maximum_fusion.3.refs_10_), channel_id=1, source_target_pairs={{0,8},{8,0},{16,24},{24,16},{1,9},{9,1},{17,25},{25,17},{2,10},{10... | collective-permute-start | bytes 2359304 | tf_op jit(solution)/shard_map/ppermute | solution.py:291
  108.7 35.1 %collective-permute-start.15 = (bf16[1024,384]{1,0:T(8,128)(2,1)S(1)}, bf16[1024,384]{1,0:T(8,128)(2,1)}, u32[]{:S(2)}, u32[]{:S(2)}) collective-permute-start(bf16[1024,384]{1,0:T(8,128)(2,1)S(1)} %pad_maximum_fusion.3.refs_10_), channel_id=1, source_target_pairs={{0,16},{8,24},{16,0},{24,8},{1,17},{9,25},{17,1},{25,9},{2,18},{10... | collective-permute-start | bytes 2359304 | tf_op jit(solution)/shard_map/ppermute | solution.py:291
  126.4 16.5 %copy-start.34 = (bf16[1024,384]{1,0:T(8,128)(2,1)}, bf16[1024,384]{1,0:T(8,128)(2,1)S(1)}, u32[]{:S(2)}) copy-start(bf16[1024,384]{1,0:T(8,128)(2,1)S(1)} %collective-permute-done.12.refs_7_) | copy-start | bytes 2359300
  126.4 16.4 %copy-start.35 = (bf16[1024,384]{1,0:T(8,128)(2,1)}, bf16[1024,384]{1,0:T(8,128)(2,1)S(1)}, u32[]{:S(2)}) copy-start(bf16[1024,384]{1,0:T(8,128)(2,1)S(1)} %collective-permute-done.13.refs_8_) | copy-start | bytes 2359300
  143.8 44.5 %all-to-all-start.3 = ((bf16[8,128,768]{2,1,0:T(8,128)(2,1)}), bf16[8,128,768]{2,1,0:T(8,128)(2,1)}, u32[]{:S(2)}, u32[]{:S(2)}) async-start(bf16[8,128,768]{2,1,0:T(8,128)(2,1)} %bitcast.10), calls=%async_computation.3 | async-start | bytes 3145728 | tf_op jit(solution)/shard_map/all_to_all | solution.py:277
  148.6 5.2 %collective-permute-start = (s32[8,4,4]{0,2,1:T(4,128)S(1)}, s32[8,4,4]{0,2,1:T(4,128)S(1)}, u32[]{:S(2)}, u32[]{:S(2)}) collective-permute-start(s32[8,4,4]{0,2,1:T(4,128)S(1)} %copy-done.32), channel_id=1, source_target_pairs={{0,4},{4,0},{1,5},{5,1},{2,6},{6,2},{3,7},{7,3},{8,12},{12,8},{9,1... | collective-permute-start | bytes 1544 | tf_op jit(solution)/shard_map/ppermute | solution.py:288
  149.8 35.1 %collective-permute-start.16 = (bf16[512,768]{1,0:T(8,128)(2,1)S(1)}, bf16[512,768]{1,0:T(8,128)(2,1)}, u32[]{:S(2)}, u32[]{:S(2)}) collective-permute-start(bf16[512,768]{1,0:T(8,128)(2,1)S(1)} %slice.40), channel_id=1, source_target_pairs={{0,8},{8,16},{16,24},{1,9},{9,17},{17,25},{2,10},{10,18},{18,26},{... | collective-permute-start | bytes 2359304 | tf_op jit(solution)/shard_map/ppermute | solution.py:360
  153.6 34.6 %collective-permute-start.17 = (bf16[1024,384]{1,0:T(8,128)(2,1)}, bf16[1024,384]{1,0:T(8,128)(2,1)}, u32[]{:S(2)}, u32[]{:S(2)}) collective-permute-start(bf16[1024,384]{1,0:T(8,128)(2,1)} %copy-done.35), channel_id=1, source_target_pairs={{0,8},{8,0},{16,24},{24,16},{1,9},{9,1},{17,25},{25,17},{2,10},{10... | collective-permute-start | bytes 2359304 | tf_op jit(solution)/shard_map/ppermute | solution.py:291
  153.9 34.4 %collective-permute-start.18 = (bf16[1024,384]{1,0:T(8,128)(2,1)}, bf16[1024,384]{1,0:T(8,128)(2,1)}, u32[]{:S(2)}, u32[]{:S(2)}) collective-permute-start(bf16[1024,384]{1,0:T(8,128)(2,1)} %copy-done.36), channel_id=1, source_target_pairs={{0,16},{8,24},{16,0},{24,8},{1,17},{9,25},{17,1},{25,9},{2,18},{10... | collective-permute-start | bytes 2359304 | tf_op jit(solution)/shard_map/ppermute | solution.py:291
  184.8 45.5 %copy-start.4 = (bf16[1024,384]{1,0:T(8,128)(2,1)S(1)}, bf16[1024,384]{1,0:T(8,128)(2,1)}, u32[]{:S(2)}) copy-start(bf16[1024,384]{1,0:T(8,128)(2,1)} %get-tuple-element.135.k_ref) | copy-start | bytes 2359300
  184.8 45.5 %copy-start.5 = (bf16[1024,384]{1,0:T(8,128)(2,1)S(1)}, bf16[1024,384]{1,0:T(8,128)(2,1)}, u32[]{:S(2)}) copy-start(bf16[1024,384]{1,0:T(8,128)(2,1)} %get-tuple-element.136.v_ref) | copy-start | bytes 2359300
  188.3 45.7 %all-to-all-start.4 = ((bf16[8,128,384]{2,1,0:T(8,128)(2,1)}), bf16[8,128,384]{2,1,0:T(8,128)(2,1)S(1)}, u32[]{:S(2)}, u32[]{:S(2)}) async-start(bf16[8,128,384]{2,1,0:T(8,128)(2,1)} %bitcast.36), calls=%async_computation.4 | async-start | bytes 1572864 | tf_op jit(solution)/shard_map/all_to_all | solution.py:277
  193.3 40.6 %collective-permute-start.19 = (bf16[1024,384]{1,0:T(8,128)(2,1)}, bf16[1024,384]{1,0:T(8,128)(2,1)}, u32[]{:S(2)}, u32[]{:S(2)}) collective-permute-start(bf16[1024,384]{1,0:T(8,128)(2,1)} %get-tuple-element.132), channel_id=1, source_target_pairs={{0,8},{8,0},{16,24},{24,16},{1,9},{9,1},{17,25},{25,17},{2,10},{10... | collective-permute-start | bytes 2359304 | tf_op jit(solution)/shard_map/ppermute | solution.py:291
  194.1 39.8 %collective-permute-start.20 = (bf16[1024,384]{1,0:T(8,128)(2,1)}, bf16[1024,384]{1,0:T(8,128)(2,1)S(1)}, u32[]{:S(2)}, u32[]{:S(2)}) collective-permute-start(bf16[1024,384]{1,0:T(8,128)(2,1)} %get-tuple-element.133), channel_id=1, source_target_pairs={{0,16},{8,24},{16,0},{24,8},{1,17},{9,25},{17,1},{25,9},{2,18},{10... | collective-permute-start | bytes 2359304 | tf_op jit(solution)/shard_map/ppermute | solution.py:291
  194.8 27.5 %collective-permute-start.21 = (bf16[512,384]{1,0:T(8,128)(2,1)}, bf16[512,384]{1,0:T(8,128)(2,1)S(1)}, u32[]{:S(2)}, u32[]{:S(2)}) collective-permute-start(bf16[512,384]{1,0:T(8,128)(2,1)} %get-tuple-element.139), channel_id=1, source_target_pairs={{8,0},{16,8},{24,16},{9,1},{17,9},{25,17},{10,2},{18,10},{26,18},{... | collective-permute-start | bytes 1179656 | tf_op jit(solution)/shard_map/ppermute | solution.py:371
  196.1 34.2 %collective-permute-start.22 = (bf16[512,384]{1,0:T(8,128)(2,1)}, bf16[512,384]{1,0:T(8,128)(2,1)S(1)}, u32[]{:S(2)}, u32[]{:S(2)}) collective-permute-start(bf16[512,384]{1,0:T(8,128)(2,1)} %get-tuple-element.140), channel_id=1, source_target_pairs={{8,0},{16,8},{24,16},{9,1},{17,9},{25,17},{10,2},{18,10},{26,18},{... | collective-permute-start | bytes 1179656 | tf_op jit(solution)/shard_map/ppermute | solution.py:371
  234.8 45.3 %all-to-all-start.5 = ((bf16[8,128,768]{2,1,0:T(8,128)(2,1)}), bf16[8,128,768]{2,1,0:T(8,128)(2,1)}, u32[]{:S(2)}, u32[]{:S(2)}) async-start(bf16[8,128,768]{2,1,0:T(8,128)(2,1)} %bitcast.14), calls=%async_computation.5 | async-start | bytes 3145728 | tf_op jit(solution)/shard_map/all_to_all | solution.py:277
  239.6 36.7 %collective-permute-start.23 = (bf16[1024,384]{1,0:T(8,128)(2,1)}, bf16[1024,384]{1,0:T(8,128)(2,1)}, u32[]{:S(2)}, u32[]{:S(2)}) collective-permute-start(bf16[1024,384]{1,0:T(8,128)(2,1)} %get-tuple-element.159), channel_id=1, source_target_pairs={{0,8},{8,0},{16,24},{24,16},{1,9},{9,1},{17,25},{25,17},{2,10},{10... | collective-permute-start | bytes 2359304 | tf_op jit(solution)/shard_map/ppermute | solution.py:291
  242.2 34.1 %collective-permute-start.24 = (bf16[1024,384]{1,0:T(8,128)(2,1)S(1)}, bf16[1024,384]{1,0:T(8,128)(2,1)}, u32[]{:S(2)}, u32[]{:S(2)}) collective-permute-start(bf16[1024,384]{1,0:T(8,128)(2,1)S(1)} %add_convert_fusion.7), channel_id=1, source_target_pairs={{0,16},{8,24},{16,0},{24,8},{1,17},{9,25},{17,1},{25,9},{2,18},{10... | collective-permute-start | bytes 2359304 | tf_op jit(solution)/shard_map/ppermute | solution.py:291
  242.5 36.4 %collective-permute-start.26 = (bf16[1024,384]{1,0:T(8,128)(2,1)}, bf16[1024,384]{1,0:T(8,128)(2,1)S(1)}, u32[]{:S(2)}, u32[]{:S(2)}) collective-permute-start(bf16[1024,384]{1,0:T(8,128)(2,1)} %get-tuple-element.165), channel_id=1, source_target_pairs={{0,16},{8,24},{16,0},{24,8},{1,17},{9,25},{17,1},{25,9},{2,18},{10... | collective-permute-start | bytes 2359304 | tf_op jit(solution)/shard_map/ppermute | solution.py:291
  244.5 34.4 %collective-permute-start.25 = (bf16[1024,384]{1,0:T(8,128)(2,1)S(1)}, bf16[1024,384]{1,0:T(8,128)(2,1)S(1)}, u32[]{:S(2)}, u32[]{:S(2)}) collective-permute-start(bf16[1024,384]{1,0:T(8,128)(2,1)S(1)} %add_convert_fusion.5), channel_id=1, source_target_pairs={{0,8},{8,0},{16,24},{24,16},{1,9},{9,1},{17,25},{25,17},{2,10},{10... | collective-permute-start | bytes 2359304 | tf_op jit(solution)/shard_map/ppermute | solution.py:291
  246.1 30.2 %copy-start.18 = (f32[1024,384]{1,0:T(8,128)S(1)}, f32[1024,384]{1,0:T(8,128)}, u32[]{:S(2)}) copy-start(f32[1024,384]{1,0:T(8,128)} %get-tuple-element.158) | copy-start | bytes 4718596
  279.0 9.4 %copy-start.39 = (bf16[512,384]{1,0:T(8,128)(2,1)S(1)}, bf16[512,384]{1,0:T(8,128)(2,1)}, u32[]{:S(2)}) copy-start(bf16[512,384]{1,0:T(8,128)(2,1)} %get-tuple-element.174) | copy-start | bytes 1179652
  279.0 43.8 %copy-start.2 = (f32[512,384]{1,0:T(8,128)S(1)}, f32[512,384]{1,0:T(8,128)}, u32[]{:S(2)}) copy-start(f32[512,384]{1,0:T(8,128)} %get-tuple-element.171.k_late_ref) | copy-start | bytes 2359300
  279.0 43.8 %copy-start.3 = (f32[512,384]{1,0:T(8,128)S(1)}, f32[512,384]{1,0:T(8,128)}, u32[]{:S(2)}) copy-start(f32[512,384]{1,0:T(8,128)} %get-tuple-element.172.v_late_ref) | copy-start | bytes 2359300
  280.2 42.6 %copy-start = (bf16[1024,384]{1,0:T(8,128)(2,1)S(1)}, bf16[1024,384]{1,0:T(8,128)(2,1)}, u32[]{:S(2)}) copy-start(bf16[1024,384]{1,0:T(8,128)(2,1)} %get-tuple-element.169.k_ref) | copy-start | bytes 2359300
  280.2 42.6 %copy-start.1 = (bf16[1024,384]{1,0:T(8,128)(2,1)S(1)}, bf16[1024,384]{1,0:T(8,128)(2,1)}, u32[]{:S(2)}) copy-start(bf16[1024,384]{1,0:T(8,128)(2,1)} %get-tuple-element.170.v_ref) | copy-start | bytes 2359300
  280.2 43.9 %all-to-all-start.6 = ((bf16[8,128,384]{2,1,0:T(8,128)(2,1)}), bf16[8,128,384]{2,1,0:T(8,128)(2,1)}, u32[]{:S(2)}, u32[]{:S(2)}) async-start(bf16[8,128,384]{2,1,0:T(8,128)(2,1)} %bitcast.35), calls=%async_computation.6 | async-start | bytes 1572864 | tf_op jit(solution)/shard_map/all_to_all | solution.py:277
  285.4 38.8 %collective-permute-start.27 = (bf16[1024,384]{1,0:T(8,128)(2,1)}, bf16[1024,384]{1,0:T(8,128)(2,1)}, u32[]{:S(2)}, u32[]{:S(2)}) collective-permute-start(bf16[1024,384]{1,0:T(8,128)(2,1)} %get-tuple-element.166), channel_id=1, source_target_pairs={{0,8},{8,0},{16,24},{24,16},{1,9},{9,1},{17,25},{25,17},{2,10},{10... | collective-permute-start | bytes 2359304 | tf_op jit(solution)/shard_map/ppermute | solution.py:291
  286.6 37.5 %collective-permute-start.28 = (bf16[1024,384]{1,0:T(8,128)(2,1)}, bf16[1024,384]{1,0:T(8,128)(2,1)}, u32[]{:S(2)}, u32[]{:S(2)}) collective-permute-start(bf16[1024,384]{1,0:T(8,128)(2,1)} %get-tuple-element.167), channel_id=1, source_target_pairs={{0,16},{8,24},{16,0},{24,8},{1,17},{9,25},{17,1},{25,9},{2,18},{10... | collective-permute-start | bytes 2359304 | tf_op jit(solution)/shard_map/ppermute | solution.py:291
  287.1 27.3 %collective-permute-start.29 = (bf16[512,384]{1,0:T(8,128)(2,1)}, bf16[512,384]{1,0:T(8,128)(2,1)S(1)}, u32[]{:S(2)}, u32[]{:S(2)}) collective-permute-start(bf16[512,384]{1,0:T(8,128)(2,1)} %get-tuple-element.173), channel_id=1, source_target_pairs={{8,0},{16,8},{24,16},{9,1},{17,9},{25,17},{10,2},{18,10},{26,18},{... | collective-permute-start | bytes 1179656 | tf_op jit(solution)/shard_map/ppermute | solution.py:371
  288.4 34.4 %collective-permute-start.30 = (bf16[512,384]{1,0:T(8,128)(2,1)S(1)}, bf16[512,384]{1,0:T(8,128)(2,1)S(1)}, u32[]{:S(2)}, u32[]{:S(2)}) collective-permute-start(bf16[512,384]{1,0:T(8,128)(2,1)S(1)} %copy-done.39), channel_id=1, source_target_pairs={{8,0},{16,8},{24,16},{9,1},{17,9},{25,17},{10,2},{18,10},{26,18},{... | collective-permute-start | bytes 1179656 | tf_op jit(solution)/shard_map/ppermute | solution.py:371
  289.7 53.3 %collective-permute-start.31 = (bf16[1024,384]{1,0:T(8,128)(2,1)}, bf16[1024,384]{1,0:T(8,128)(2,1)}, u32[]{:S(2)}, u32[]{:S(2)}) collective-permute-start(bf16[1024,384]{1,0:T(8,128)(2,1)} %get-tuple-element.178), channel_id=1, source_target_pairs={{0,8},{8,0},{16,24},{24,16},{1,9},{9,1},{17,25},{25,17},{2,10},{10... | collective-permute-start | bytes 2359304 | tf_op jit(solution)/shard_map/ppermute | solution.py:291
  324.1 50.5 %all-to-all-start.7 = ((bf16[8,128,768]{2,1,0:T(8,128)(2,1)}), bf16[8,128,768]{2,1,0:T(8,128)(2,1)S(1)}, u32[]{:S(2)}, u32[]{:S(2)}) async-start(bf16[8,128,768]{2,1,0:T(8,128)(2,1)} %bitcast.18), calls=%async_computation.7 | async-start | bytes 3145728 | tf_op jit(solution)/shard_map/all_to_all | solution.py:277
  331.8 20.7 %collective-permute-start.32 = (bf16[1024,384]{1,0:T(8,128)(2,1)}, bf16[1024,384]{1,0:T(8,128)(2,1)}, u32[]{:S(2)}, u32[]{:S(2)}) collective-permute-start(bf16[1024,384]{1,0:T(8,128)(2,1)} %add_convert_fusion.3), channel_id=1, source_target_pairs={{0,16},{8,24},{16,0},{24,8},{1,17},{9,25},{17,1},{25,9},{2,18},{10... | collective-permute-start | bytes 2359304 | tf_op jit(solution)/shard_map/ppermute | solution.py:291
  334.0 36.7 %collective-permute-start.33 = (bf16[512,384]{1,0:T(8,128)(2,1)}, bf16[512,384]{1,0:T(8,128)(2,1)}, u32[]{:S(2)}, u32[]{:S(2)}) collective-permute-start(bf16[512,384]{1,0:T(8,128)(2,1)} %get-tuple-element.198), channel_id=1, source_target_pairs={{0,4},{4,0},{1,5},{5,1},{2,6},{6,2},{3,7},{7,3},{8,12},{12,8},{9,1... | collective-permute-start | bytes 1179656 | tf_op jit(solution)/shard_map/ppermute | solution.py:288
  334.3 34.6 %collective-permute-start.36 = (bf16[1024,384]{1,0:T(8,128)(2,1)}, bf16[1024,384]{1,0:T(8,128)(2,1)}, u32[]{:S(2)}, u32[]{:S(2)}) collective-permute-start(bf16[1024,384]{1,0:T(8,128)(2,1)} %get-tuple-element.184), channel_id=1, source_target_pairs={{0,16},{8,24},{16,0},{24,8},{1,17},{9,25},{17,1},{25,9},{2,18},{10... | collective-permute-start | bytes 2359304 | tf_op jit(solution)/shard_map/ppermute | solution.py:291
  337.1 31.8 %collective-permute-start.35 = (bf16[1024,384]{1,0:T(8,128)(2,1)}, bf16[1024,384]{1,0:T(8,128)(2,1)}, u32[]{:S(2)}, u32[]{:S(2)}) collective-permute-start(bf16[1024,384]{1,0:T(8,128)(2,1)} %add_convert_fusion.1), channel_id=1, source_target_pairs={{0,8},{8,0},{16,24},{24,16},{1,9},{9,1},{17,25},{25,17},{2,10},{10... | collective-permute-start | bytes 2359304 | tf_op jit(solution)/shard_map/ppermute | solution.py:291
  339.2 13.2 %copy-start.19 = (f32[1024,384]{1,0:T(8,128)S(1)}, f32[1024,384]{1,0:T(8,128)}, u32[]{:S(2)}) copy-start(f32[1024,384]{1,0:T(8,128)} %get-tuple-element.177) | copy-start | bytes 4718596
  343.0 30.2 %collective-permute-start.37 = (bf16[512,384]{1,0:T(8,128)(2,1)}, bf16[512,384]{1,0:T(8,128)(2,1)S(1)}, u32[]{:S(2)}, u32[]{:S(2)}) collective-permute-start(bf16[512,384]{1,0:T(8,128)(2,1)} %get-tuple-element.194), channel_id=1, source_target_pairs={{0,4},{4,0},{1,5},{5,1},{2,6},{6,2},{3,7},{7,3},{8,12},{12,8},{9,1... | collective-permute-start | bytes 1179656 | tf_op jit(solution)/shard_map/ppermute | solution.py:288
  354.1 14.9 %copy-start.16 = (f32[1024,384]{1,0:T(8,128)S(1)}, f32[1024,384]{1,0:T(8,128)}, u32[]{:S(2)}) copy-start(f32[1024,384]{1,0:T(8,128)} %get-tuple-element.181) | copy-start | bytes 4718596
  354.2 16.6 %collective-permute-start.34 = (bf16[512,384]{1,0:T(8,128)(2,1)S(1)}, bf16[512,384]{1,0:T(8,128)(2,1)S(1)}, u32[]{:S(2)}, u32[]{:S(2)}) collective-permute-start(bf16[512,384]{1,0:T(8,128)(2,1)S(1)} %get-tuple-element.200), channel_id=1, source_target_pairs={{0,4},{4,0},{1,5},{5,1},{2,6},{6,2},{3,7},{7,3},{8,12},{12,8},{9,1... | collective-permute-start | bytes 1179656 | tf_op jit(solution)/shard_map/ppermute | solution.py:288
  370.7 2.5 collective-permute-start.38
  (23 other events, 84.5 us)

commit v3 on v1

v3 whole, which is shorter than its diff:
```python
import functools
import math

import jax
import jax.numpy as jnp
from jax import lax
from jax.experimental import pallas as pl
from jax.experimental.pallas import tpu as pltpu
from jax.sharding import Mesh
from jax.sharding import PartitionSpec as P

HEAD_DIM = 128
GROUP_HEADS = 3
BLOCK = 64
READS = 4
WINDOW = 512
TILE = 128
MASKED = -1e30
UNROLL = 4
SCALE = 1.0 / math.sqrt(HEAD_DIM)


def dot(a, b, contract):
    return lax.dot_general(a, b, ((contract[:1], contract[1:]), ((), ())), preferred_element_type=jnp.float32)


def after(values, others):
    return lax.optimization_barrier((values, others))[0]


def moved_bytes(count):
    return pl.CostEstimate(flops=0, bytes_accessed=count, transcendentals=0)


def pack_tokens(arrays, split, zs, cuts):
    rows, features = arrays[0].shape
    group = features // (split * zs)
    count = len(arrays)

    def body(*refs):
        for out, (low, high) in zip(refs[count:], cuts):
            for c in range(split):
                for n in range(count):
                    out[c, 0, :, n * (high - low) : (n + 1) * (high - low)] = refs[n][:, c * group + low : c * group + high]

    widths = [count * (high - low) for low, high in cuts]
    return pl.pallas_call(
        body,
        grid=(zs,),
        in_specs=[pl.BlockSpec((rows, features // zs), lambda z: (0, z))] * count,
        out_specs=[pl.BlockSpec((split, 1, rows, w), lambda z: (0, z, 0, 0)) for w in widths],
        out_shape=[jax.ShapeDtypeStruct((split, zs, rows, w), arrays[0].dtype) for w in widths],
        cost_estimate=moved_bytes(4 * count * rows * features),
        name="pack_tokens",
    )(*arrays)


def unpack_tokens(moved, cuts, count):
    split, zs, rows, _ = moved[0].shape
    group = cuts[-1][1]

    def body(*refs):
        for ref, (low, high) in zip(refs, cuts):
            for c in range(split):
                for n in range(count):
                    refs[len(cuts) + n][:, c * group + low : c * group + high] = ref[
                        c, 0, :, n * (high - low) : (n + 1) * (high - low)
                    ]

    features = zs * split * group
    return pl.pallas_call(
        body,
        grid=(zs,),
        in_specs=[pl.BlockSpec((split, 1, rows, m.shape[3]), lambda z: (0, z, 0, 0)) for m in moved],
        out_specs=[pl.BlockSpec((rows, split * group), lambda z: (0, z))] * count,
        out_shape=[jax.ShapeDtypeStruct((rows, features), moved[0].dtype)] * count,
        cost_estimate=moved_bytes(4 * count * rows * features),
        name="unpack_tokens",
    )(*moved)


def pack_cache(cache_k, cache_v, order):
    rows, features = cache_k.shape
    parts = order.shape[0]
    group = features // parts

    def body(order_ref, k_ref, v_ref, *outs):
        for p in range(parts):

            @pl.when(pl.program_id(0) == p)
            def _(p=p):
                outs[p][:, :group] = k_ref[...]
                outs[p][:, group:] = v_ref[...]

    return pl.pallas_call(
        body,
        grid_spec=pltpu.PrefetchScalarGridSpec(
            num_scalar_prefetch=1,
            grid=(parts,),
            in_specs=[pl.BlockSpec((rows, group), lambda p, order: (0, order[p]))] * 2,
            out_specs=[pl.BlockSpec((rows, 2 * group), lambda p, order: (0, 0))] * parts,
        ),
        out_shape=[jax.ShapeDtypeStruct((rows, 2 * group), cache_k.dtype)] * parts,
        compiler_params=pltpu.CompilerParams(vmem_limit_bytes=32 * 2**20),
        cost_estimate=moved_bytes(8 * rows * features),
        name="pack_cache",
    )(order, cache_k, cache_v)


def sum_cores(mine_k, mine_v, recv_k, recv_v, parts):
    rows, width = mine_k.shape[0] // parts, mine_k.shape[1]

    def body(mine_k_ref, mine_v_ref, recv_k_ref, recv_v_ref, *outs):
        for p in range(parts):

            @pl.when(pl.program_id(0) == p)
            def _(p=p):
                outs[p][:, :width] = (mine_k_ref[...] + recv_k_ref[...]).astype(outs[p].dtype)
                outs[p][:, width:] = (mine_v_ref[...] + recv_v_ref[...]).astype(outs[p].dtype)

    return pl.pallas_call(
        body,
        grid=(parts,),
        in_specs=[pl.BlockSpec((rows, width), lambda p: (p, 0))] * 4,
        out_specs=[pl.BlockSpec((rows, 2 * width), lambda p: (0, 0))] * parts,
        out_shape=[jax.ShapeDtypeStruct((rows, 2 * width), jnp.bfloat16)] * parts,
        compiler_params=pltpu.CompilerParams(vmem_limit_bytes=32 * 2**20),
        cost_estimate=moved_bytes(20 * parts * rows * width),
        name="sum_cores",
    )(mine_k, mine_v, recv_k, recv_v)


def place_cache(stages, order, cuts):
    parts = order.shape[0]
    rows, group = stages[0][0].shape[0], cuts[-1][1]
    arrays = [a for stage in stages for a in stage]

    def body(order_ref, *refs):
        k_ref, v_ref = refs[len(arrays) :]
        for p in range(parts):

            @pl.when(pl.program_id(0) == p)
            def _(p=p):
                for s, (low, high) in enumerate(cuts):
                    k_ref[:, low:high] = refs[s * parts + p][:, : high - low]
                    v_ref[:, low:high] = refs[s * parts + p][:, high - low :]

    return pl.pallas_call(
        body,
        grid_spec=pltpu.PrefetchScalarGridSpec(
            num_scalar_prefetch=1,
            grid=(parts,),
            in_specs=[pl.BlockSpec(a.shape, lambda p, order: (0, 0)) for a in arrays],
            out_specs=[pl.BlockSpec((rows, group), lambda p, order: (0, order[p]))] * 2,
        ),
        out_shape=[jax.ShapeDtypeStruct((rows, parts * group), arrays[0].dtype)] * 2,
        compiler_params=pltpu.CompilerParams(vmem_limit_bytes=32 * 2**20),
        cost_estimate=moved_bytes(8 * rows * parts * group),
        name="place_cache",
    )(order, *arrays)


def finish_tokens(back_at, back_on, dq, dk, dv, back_k, back_v):
    tokens, width = dq.shape

    def body(back_at_ref, back_on_ref, dq_ref, dk_ref, dv_ref, back_k_ref, back_v_ref, out_ref):
        on = back_on_ref[pl.program_id(0)] > 0
        out_ref[:, :width] = dq_ref[...]
        out_ref[:, width : 2 * width] = (dk_ref[...] + jnp.where(on, back_k_ref[...], 0.0)).astype(out_ref.dtype)
        out_ref[:, 2 * width :] = (dv_ref[...] + jnp.where(on, back_v_ref[...], 0.0)).astype(out_ref.dtype)

    own = pl.BlockSpec((WINDOW, width), lambda j, at, on: (j, 0))
    back = pl.BlockSpec((WINDOW, width), lambda j, at, on: (at[j], 0))
    return pl.pallas_call(
        body,
        grid_spec=pltpu.PrefetchScalarGridSpec(
            num_scalar_prefetch=2,
            grid=(tokens // WINDOW,),
            in_specs=[own, own, own, back, back],
            out_specs=pl.BlockSpec((WINDOW, 3 * width), lambda j, at, on: (j, 0)),
        ),
        out_shape=jax.ShapeDtypeStruct((tokens, 3 * width), jnp.bfloat16),
        compiler_params=pltpu.CompilerParams(vmem_limit_bytes=32 * 2**20),
        cost_estimate=moved_bytes(24 * tokens * width),
        name="finish_tokens",
    )(back_at, back_on, dq, dk, dv, back_k, back_v)


def attention_kernel(parts, outs, first_head, slots_ref, reads_ref, before_ref, start_ref, order_ref, *refs):
    q_ref, do_ref, k_ref, v_ref, kt_ref, vt_ref = refs[:6]
    refs = refs[6:]
    ck_refs, cv_refs, refs = refs[:parts], refs[parts : 2 * parts], refs[2 * parts :]
    dq_ref, dk_ref, dv_ref, dkt_ref, dvt_ref = refs[:5]
    refs = refs[5:]
    gk_refs, gv_refs, refs = refs[:outs], refs[outs : 2 * outs], refs[2 * outs :]
    kx, vx, dkx, dvx = refs[:4]
    if parts > 1:
        ckx, cvx, gkx, gvx = refs[4:]
    else:
        ckx, cvx, gkx, gvx = ck_refs[0], cv_refs[0], gk_refs[0], gv_refs[0]
    rows = q_ref.shape[0]
    span = WINDOW + TILE
    chunk, chunks = pl.program_id(1), pl.num_programs(1)
    group = (first_head + pl.program_id(0)) // GROUP_HEADS
    table = (group * chunks + order_ref[chunk]) * (rows // BLOCK)

    kx[:WINDOW] = kt_ref[...]
    kx[WINDOW:] = k_ref[...]
    vx[:WINDOW] = vt_ref[...]
    vx[WINDOW:] = v_ref[...]
    dkx[...] = jnp.zeros_like(dkx)
    dvx[...] = jnp.zeros_like(dvx)

    @pl.when(chunk == 0)
    def _():
        gkx[...] = jnp.zeros_like(gkx)
        gvx[...] = jnp.zeros_like(gvx)
        if parts > 1:
            part_rows = ck_refs[0].shape[0]
            for p in range(parts):
                ckx[p * part_rows : (p + 1) * part_rows] = ck_refs[p][...]
                cvx[p * part_rows : (p + 1) * part_rows] = cv_refs[p][...]

    key_at = lax.broadcasted_iota(jnp.int32, (TILE, TILE), 0)
    query_at = lax.broadcasted_iota(jnp.int32, (TILE, TILE), 1)
    first_half = lax.broadcasted_iota(jnp.int32, (1, TILE), 1) < BLOCK
    first_rows = lax.broadcasted_iota(jnp.int32, (TILE, 1), 0) < BLOCK
    at_start = start_ref[chunk]

    def tile(t, carry):
        at = pl.multiple_of(t * TILE, TILE)
        q = q_ref[pl.ds(at, TILE)]
        do = do_ref[pl.ds(at, TILE)]
        k_loc = kx[pl.ds(at, span)]
        v_loc = vx[pl.ds(at, span)]
        places = []
        k_mem, v_mem = [], []
        for b in range(TILE // BLOCK):
            block = (table + t * (TILE // BLOCK) + b) * READS
            where = [pl.multiple_of(slots_ref[reads_ref[block + r]] * BLOCK, BLOCK) for r in range(READS)]
            places.append(where)
            k_mem.append(jnp.concatenate([ckx[pl.ds(w, BLOCK)] for w in where], 0))
            v_mem.append(jnp.concatenate([cvx[pl.ds(w, BLOCK)] for w in where], 0))

        s_loc = dot(k_loc, q, (1, 1))
        s_mem = jnp.where(first_half, dot(k_mem[0], q, (1, 1)), dot(k_mem[1], q, (1, 1)))
        pieces = []
        for c in range(span // TILE):
            piece = s_loc[c * TILE : (c + 1) * TILE]
            if c < span // TILE - 1:
                before = (at_start > 0) & (at + c * TILE < WINDOW)
                piece = piece + jnp.where(before, MASKED, 0.0)
            else:
                piece = jnp.where(key_at <= query_at, piece, MASKED)
            if c == 0:
                piece = jnp.where(key_at >= query_at, piece, MASKED)
            pieces.append(piece)
        s_loc = jnp.concatenate(pieces, 0)
        top = jnp.maximum(jnp.max(s_loc, 0, keepdims=True), jnp.max(s_mem, 0, keepdims=True))
        unit = SCALE * math.log2(math.e)
        e_loc = jnp.exp2((s_loc - top) * unit)
        e_mem = jnp.exp2((s_mem - top) * unit)
        total = jnp.sum(e_loc, 0, keepdims=True) + jnp.sum(e_mem, 0, keepdims=True)
        inverse = 1.0 / total
        p_loc = e_loc * inverse
        p_mem = e_mem * inverse
        w_loc = p_loc.astype(jnp.bfloat16)
        w_mem = p_mem.astype(jnp.bfloat16)
        dp_loc = dot(v_loc, do, (1, 1))
        dp_mem = jnp.where(first_half, dot(v_mem[0], do, (1, 1)), dot(v_mem[1], do, (1, 1)))
        delta = jnp.sum(w_loc.astype(jnp.float32) * dp_loc, 0, keepdims=True) + jnp.sum(
            w_mem.astype(jnp.float32) * dp_mem, 0, keepdims=True
        )
        ds_loc = (p_loc * (dp_loc - delta)).astype(jnp.bfloat16)
        ds_mem = (p_mem * (dp_mem - delta)).astype(jnp.bfloat16)

        dq_mem = jnp.where(first_rows, dot(ds_mem, k_mem[0], (0, 0)), dot(ds_mem, k_mem[1], (0, 0)))
        dq_ref[pl.ds(at, TILE)] = ((dot(ds_loc, k_loc, (0, 0)) + dq_mem) * SCALE).astype(dq_ref.dtype)
        dkx[pl.ds(at, span)] += dot(ds_loc, q, (1, 0))
        dvx[pl.ds(at, span)] += dot(w_loc, do, (1, 0))
        zero = jnp.zeros_like(q)
        q_two = jnp.concatenate([jnp.where(first_rows, q, zero), jnp.where(first_rows, zero, q)], 1)
        do_two = jnp.concatenate([jnp.where(first_rows, do, zero), jnp.where(first_rows, zero, do)], 1)
        read_k = (dot(ds_mem, q_two, (1, 0)) * SCALE).astype(jnp.bfloat16).astype(jnp.float32)
        read_v = dot(w_mem, do_two, (1, 0)).astype(jnp.bfloat16).astype(jnp.float32)
        for b in range(TILE // BLOCK):
            for r in range(READS):
                here = (slice(r * BLOCK, (r + 1) * BLOCK), slice(b * HEAD_DIM, (b + 1) * HEAD_DIM))
                gkx[pl.ds(places[b][r], BLOCK)] += read_k[here]
                gvx[pl.ds(places[b][r], BLOCK)] += read_v[here]
        return carry

    lax.fori_loop(0, rows // TILE, tile, 0, unroll=UNROLL)
    dkt_ref[...] = dkx[:WINDOW] * SCALE
    dvt_ref[...] = dvx[:WINDOW]
    dk_ref[...] = dkx[WINDOW:] * SCALE
    dv_ref[...] = dvx[WINDOW:]
    if parts > 1:

        @pl.when(chunk == chunks - 1)
        def _():
            out_rows = gk_refs[0].shape[0]
            for p in range(outs):
                gk_refs[p][...] = gkx[p * out_rows : (p + 1) * out_rows]
                gv_refs[p][...] = gvx[p * out_rows : (p + 1) * out_rows]


def attention(tables, tokens_in, prev, cache, cut, group_width):
    rows, width = tokens_in.shape[0], tokens_in.shape[1] // 4
    heads, first_head = width // HEAD_DIM, cut[0] // HEAD_DIM
    group_heads = group_width // HEAD_DIM
    parts, part_rows = len(cache), cache[0].shape[0]
    outs = min(2, parts)
    out_rows = parts * part_rows // outs

    def chunk_of(offset):
        return pl.BlockSpec((WINDOW, HEAD_DIM), lambda h, j, *_: (j, h + offset))

    def before(offset):
        return pl.BlockSpec((WINDOW, HEAD_DIM), lambda h, j, slots, reads, at, *_: (at[j], h + offset))

    def column(height, offset):
        return pl.BlockSpec((height, HEAD_DIM), lambda h, j, *_: (0, h + offset))

    bf16, f32 = jnp.bfloat16, jnp.float32
    shape = jax.ShapeDtypeStruct
    scratch = [pltpu.VMEM((2 * WINDOW, HEAD_DIM), kind) for kind in (bf16, bf16, f32, f32)]
    if parts > 1:
        scratch += [pltpu.VMEM((parts * part_rows, HEAD_DIM), kind) for kind in (bf16, bf16, f32, f32)]
    pairs = heads * rows * (WINDOW + TILE + 2 * READS * BLOCK)
    results = pl.pallas_call(
        functools.partial(attention_kernel, parts, outs, first_head),
        grid_spec=pltpu.PrefetchScalarGridSpec(
            num_scalar_prefetch=5,
            grid=(heads, rows // WINDOW),
            in_specs=[chunk_of(n * heads) for n in range(4)]
            + [before(0), before(heads)]
            + [column(part_rows, first_head)] * parts
            + [column(part_rows, first_head + group_heads)] * parts,
            out_specs=[chunk_of(0)] * 5 + [column(out_rows, 0)] * (2 * outs),
            scratch_shapes=scratch,
        ),
        out_shape=[shape((rows, width), bf16)]
        + [shape((rows, width), f32)] * 4
        + [shape((out_rows, width), f32)] * (2 * outs),
        compiler_params=pltpu.CompilerParams(vmem_limit_bytes=56 * 2**20),
        cost_estimate=pl.CostEstimate(
            flops=10 * pairs * HEAD_DIM, bytes_accessed=heads * part_rows * parts * 3000, transcendentals=pairs
        ),
        name="attention",
    )(*tables, *[tokens_in] * 4, prev, prev, *cache, *cache)
    return results[:5], results[5 : 5 + outs], results[5 + outs :]


def per_device(queries, keys_local, values_local, cache_keys, cache_values, block_map, retrieved, out_grad):
    chips, zs = lax.axis_size("chip"), lax.axis_size("head")
    chip, core = lax.axis_index("chip"), lax.axis_index("core")
    rows, features = queries.shape
    cache_rows = cache_keys.shape[0]
    blk_dev = cache_rows // BLOCK
    groups = retrieved.shape[1]
    shared = groups == chips and chips in (2, 4)
    split = chips if shared else 1
    head_axes = ("chip", "head") if shared else ("head",)
    peers = split * zs
    group_width = features // peers
    low = group_width - group_width // GROUP_HEADS
    cuts = ((0, low), (low, group_width))
    tokens = rows * peers
    chunks = tokens // WINDOW
    seq_parts = min(8, 2 * chips)
    numbers = jnp.arange(chunks, dtype=jnp.int32)
    bf16, f32 = jnp.bfloat16, jnp.float32

    def exchange(array):
        return lax.all_to_all(array, head_axes, split_axis=0, concat_axis=0, tiled=True)

    def to_heads(packed):
        return exchange(packed.reshape(peers, rows, packed.shape[3])).reshape(tokens, packed.shape[3])

    def to_tokens(array):
        return exchange(array.reshape(peers, rows, array.shape[1])).reshape(split, zs, rows, array.shape[1])

    def other_core(array):
        return lax.ppermute(array, "core", [(0, 1), (1, 0)])

    def other_chip(array, by):
        return lax.ppermute(array, "chip", [(i, i ^ by) for i in range(chips)]) if by else array

    everyone = ("chip", "core")
    parts = 2 * chips
    if shared:
        before, back_at = jnp.maximum(numbers - 1 + core, 0), jnp.minimum(numbers + core, chunks - 1)
        back_on = (numbers + core < chunks).astype(jnp.int32)
        start = ((2 * numbers + core) % seq_parts == 0).astype(jnp.int32)
        order = jnp.arange(chips, dtype=jnp.int32) ^ chip
        ids = jnp.stack([other_chip(retrieved, k) for k in range(chips)])
        reads = lax.dynamic_slice_in_dim(ids, chip, 1, 2)
        reads = reads.reshape(-1)
    else:
        before, back_at, back_on = numbers, numbers, numbers + 1
        start = (lax.axis_index(everyone) % seq_parts == 0).astype(jnp.int32) + numbers
        order = numbers
        reads = jnp.transpose(retrieved, (1, 0, 2)).reshape(-1)
    owner, local = block_map // blk_dev, block_map % blk_dev
    if shared:
        slots = (((owner % 2) ^ core) * chips + ((owner // 2) ^ chip)) * blk_dev + local
    else:
        slots = block_map
    before, back_at, start = (a.astype(jnp.int32) for a in (before, back_at, start))
    tables = (slots.astype(jnp.int32), reads, before, start, order.astype(jnp.int32))

    packed = pack_tokens([queries, out_grad, keys_local, values_local], split, zs, cuts)
    if shared:
        pieces = pack_cache(cache_keys, cache_values, order)
        mine = [other_chip(piece, k) for k, piece in enumerate(pieces)]
        cache = mine + [other_core(piece) for piece in mine]
    else:
        cache = [lax.all_gather(jnp.concatenate([cache_keys, cache_values], 1), everyone, tiled=True)]

    def chunks_before(keys_values):
        if shared:
            return other_core(keys_values)
        return lax.ppermute(keys_values, everyone, [(i, i + 1) for i in range(parts - 1)])

    def send_back(grads):
        if shared:
            return other_core(grads)
        return lax.ppermute(grads, everyone, [(i + 1, i) for i in range(parts - 1)])

    def run(stage, moved):
        (low, high), width = cuts[stage], cuts[stage][1] - cuts[stage][0]
        prev = chunks_before(moved[:, 2 * width :])
        (dq, dk, dv, dkt, dvt), gk, gv = attention(tables, moved, prev, cache, cuts[stage], group_width)
        back_k, back_v = send_back(dkt), send_back(dvt)
        out = finish_tokens(back_at, back_on, dq, dk, dv, back_k, back_v)
        if not shared:
            sums = [lax.psum_scatter(g[0], everyone, scatter_dimension=0, tiled=True).astype(bf16) for g in (gk, gv)]
            return out, sums
        return out, sum_cores(gk[0], gv[0], other_core(gk[1]), other_core(gv[1]), chips)

    moved_a = to_heads(packed[0])
    moved_a, second, cache, tables = after((moved_a, packed[1], cache, tables), ())
    moved_b = to_heads(second)
    out_a, sums_a = run(0, moved_a)
    out_a, moved_b = after((out_a, moved_b), ())
    out_a = to_tokens(out_a)
    out_b, sums_b = run(1, moved_b)
    if shared:
        sums_a = [other_chip(s, k) for k, s in enumerate(sums_a)]
    out_b, out_a, sums_a = after((out_b, out_a, sums_a), ())
    if shared:
        sums_b = [other_chip(s, k) for k, s in enumerate(sums_b)]
        grad_cache = place_cache([sums_a, sums_b], order.astype(jnp.int32), cuts)
    else:
        grad_cache = [jnp.concatenate([a, b], 1) for a, b in zip(sums_a, sums_b)]
    out_b = to_tokens(out_b)
    return (*unpack_tokens([out_a, out_b], cuts, 3), *grad_cache)


def solution(mesh):
    shape = mesh.shape
    fine = Mesh(mesh.devices.reshape(shape["mem"] // 2, 2, shape["head"]), ("chip", "core", "head"))
    by_token = P(("chip", "core", "head"), None)
    by_block = P(("chip", "core"), "head")
    return jax.shard_map(
        per_device,
        mesh=fine,
        in_specs=(
            by_token,
            by_token,
            by_token,
            by_block,
            by_block,
            P(),
            P(("chip", "core"), "head", None),
            by_token,
        ),
        out_specs=(by_token, by_token, by_token, by_block, by_block),
        check_vma=False,
    )
```

time: 495 us -> 311 us (0.63); the launches traced: 488 us -> 310 us
  waiting for transfers between devices: 307 us -> 175 us
  local copies, waits for them, and re-layouts: 50 us -> 13.6 us
  other arithmetic: 25.9 us -> 1.6 us
  Pallas kernels: 55.8 us -> 77 us
  starting transfers between devices: 48.8 us -> 41.9 us
    ppermute x15 -> x12, waiting for transfers between devices: 238 us -> 129 us  [other_chip(): lax.ppermute(array, 'chip', [(i, i ^ by) for i in range(chips)])]
    all_to_all x5 -> x4, waiting for transfers between devices: 67.4 us -> 28.7 us  [exchange(): lax.all_to_all(array, head_axes, split_axis=0, concat_axis=0, tiled=True)]
    reshape x11 -> x1, local copies, waits for them, and re-layouts: 34.9 us -> 0.59 us  [per_device(): reads = reads.reshape(-1)]
    pallas_call x1 -> x10, Pallas kernels: 55.8 us -> 77 us  [the longest x2 53.5 us: attention(): pl.pallas_call(functools.partial(attention_kernel, parts, outs, first_hea...]
    ppermute x5 -> x14, waiting for transfers between devices: 1.53 us -> 17.4 us  [other_core(): return lax.ppermute(array, 'core', [(0, 1), (1, 0)])]
    ppermute x15 -> x12, starting transfers between devices: 23.9 us -> 12.5 us  [other_chip(): lax.ppermute(array, 'chip', [(i, i ^ by) for i in range(chips)])]
    concatenate x6 -> x0, other arithmetic: 8.82 us -> none  [the longest x2 3.84 us: to_heads(): packed = jnp.concatenate(packed, 2)]
    convert_element_type x4 -> x2, other arithmetic: 8.83 us -> 0.53 us  [the longest x1 0.52 us: per_device(): start = ((2 * numbers + core) % seq_parts == 0).astype(jnp.int32)]
  transfers between devices with their start and end apart: 25 -> 30, of which waited for: 13 -> 18; matrix products, arithmetic and copies ran while one was open for 13% -> 1% of each run, Pallas kernels for 0% -> 21%
where the time goes in v3:
time: 311 us; the launch traced here: 310 us
  waiting for transfers between devices  175 us (56%)
  Pallas kernels  77 us (25%)
  starting transfers between devices  41.9 us (13%)
  local copies, waits for them, and re-layouts  13.6 us (4%)
    ppermute x12, waiting for transfers between devices, other_chip(): lax.ppermute(array, 'chip', [(i, i ^ by) for i in range(chips)])  129 us
    pallas_call x2, Pallas kernels, attention(): pl.pallas_call(functools.partial(attention_kernel, parts, outs, first_hea...  53.5 us
    all_to_all x4, waiting for transfers between devices, exchange(): lax.all_to_all(array, head_axes, split_axis=0, concat_axis=0, tiled=True)  28.7 us
    all_to_all x4, starting transfers between devices, exchange(): lax.all_to_all(array, head_axes, split_axis=0, concat_axis=0, tiled=True)  26.4 us
    ppermute x14, waiting for transfers between devices, other_core(): return lax.ppermute(array, 'core', [(0, 1), (1, 0)])  17.4 us
    ppermute x12, starting transfers between devices, other_chip(): lax.ppermute(array, 'chip', [(i, i ^ by) for i in range(chips)])  12.5 us
    unnamed x48, local copies, waits for them, and re-layouts  8.44 us
  transfers between devices with their start and end apart: 30, of which 18 were waited for; matrix products, arithmetic and copies ran while one was open for 1% of the time, Pallas kernels for 21%

profile of v3, /device:TPU:0, one launch (start us, length us, event | category | flops | bytes accessed | tf_op | source)
XLA Modules:
  0.0 309.9 jit_solution(9935769483272283823)
XLA Ops:
  0.6 6.0 %pack_tokens.1 = (bf16[4,4,128,1024]{3,2,1,0:T(8,128)(2,1)}, bf16[4,4,128,512]{3,2,1,0:T(8,128)(2,1)}) custom-call(bf16[128,6144]{1,0:T(8,128)(2,1)} %refs_0_.1, bf16[128,6144]{1,0:T(8,128)(2,1)} %refs_1_.1, bf16[128,6144]{1,0:T(8,128)(2,1)} %refs_2_.1, bf16[128,6144]{1,0:T(8,128)(2,1)} %refs_3_.1), custom_call_target="tpu_custom_call" | custom-call | bytes 12582912 | tf_op jit(solution)/shard_map/pack_tokens/pallas_call | solution.py:47
  6.7 8.5 %all-to-all-start = ((bf16[16,128,1024]{2,1,0:T(8,128)(2,1)}), bf16[16,128,1024]{2,1,0:T(8,128)(2,1)}, u32[]{:S(2)}, u32[]{:S(2)}) async-start(bf16[16,128,1024]{2,1,0:T(8,128)(2,1)} %bitcast.16), calls=%async_computation | async-start | bytes 8388608 | tf_op jit(solution)/shard_map/all_to_all | solution.py:376
  15.2 1.4 copy-done.6
  16.6 1.3 pack_cache.1
  18.0 1.9 collective-permute-start
  19.9 1.5 collective-permute-start.1
  21.4 0.1 collective-permute-start.2
  21.5 59.1 %collective-permute-done.refs_7_.refs_15_ = bf16[512,768]{1,0:T(8,128)(2,1)S(1)} collective-permute-done((bf16[512,768]{1,0:T(8,128)(2,1)S(1)}, bf16[512,768]{1,0:T(8,128)(2,1)S(1)}, u32[]{:S(2)}, u32[]{:S(2)}) %collective-permute-start) | collective-permute-done | bytes 786464 | tf_op jit(solution)/shard_map/ppermute | solution.py:388
  80.7 0.5 collective-permute-start.5
  81.2 16.3 %collective-permute-done.2.refs_9_.refs_17_ = bf16[512,768]{1,0:T(8,128)(2,1)} collective-permute-done((bf16[512,768]{1,0:T(8,128)(2,1)S(1)}, bf16[512,768]{1,0:T(8,128)(2,1)}, u32[]{:S(2)}, u32[]{:S(2)}) %collective-permute-start.2) | collective-permute-done | bytes 786464 | tf_op jit(solution)/shard_map/ppermute | solution.py:388
  97.5 0.6 collective-permute-start.7
  98.1 0.5 fusion.3.slots_ref
  98.6 2.5 collective-permute-done.7
  101.1 0.6 collective-permute-start.8
  101.7 0.5 add_maximum_fusion.before_ref
  102.2 2.5 collective-permute-done.8
  104.8 0.6 collective-permute-start.9
  105.4 0.5 compare_convert_fusion.start_ref
  105.9 3.4 %collective-permute-done.9 = s32[8,4,4]{0,2,1:T(4,128)S(1)} collective-permute-done((s32[8,4,4]{0,2,1:T(4,128)S(1)}, s32[8,4,4]{0,2,1:T(4,128)S(1)}, u32[]{:S(2)}, u32[]{:S(2)}) %collective-permute-start.9) | collective-permute-done | bytes 544 | tf_op jit(solution)/shard_map/ppermute | solution.py:388
  109.4 0.6 reshape.39.reads_ref
  110.1 9.8 %all-to-all-done = bf16[16,128,1024]{2,1,0:T(8,128)(2,1)} async-done(((bf16[16,128,1024]{2,1,0:T(8,128)(2,1)}), bf16[16,128,1024]{2,1,0:T(8,128)(2,1)}, u32[]{:S(2)}, u32[]{:S(2)}) %all-to-all-start) | async-done | bytes 4194336 | tf_op jit(solution)/shard_map/all_to_all | solution.py:376
  119.9 3.1 %slice.6 = bf16[2048,512]{1,0:T(8,128)(2,1)} slice(bf16[2048,1024]{1,0:T(8,128)(2,1)} %bitcast.1.refs_0_.refs_1_.refs_2_.refs_3_), slice={[0:2048], [512:1024]} | slice | bytes 4194304 | tf_op jit(solution)/shard_map/slice | solution.py:433
  123.1 4.8 %all-to-all-start.1 = ((bf16[16,128,512]{2,1,0:T(8,128)(2,1)}), bf16[16,128,512]{2,1,0:T(8,128)(2,1)}, u32[]{:S(2)}, u32[]{:S(2)}) async-start(bf16[16,128,512]{2,1,0:T(8,128)(2,1)} %bitcast.17), calls=%async_computation.1 | async-start | bytes 4194304 | tf_op jit(solution)/shard_map/all_to_all | solution.py:376
  127.9 34.1 %attention.2 = (bf16[2048,256]{1,0:T(8,128)(2,1)}, f32[2048,256]{1,0:T(8,128)}, f32[2048,256]{1,0:T(8,128)}, f32[2048,256]{1,0:T(8,128)}, f32[2048,256]{1,0:T(8,...) custom-call(s32[64]{0:T(128)} %fusion.3.slots_ref, ...), custom_call_target="tpu_custom_call" | custom-call | flops 6039797760 | bytes 24576000 | tf_op jit(solution)/shard_map/attention/pallas_call | solution.py:331
  162.0 0.3 collective-permute-start.11
  162.3 0.3 collective-permute-start.12
  162.6 3.8 %collective-permute-done.11.back_k_ref = f32[2048,256]{1,0:T(8,128)S(1)} collective-permute-done((f32[2048,256]{1,0:T(8,128)}, f32[2048,256]{1,0:T(8,128)S(1)}, u32[]{:S(2)}, u32[]{:S(2)}) %collective-permute-start.11) | collective-permute-done | bytes 2097184 | tf_op jit(solution)/shard_map/ppermute | solution.py:385
  166.5 3.0 collective-permute-done.12.back_v_ref
  169.5 1.6 copy-done.1
  171.1 1.6 copy-done.2
  172.7 1.2 copy-done.7
  173.9 3.0 finish_tokens.2
  176.9 3.8 %all-to-all-done.1 = bf16[16,128,512]{2,1,0:T(8,128)(2,1)} async-done(((bf16[16,128,512]{2,1,0:T(8,128)(2,1)}), bf16[16,128,512]{2,1,0:T(8,128)(2,1)}, u32[]{:S(2)}, u32[]{:S(2)}) %all-to-all-start.1) | async-done | bytes 2097184 | tf_op jit(solution)/shard_map/all_to_all | solution.py:376
  180.7 4.7 %all-to-all-start.2 = ((bf16[16,128,768]{2,1,0:T(8,128)(2,1)}), bf16[16,128,768]{2,1,0:T(8,128)(2,1)}, u32[]{:S(2)}, u32[]{:S(2)}) async-start(bf16[16,128,768]{2,1,0:T(8,128)(2,1)} %bitcast.8), calls=%async_computation.2 | async-start | bytes 6291456 | tf_op jit(solution)/shard_map/all_to_all | solution.py:376
  185.5 0.5 collective-permute-start.17
  186.0 1.3 slice.7
  187.4 6.7 %collective-permute-done.13.refs_4_.refs_5_ = bf16[2048,256]{1,0:T(8,128)(2,1)S(1)} collective-permute-done((bf16[2048,256]{1,0:T(8,128)(2,1)S(1)}, bf16[2048,256]{1,0:T(8,128)(2,1)S(1)}, u32[]{:S(2)}, u32[]{:S(2)}) %collective-permute-start.13) | collective-permute-done | bytes 1048608 | tf_op jit(solution)/shard_map/ppermute | solution.py:385
  194.1 1.0 copy-done.21
  195.1 19.4 %attention.3 = (bf16[2048,128]{1,0:T(8,128)(2,1)}, f32[2048,128]{1,0:T(8,128)}, f32[2048,128]{1,0:T(8,128)}, f32[2048,128]{1,0:T(8,128)}, f32[2048,128]{1,0:T(8,...) custom-call(s32[64]{0:T(128)} %fusion.3.slots_ref, ...), custom_call_target="tpu_custom_call" | custom-call | flops 3019898880 | bytes 12288000 | tf_op jit(solution)/shard_map/attention/pallas_call | solution.py:331
  214.4 0.2 collective-permute-start.14
  214.6 0.4 collective-permute-start.15
  215.1 2.7 sum_cores.2
  217.7 1.7 collective-permute-start.18
  219.4 1.5 collective-permute-start.19
  220.9 0.4 collective-permute-start.20
  221.3 2.4 finish_tokens.3
  223.7 12.2 %collective-permute-done.18.refs_1_ = bf16[512,512]{1,0:T(8,128)(2,1)S(1)} collective-permute-done((bf16[512,512]{1,0:T(8,128)(2,1)S(1)}, bf16[512,512]{1,0:T(8,128)(2,1)S(1)}, u32[]{:S(2)}, u32[]{:S(2)}) %collective-permute-start.18) | collective-permute-done | bytes 524320 | tf_op jit(solution)/shard_map/ppermute | solution.py:388
  235.9 0.8 copy-done.12
  236.7 11.0 %collective-permute-done.20.refs_3_ = bf16[512,512]{1,0:T(8,128)(2,1)S(1)} collective-permute-done((bf16[512,512]{1,0:T(8,128)(2,1)S(1)}, bf16[512,512]{1,0:T(8,128)(2,1)S(1)}, u32[]{:S(2)}, u32[]{:S(2)}) %collective-permute-start.20) | collective-permute-done | bytes 524320 | tf_op jit(solution)/shard_map/ppermute | solution.py:388
  247.7 0.8 copy-done.14
  248.5 9.4 %all-to-all-done.2 = bf16[16,128,768]{2,1,0:T(8,128)(2,1)} async-done(((bf16[16,128,768]{2,1,0:T(8,128)(2,1)}), bf16[16,128,768]{2,1,0:T(8,128)(2,1)}, u32[]{:S(2)}, u32[]{:S(2)}) %all-to-all-start.2) | async-done | bytes 3145760 | tf_op jit(solution)/shard_map/all_to_all | solution.py:376
  257.9 8.4 %all-to-all-start.3 = ((bf16[16,128,384]{2,1,0:T(8,128)(2,1)}), bf16[16,128,384]{2,1,0:T(8,128)(2,1)}, u32[]{:S(2)}, u32[]{:S(2)}) async-start(bf16[16,128,384]{2,1,0:T(8,128)(2,1)} %bitcast.10), calls=%async_computation.3 | async-start | bytes 3145728 | tf_op jit(solution)/shard_map/all_to_all | solution.py:376
  266.5 0.5 collective-permute-start.22
  267.0 2.4 collective-permute-done.21.recv_k_ref
  269.3 1.5 collective-permute-done.22.recv_v_ref
  270.8 0.3 sum_cores.3
  271.2 1.9 collective-permute-start.23
  273.1 1.5 collective-permute-start.24
  274.5 0.2 collective-permute-start.25
  274.7 16.2 %collective-permute-done.23.refs_5_ = bf16[512,256]{1,0:T(8,128)(2,1)S(1)} collective-permute-done((bf16[512,256]{1,0:T(8,128)(2,1)S(1)}, bf16[512,256]{1,0:T(8,128)(2,1)S(1)}, u32[]{:S(2)}, u32[]{:S(2)}) %collective-permute-start.23) | collective-permute-done | bytes 262176 | tf_op jit(solution)/shard_map/ppermute | solution.py:388
  291.0 5.5 %collective-permute-done.25.refs_7_ = bf16[512,256]{1,0:T(8,128)(2,1)S(1)} collective-permute-done((bf16[512,256]{1,0:T(8,128)(2,1)S(1)}, bf16[512,256]{1,0:T(8,128)(2,1)S(1)}, u32[]{:S(2)}, u32[]{:S(2)}) %collective-permute-start.25) | collective-permute-done | bytes 262176 | tf_op jit(solution)/shard_map/ppermute | solution.py:388
  296.5 2.8 place_cache.1
  299.3 5.7 %all-to-all-done.3 = bf16[16,128,384]{2,1,0:T(8,128)(2,1)} async-done(((bf16[16,128,384]{2,1,0:T(8,128)(2,1)}), bf16[16,128,384]{2,1,0:T(8,128)(2,1)}, u32[]{:S(2)}, u32[]{:S(2)}) %all-to-all-start.3) | async-done | bytes 1572896 | tf_op jit(solution)/shard_map/all_to_all | solution.py:376
  304.9 5.0 %unpack_tokens.1 = (bf16[128,6144]{1,0:T(8,128)(2,1)}, bf16[128,6144]{1,0:T(8,128)(2,1)}, bf16[128,6144]{1,0:T(8,128)(2,1)}) custom-call(bf16[4,4,128,768]{3,2,1,0:T(8,128)(2,1)} %bitcast.9.refs_0_, bf16[4,4,128,384]{3,2,1,0:T(8,128)(2,1)} %bitcast.11.refs_1_), custom_call_target="tpu_custom_call" | custom-call | bytes 9437184 | tf_op jit(solution)/shard_map/unpack_tokens/pallas_call | solution.py:71
  (65 shorter events, 0.6 us)
Async XLA Ops:
  6.7 8.5 %copy-start.5 = (bf16[512,1536]{1,0:T(8,128)(2,1)S(1)}, bf16[512,1536]{1,0:T(8,128)(2,1)}, u32[]{:S(2)}) copy-start(bf16[512,1536]{1,0:T(8,128)(2,1)} %k_ref.1) | copy-start | bytes 4718596
  6.7 113.2 %all-to-all-start = ((bf16[16,128,1024]{2,1,0:T(8,128)(2,1)}), bf16[16,128,1024]{2,1,0:T(8,128)(2,1)}, u32[]{:S(2)}, u32[]{:S(2)}) async-start(bf16[16,128,1024]{2,1,0:T(8,128)(2,1)} %bitcast.16), calls=%async_computation | async-start | bytes 8388608 | tf_op jit(solution)/shard_map/all_to_all | solution.py:376
  15.2 82.3 %copy-start.22 = (s32[8,4,4]{0,2,1:T(4,128)S(1)}, s32[8,4,4]{0,2,1:T(4,128)}, u32[]{:S(2)}) copy-start(s32[8,4,4]{0,2,1:T(4,128)} %param.14) | copy-start | bytes 1540
  15.2 82.9 %copy-start.23 = (s32[64]{0:T(128)S(1)}, s32[64]{0:T(128)}, u32[]{:S(2)}) copy-start(s32[64]{0:T(128)} %param.13) | copy-start | bytes 772
  15.2 1.4 copy-start.6
  16.6 106.4 %copy-start.17 = (s32[4]{0:T(128)}, s32[4]{0:T(128)S(1)}, u32[]{:S(2)}) copy-start(s32[4]{0:T(128)S(1)} %iota_xor_fusion.order_ref) | copy-start | bytes 52
  18.0 105.0 %copy-start = (bf16[512,768]{1,0:T(8,128)(2,1)}, bf16[512,768]{1,0:T(8,128)(2,1)S(1)}, u32[]{:S(2)}) copy-start(bf16[512,768]{1,0:T(8,128)(2,1)S(1)} %get-tuple-element.77.refs_6_.refs_14_) | copy-start | bytes 2359300
  18.0 62.7 %collective-permute-start = (bf16[512,768]{1,0:T(8,128)(2,1)S(1)}, bf16[512,768]{1,0:T(8,128)(2,1)S(1)}, u32[]{:S(2)}, u32[]{:S(2)}) collective-permute-start(bf16[512,768]{1,0:T(8,128)(2,1)S(1)} %get-tuple-element.68), channel_id=1, source_target_pairs={{0,8},{8,0},{16,24},{24,16},{1,9},{9,1},{17,25},{25,17},{2,10},{10... | collective-permute-start | bytes 2359304 | tf_op jit(solution)/shard_map/ppermute | solution.py:388
  19.9 60.8 %collective-permute-start.1 = (bf16[512,768]{1,0:T(8,128)(2,1)S(1)}, bf16[512,768]{1,0:T(8,128)(2,1)}, u32[]{:S(2)}, u32[]{:S(2)}) collective-permute-start(bf16[512,768]{1,0:T(8,128)(2,1)S(1)} %get-tuple-element.69), channel_id=1, source_target_pairs={{0,16},{8,24},{16,0},{24,8},{1,17},{9,25},{17,1},{25,9},{2,18},{10... | collective-permute-start | bytes 2359304 | tf_op jit(solution)/shard_map/ppermute | solution.py:388
  21.4 76.1 %collective-permute-start.2 = (bf16[512,768]{1,0:T(8,128)(2,1)S(1)}, bf16[512,768]{1,0:T(8,128)(2,1)}, u32[]{:S(2)}, u32[]{:S(2)}) collective-permute-start(bf16[512,768]{1,0:T(8,128)(2,1)S(1)} %get-tuple-element.70), channel_id=1, source_target_pairs={{0,24},{8,16},{16,8},{24,0},{1,25},{9,17},{17,9},{25,1},{2,26},{10... | collective-permute-start | bytes 2359304 | tf_op jit(solution)/shard_map/ppermute | solution.py:388
  21.5 88.5 %collective-permute-start.3 = (bf16[512,768]{1,0:T(8,128)(2,1)S(1)}, bf16[512,768]{1,0:T(8,128)(2,1)}, u32[]{:S(2)}, u32[]{:S(2)}) collective-permute-start(bf16[512,768]{1,0:T(8,128)(2,1)S(1)} %get-tuple-element.77.refs_6_.refs_14_), channel_id=1, source_target_pairs={{0,4},{4,0},{1,5},{5,1},{2,6},{6,2},{3,7},{7,3},{8,12},{12,8},{9,1... | collective-permute-start | bytes 2359304 | tf_op jit(solution)/shard_map/ppermute | solution.py:385
  80.7 42.3 %copy-start.19 = (bf16[512,768]{1,0:T(8,128)(2,1)}, bf16[512,768]{1,0:T(8,128)(2,1)S(1)}, u32[]{:S(2)}) copy-start(bf16[512,768]{1,0:T(8,128)(2,1)S(1)} %collective-permute-done.refs_7_.refs_15_) | copy-start | bytes 2359300
  80.7 29.3 %collective-permute-start.4 = (bf16[512,768]{1,0:T(8,128)(2,1)S(1)}, bf16[512,768]{1,0:T(8,128)(2,1)}, u32[]{:S(2)}, u32[]{:S(2)}) collective-permute-start(bf16[512,768]{1,0:T(8,128)(2,1)S(1)} %collective-permute-done.refs_7_.refs_15_), channel_id=1, source_target_pairs={{0,4},{4,0},{1,5},{5,1},{2,6},{6,2},{3,7},{7,3},{8,12},{12,8},{9,1... | collective-permute-start | bytes 2359304 | tf_op jit(solution)/shard_map/ppermute | solution.py:385
  80.7 29.3 %collective-permute-start.5 = (bf16[512,768]{1,0:T(8,128)(2,1)}, bf16[512,768]{1,0:T(8,128)(2,1)}, u32[]{:S(2)}, u32[]{:S(2)}) collective-permute-start(bf16[512,768]{1,0:T(8,128)(2,1)} %collective-permute-done.1.refs_8_.refs_16_), channel_id=1, source_target_pairs={{0,4},{4,0},{1,5},{5,1},{2,6},{6,2},{3,7},{7,3},{8,12},{12,8},{9,1... | collective-permute-start | bytes 2359304 | tf_op jit(solution)/shard_map/ppermute | solution.py:385
  97.5 12.6 %collective-permute-start.6 = (bf16[512,768]{1,0:T(8,128)(2,1)}, bf16[512,768]{1,0:T(8,128)(2,1)S(1)}, u32[]{:S(2)}, u32[]{:S(2)}) collective-permute-start(bf16[512,768]{1,0:T(8,128)(2,1)} %collective-permute-done.2.refs_9_.refs_17_), channel_id=1, source_target_pairs={{0,4},{4,0},{1,5},{5,1},{2,6},{6,2},{3,7},{7,3},{8,12},{12,8},{9,1... | collective-permute-start | bytes 2359304 | tf_op jit(solution)/shard_map/ppermute | solution.py:385
  97.5 3.7 %collective-permute-start.7 = (s32[8,4,4]{0,2,1:T(4,128)S(1)}, s32[8,4,4]{0,2,1:T(4,128)S(1)}, u32[]{:S(2)}, u32[]{:S(2)}) collective-permute-start(s32[8,4,4]{0,2,1:T(4,128)S(1)} %copy-done.22), channel_id=1, source_target_pairs={{0,8},{8,0},{16,24},{24,16},{1,9},{9,1},{17,25},{25,17},{2,10},{10... | collective-permute-start | bytes 1544 | tf_op jit(solution)/shard_map/ppermute | solution.py:388
  101.1 3.7 %collective-permute-start.8 = (s32[8,4,4]{0,2,1:T(4,128)S(1)}, s32[8,4,4]{0,2,1:T(4,128)S(1)}, u32[]{:S(2)}, u32[]{:S(2)}) collective-permute-start(s32[8,4,4]{0,2,1:T(4,128)S(1)} %copy-done.22), channel_id=1, source_target_pairs={{0,16},{8,24},{16,0},{24,8},{1,17},{9,25},{17,1},{25,9},{2,18},{10... | collective-permute-start | bytes 1544 | tf_op jit(solution)/shard_map/ppermute | solution.py:388
  104.8 4.5 %collective-permute-start.9 = (s32[8,4,4]{0,2,1:T(4,128)S(1)}, s32[8,4,4]{0,2,1:T(4,128)S(1)}, u32[]{:S(2)}, u32[]{:S(2)}) collective-permute-start(s32[8,4,4]{0,2,1:T(4,128)S(1)} %copy-done.22), channel_id=1, source_target_pairs={{0,24},{8,16},{16,8},{24,0},{1,25},{9,17},{17,9},{25,1},{2,26},{10... | collective-permute-start | bytes 1544 | tf_op jit(solution)/shard_map/ppermute | solution.py:388
  110.0 13.0 %copy-start.20 = (bf16[512,768]{1,0:T(8,128)(2,1)}, bf16[512,768]{1,0:T(8,128)(2,1)S(1)}, u32[]{:S(2)}) copy-start(bf16[512,768]{1,0:T(8,128)(2,1)S(1)} %collective-permute-done.6.refs_13_.refs_21_) | copy-start | bytes 2359300
  123.0 4.8 %collective-permute-start.10 = (bf16[2048,512]{1,0:T(8,128)(2,1)}, bf16[2048,512]{1,0:T(8,128)(2,1)}, u32[]{:S(2)}, u32[]{:S(2)}) collective-permute-start(bf16[2048,512]{1,0:T(8,128)(2,1)} %slice.6), channel_id=1, source_target_pairs={{0,4},{4,0},{1,5},{5,1},{2,6},{6,2},{3,7},{7,3},{8,12},{12,8},{9,1... | collective-permute-start | bytes 6291464 | tf_op jit(solution)/shard_map/ppermute | solution.py:385
  123.1 57.6 %all-to-all-start.1 = ((bf16[16,128,512]{2,1,0:T(8,128)(2,1)}), bf16[16,128,512]{2,1,0:T(8,128)(2,1)}, u32[]{:S(2)}, u32[]{:S(2)}) async-start(bf16[16,128,512]{2,1,0:T(8,128)(2,1)} %bitcast.17), calls=%async_computation.1 | async-start | bytes 4194304 | tf_op jit(solution)/shard_map/all_to_all | solution.py:376
  162.0 4.4 %collective-permute-start.11 = (f32[2048,256]{1,0:T(8,128)}, f32[2048,256]{1,0:T(8,128)S(1)}, u32[]{:S(2)}, u32[]{:S(2)}) collective-permute-start(f32[2048,256]{1,0:T(8,128)} %get-tuple-element.88), channel_id=1, source_target_pairs={{0,4},{4,0},{1,5},{5,1},{2,6},{6,2},{3,7},{7,3},{8,12},{12,8},{9,1... | collective-permute-start | bytes 6291464 | tf_op jit(solution)/shard_map/ppermute | solution.py:385
  162.3 7.2 %collective-permute-start.12 = (f32[2048,256]{1,0:T(8,128)}, f32[2048,256]{1,0:T(8,128)S(1)}, u32[]{:S(2)}, u32[]{:S(2)}) collective-permute-start(f32[2048,256]{1,0:T(8,128)} %get-tuple-element.89), channel_id=1, source_target_pairs={{0,4},{4,0},{1,5},{5,1},{2,6},{6,2},{3,7},{7,3},{8,12},{12,8},{9,1... | collective-permute-start | bytes 6291464 | tf_op jit(solution)/shard_map/ppermute | solution.py:385
  169.5 1.6 copy-start.1
  171.1 1.6 copy-start.2
  172.7 1.2 copy-start.7
  180.7 77.2 %all-to-all-start.2 = ((bf16[16,128,768]{2,1,0:T(8,128)(2,1)}), bf16[16,128,768]{2,1,0:T(8,128)(2,1)}, u32[]{:S(2)}, u32[]{:S(2)}) async-start(bf16[16,128,768]{2,1,0:T(8,128)(2,1)} %bitcast.8), calls=%async_computation.2 | async-start | bytes 6291456 | tf_op jit(solution)/shard_map/all_to_all | solution.py:376
  185.4 29.6 %collective-permute-start.16 = (f32[2048,256]{1,0:T(8,128)}, f32[2048,256]{1,0:T(8,128)S(1)}, u32[]{:S(2)}, u32[]{:S(2)}) collective-permute-start(f32[2048,256]{1,0:T(8,128)} %get-tuple-element.100), channel_id=1, source_target_pairs={{0,4},{4,0},{1,5},{5,1},{2,6},{6,2},{3,7},{7,3},{8,12},{12,8},{9,1... | collective-permute-start | bytes 6291464 | tf_op jit(solution)/shard_map/ppermute | solution.py:385
  185.5 29.6 %collective-permute-start.17 = (f32[2048,256]{1,0:T(8,128)}, f32[2048,256]{1,0:T(8,128)}, u32[]{:S(2)}, u32[]{:S(2)}) collective-permute-start(f32[2048,256]{1,0:T(8,128)} %get-tuple-element.101), channel_id=1, source_target_pairs={{0,4},{4,0},{1,5},{5,1},{2,6},{6,2},{3,7},{7,3},{8,12},{12,8},{9,1... | collective-permute-start | bytes 6291464 | tf_op jit(solution)/shard_map/ppermute | solution.py:385
  187.3 27.8 %copy-start.3 = (f32[2048,256]{1,0:T(8,128)S(1)}, f32[2048,256]{1,0:T(8,128)}, u32[]{:S(2)}) copy-start(f32[2048,256]{1,0:T(8,128)} %get-tuple-element.98.mine_k_ref) | copy-start | bytes 6291460
  187.3 27.8 %copy-start.4 = (f32[2048,256]{1,0:T(8,128)S(1)}, f32[2048,256]{1,0:T(8,128)}, u32[]{:S(2)}) copy-start(f32[2048,256]{1,0:T(8,128)} %get-tuple-element.99.mine_v_ref) | copy-start | bytes 6291460
  187.3 6.8 %collective-permute-start.13 = (bf16[2048,256]{1,0:T(8,128)(2,1)S(1)}, bf16[2048,256]{1,0:T(8,128)(2,1)S(1)}, u32[]{:S(2)}, u32[]{:S(2)}) collective-permute-start(bf16[2048,256]{1,0:T(8,128)(2,1)S(1)} %slice.7), channel_id=1, source_target_pairs={{0,4},{4,0},{1,5},{5,1},{2,6},{6,2},{3,7},{7,3},{8,12},{12,8},{9,1... | collective-permute-start | bytes 3145736 | tf_op jit(solution)/shard_map/ppermute | solution.py:385
  194.1 1.0 copy-start.21
  214.4 6.9 %collective-permute-start.14 = (f32[2048,128]{1,0:T(8,128)}, f32[2048,128]{1,0:T(8,128)S(1)}, u32[]{:S(2)}, u32[]{:S(2)}) collective-permute-start(f32[2048,128]{1,0:T(8,128)} %get-tuple-element.95), channel_id=1, source_target_pairs={{0,4},{4,0},{1,5},{5,1},{2,6},{6,2},{3,7},{7,3},{8,12},{12,8},{9,1... | collective-permute-start | bytes 3145736 | tf_op jit(solution)/shard_map/ppermute | solution.py:385
  214.6 6.7 %collective-permute-start.15 = (f32[2048,128]{1,0:T(8,128)}, f32[2048,128]{1,0:T(8,128)S(1)}, u32[]{:S(2)}, u32[]{:S(2)}) collective-permute-start(f32[2048,128]{1,0:T(8,128)} %get-tuple-element.96), channel_id=1, source_target_pairs={{0,4},{4,0},{1,5},{5,1},{2,6},{6,2},{3,7},{7,3},{8,12},{12,8},{9,1... | collective-permute-start | bytes 3145736 | tf_op jit(solution)/shard_map/ppermute | solution.py:385
  215.0 6.3 %copy-start.10 = (f32[2048,128]{1,0:T(8,128)S(1)}, f32[2048,128]{1,0:T(8,128)}, u32[]{:S(2)}) copy-start(f32[2048,128]{1,0:T(8,128)} %get-tuple-element.93.dk_ref) | copy-start | bytes 3145732
  215.0 6.3 %copy-start.11 = (f32[2048,128]{1,0:T(8,128)S(1)}, f32[2048,128]{1,0:T(8,128)}, u32[]{:S(2)}) copy-start(f32[2048,128]{1,0:T(8,128)} %get-tuple-element.94.dv_ref) | copy-start | bytes 3145732
  215.1 6.3 %copy-start.16 = (bf16[2048,128]{1,0:T(8,128)(2,1)S(1)}, bf16[2048,128]{1,0:T(8,128)(2,1)}, u32[]{:S(2)}) copy-start(bf16[2048,128]{1,0:T(8,128)(2,1)} %get-tuple-element.92.dq_ref) | copy-start | bytes 1572868
  217.7 18.1 %collective-permute-start.18 = (bf16[512,512]{1,0:T(8,128)(2,1)S(1)}, bf16[512,512]{1,0:T(8,128)(2,1)S(1)}, u32[]{:S(2)}, u32[]{:S(2)}) collective-permute-start(bf16[512,512]{1,0:T(8,128)(2,1)S(1)} %get-tuple-element.103), channel_id=1, source_target_pairs={{0,8},{8,0},{16,24},{24,16},{1,9},{9,1},{17,25},{25,17},{2,10},{10... | collective-permute-start | bytes 1572872 | tf_op jit(solution)/shard_map/ppermute | solution.py:388
  219.4 16.5 %collective-permute-start.19 = (bf16[512,512]{1,0:T(8,128)(2,1)S(1)}, bf16[512,512]{1,0:T(8,128)(2,1)S(1)}, u32[]{:S(2)}, u32[]{:S(2)}) collective-permute-start(bf16[512,512]{1,0:T(8,128)(2,1)S(1)} %get-tuple-element.104), channel_id=1, source_target_pairs={{0,16},{8,24},{16,0},{24,8},{1,17},{9,25},{17,1},{25,9},{2,18},{10... | collective-permute-start | bytes 1572872 | tf_op jit(solution)/shard_map/ppermute | solution.py:388
  220.9 26.8 %collective-permute-start.20 = (bf16[512,512]{1,0:T(8,128)(2,1)S(1)}, bf16[512,512]{1,0:T(8,128)(2,1)S(1)}, u32[]{:S(2)}, u32[]{:S(2)}) collective-permute-start(bf16[512,512]{1,0:T(8,128)(2,1)S(1)} %get-tuple-element.105), channel_id=1, source_target_pairs={{0,24},{8,16},{16,8},{24,0},{1,25},{9,17},{17,9},{25,1},{2,26},{10... | collective-permute-start | bytes 1572872 | tf_op jit(solution)/shard_map/ppermute | solution.py:388
  223.7 47.1 %copy-start.8 = (f32[2048,128]{1,0:T(8,128)S(1)}, f32[2048,128]{1,0:T(8,128)}, u32[]{:S(2)}) copy-start(f32[2048,128]{1,0:T(8,128)} %get-tuple-element.115.mine_k_ref) | copy-start | bytes 3145732
  223.7 47.1 %copy-start.9 = (f32[2048,128]{1,0:T(8,128)S(1)}, f32[2048,128]{1,0:T(8,128)}, u32[]{:S(2)}) copy-start(f32[2048,128]{1,0:T(8,128)} %get-tuple-element.116.mine_v_ref) | copy-start | bytes 3145732
  235.9 0.8 copy-start.12
  247.7 0.8 copy-start.14
  257.9 47.0 %all-to-all-start.3 = ((bf16[16,128,384]{2,1,0:T(8,128)(2,1)}), bf16[16,128,384]{2,1,0:T(8,128)(2,1)}, u32[]{:S(2)}, u32[]{:S(2)}) async-start(bf16[16,128,384]{2,1,0:T(8,128)(2,1)} %bitcast.10), calls=%async_computation.3 | async-start | bytes 3145728 | tf_op jit(solution)/shard_map/all_to_all | solution.py:376
  266.4 2.9 collective-permute-start.21
  266.5 4.4 %collective-permute-start.22 = (f32[2048,128]{1,0:T(8,128)}, f32[2048,128]{1,0:T(8,128)S(1)}, u32[]{:S(2)}, u32[]{:S(2)}) collective-permute-start(f32[2048,128]{1,0:T(8,128)} %get-tuple-element.118), channel_id=1, source_target_pairs={{0,4},{4,0},{1,5},{5,1},{2,6},{6,2},{3,7},{7,3},{8,12},{12,8},{9,1... | collective-permute-start | bytes 3145736 | tf_op jit(solution)/shard_map/ppermute | solution.py:385
  270.8 25.6 %copy-start.13 = (bf16[512,512]{1,0:T(8,128)(2,1)S(1)}, bf16[512,512]{1,0:T(8,128)(2,1)}, u32[]{:S(2)}) copy-start(bf16[512,512]{1,0:T(8,128)(2,1)} %copy-done.12) | copy-start | bytes 1572868
  270.8 25.6 %copy-start.15 = (bf16[512,512]{1,0:T(8,128)(2,1)S(1)}, bf16[512,512]{1,0:T(8,128)(2,1)}, u32[]{:S(2)}) copy-start(bf16[512,512]{1,0:T(8,128)(2,1)} %copy-done.14) | copy-start | bytes 1572868
  270.8 25.6 %copy-start.18 = (s32[4]{0:T(128)S(1)}, s32[4]{0:T(128)}, u32[]{:S(2)}) copy-start(s32[4]{0:T(128)} %copy-done.17) | copy-start | bytes 52
  271.2 19.8 %collective-permute-start.23 = (bf16[512,256]{1,0:T(8,128)(2,1)S(1)}, bf16[512,256]{1,0:T(8,128)(2,1)S(1)}, u32[]{:S(2)}, u32[]{:S(2)}) collective-permute-start(bf16[512,256]{1,0:T(8,128)(2,1)S(1)} %get-tuple-element.120), channel_id=1, source_target_pairs={{0,8},{8,0},{16,24},{24,16},{1,9},{9,1},{17,25},{25,17},{2,10},{10... | collective-permute-start | bytes 786440 | tf_op jit(solution)/shard_map/ppermute | solution.py:388
  273.1 17.9 %collective-permute-start.24 = (bf16[512,256]{1,0:T(8,128)(2,1)S(1)}, bf16[512,256]{1,0:T(8,128)(2,1)S(1)}, u32[]{:S(2)}, u32[]{:S(2)}) collective-permute-start(bf16[512,256]{1,0:T(8,128)(2,1)S(1)} %get-tuple-element.121), channel_id=1, source_target_pairs={{0,16},{8,24},{16,0},{24,8},{1,17},{9,25},{17,1},{25,9},{2,18},{10... | collective-permute-start | bytes 786440 | tf_op jit(solution)/shard_map/ppermute | solution.py:388
  274.5 21.9 %collective-permute-start.25 = (bf16[512,256]{1,0:T(8,128)(2,1)S(1)}, bf16[512,256]{1,0:T(8,128)(2,1)S(1)}, u32[]{:S(2)}, u32[]{:S(2)}) collective-permute-start(bf16[512,256]{1,0:T(8,128)(2,1)S(1)} %get-tuple-element.122), channel_id=1, source_target_pairs={{0,24},{8,16},{16,8},{24,0},{1,25},{9,17},{17,9},{25,1},{2,26},{10... | collective-permute-start | bytes 786440 | tf_op jit(solution)/shard_map/ppermute | solution.py:388

commit v4 on v3

--- a/solution.py
+++ b/solution.py
@@ -32,51 +32,76 @@
     return pl.CostEstimate(flops=0, bytes_accessed=count, transcendentals=0)
 
 
-def pack_tokens(arrays, split, zs, cuts):
+def pack_tokens(arrays, zs, plan):
     rows, features = arrays[0].shape
-    group = features // (split * zs)
     count = len(arrays)
 
     def body(*refs):
-        for out, (low, high) in zip(refs[count:], cuts):
-            for c in range(split):
+        for out, (places, width) in zip(refs[count:], plan):
+            for p, low in enumerate(places):
                 for n in range(count):
-                    out[c, 0, :, n * (high - low) : (n + 1) * (high - low)] = refs[n][:, c * group + low : c * group + high]
-
-    widths = [count * (high - low) for low, high in cuts]
+                    out[p, 0, :, n * width : (n + 1) * width] = refs[n][:, low : low + width]
+
     return pl.pallas_call(
         body,
         grid=(zs,),
         in_specs=[pl.BlockSpec((rows, features // zs), lambda z: (0, z))] * count,
-        out_specs=[pl.BlockSpec((split, 1, rows, w), lambda z: (0, z, 0, 0)) for w in widths],
-        out_shape=[jax.ShapeDtypeStruct((split, zs, rows, w), arrays[0].dtype) for w in widths],
+        out_specs=[pl.BlockSpec((len(p), 1, rows, count * w), lambda z: (0, z, 0, 0)) for p, w in plan],
+        out_shape=[jax.ShapeDtypeStruct((len(p), zs, rows, count * w), arrays[0].dtype) for p, w in plan],
         cost_estimate=moved_bytes(4 * count * rows * features),
         name="pack_tokens",
     )(*arrays)
 
 
-def unpack_tokens(moved, cuts, count):
-    split, zs, rows, _ = moved[0].shape
-    group = cuts[-1][1]
-
-    def body(*refs):
-        for ref, (low, high) in zip(refs, cuts):
-            for c in range(split):
-                for n in range(count):
-                    refs[len(cuts) + n][:, c * group + low : c * group + high] = ref[
-                        c, 0, :, n * (high - low) : (n + 1) * (high - low)
-                    ]
-
-    features = zs * split * group
+def unpack_tokens(moved, places, width, features, count):
+    _, zs, rows, _ = moved.shape
+    group = features // zs
+
+    def body(moved_ref, *outs):
+        for p, low in enumerate(places):
+            for n in range(count):
+                outs[n][:, low : low + width] = moved_ref[p, 0, :, n * width : (n + 1) * width]
+
     return pl.pallas_call(
         body,
         grid=(zs,),
-        in_specs=[pl.BlockSpec((split, 1, rows, m.shape[3]), lambda z: (0, z, 0, 0)) for m in moved],
-        out_specs=[pl.BlockSpec((rows, split * group), lambda z: (0, z))] * count,
-        out_shape=[jax.ShapeDtypeStruct((rows, features), moved[0].dtype)] * count,
+        in_specs=[pl.BlockSpec((moved.shape[0], 1, rows, moved.shape[3]), lambda z: (0, z, 0, 0))],
+        out_specs=[pl.BlockSpec((rows, group), lambda z: (0, z))] * count,
+        out_shape=[jax.ShapeDtypeStruct((rows, features), moved.dtype)] * count,
         cost_estimate=moved_bytes(4 * count * rows * features),
         name="unpack_tokens",
-    )(*moved)
+    )(moved)
+
+
+def add_tokens(moved, places, width, into):
+    _, zs, rows, _ = moved.shape
+    count = len(into)
+    group = into[0].shape[1] // zs
+
+    def body(moved_ref, *refs):
+        outs, sem = refs[count : 2 * count], refs[-1]
+        copies = []
+        for z in range(zs):
+            for p, low in enumerate(places):
+                for n in range(count):
+                    source = moved_ref.at[p, z, :, pl.ds(n * width, width)]
+                    target = outs[n].at[:, pl.ds(z * group + low, width)]
+                    copies.append(pltpu.make_async_copy(source, target, sem.at[len(copies)]))
+                    copies[-1].start()
+        for copy in copies:
+            copy.wait()
+
+    anywhere = pl.BlockSpec(memory_space=pl.ANY)
+    return pl.pallas_call(
+        body,
+        in_specs=[pl.BlockSpec(memory_space=pltpu.VMEM)] + [anywhere] * count,
+        out_specs=[anywhere] * count,
+        out_shape=[jax.ShapeDtypeStruct(a.shape, a.dtype) for a in into],
+        scratch_shapes=[pltpu.SemaphoreType.DMA((zs * len(places) * count,))],
+        input_output_aliases={n + 1: n for n in range(count)},
+        cost_estimate=moved_bytes(4 * count * rows * zs * len(places) * width),
+        name="add_tokens",
+    )(moved, *into)
 
 
 def pack_cache(cache_k, cache_v, order):
@@ -130,6 +155,36 @@
     )(mine_k, mine_v, recv_k, recv_v)
 
 
+def merge_cores(first, mine_k, mine_v, recv_k, recv_v, parts):
+    rows, width = mine_k.shape[0] // parts, mine_k.shape[1]
+
+    def body(first_ref, mine_k_ref, mine_v_ref, recv_k_ref, recv_v_ref, *outs):
+        mine = pl.multiple_of(first_ref[0] * width, width)
+        recv = pl.multiple_of((1 - first_ref[0]) * width, width)
+        for p in range(parts):
+
+            @pl.when(pl.program_id(0) == p)
+            def _(p=p):
+                outs[p][:, pl.ds(mine, width)] = mine_k_ref[...]
+                outs[p][:, pl.ds(recv, width)] = recv_k_ref[...]
+                outs[p][:, pl.ds(mine + 2 * width, width)] = mine_v_ref[...]
+                outs[p][:, pl.ds(recv + 2 * width, width)] = recv_v_ref[...]
+
+    return pl.pallas_call(
+        body,
+        grid_spec=pltpu.PrefetchScalarGridSpec(
+            num_scalar_prefetch=1,
+            grid=(parts,),
+            in_specs=[pl.BlockSpec((rows, width), lambda p, first: (p, 0))] * 4,
+            out_specs=[pl.BlockSpec((rows, 4 * width), lambda p, first: (0, 0))] * parts,
+        ),
+        out_shape=[jax.ShapeDtypeStruct((rows, 4 * width), jnp.bfloat16)] * parts,
+        compiler_params=pltpu.CompilerParams(vmem_limit_bytes=32 * 2**20),
+        cost_estimate=moved_bytes(16 * parts * rows * width),
+        name="merge_cores",
+    )(first, mine_k, mine_v, recv_k, recv_v)
+
+
 def place_cache(stages, order, cuts):
     parts = order.shape[0]
     rows, group = stages[0][0].shape[0], cuts[-1][1]
@@ -166,8 +221,8 @@
     def body(back_at_ref, back_on_ref, dq_ref, dk_ref, dv_ref, back_k_ref, back_v_ref, out_ref):
         on = back_on_ref[pl.program_id(0)] > 0
         out_ref[:, :width] = dq_ref[...]
-        out_ref[:, width : 2 * width] = (dk_ref[...] + jnp.where(on, back_k_ref[...], 0.0)).astype(out_ref.dtype)
-        out_ref[:, 2 * width :] = (dv_ref[...] + jnp.where(on, back_v_ref[...], 0.0)).astype(out_ref.dtype)
+        out_ref[:, width : 2 * width] = (dk_ref[...] + jnp.where(on, back_k_ref[...].astype(jnp.float32), 0.0)).astype(out_ref.dtype)
+        out_ref[:, 2 * width :] = (dv_ref[...] + jnp.where(on, back_v_ref[...].astype(jnp.float32), 0.0)).astype(out_ref.dtype)
 
     own = pl.BlockSpec((WINDOW, width), lambda j, at, on: (j, 0))
     back = pl.BlockSpec((WINDOW, width), lambda j, at, on: (at[j], 0))
@@ -186,12 +241,19 @@
     )(back_at, back_on, dq, dk, dv, back_k, back_v)
 
 
-def attention_kernel(parts, outs, first_head, slots_ref, reads_ref, before_ref, start_ref, order_ref, *refs):
-    q_ref, do_ref, k_ref, v_ref, kt_ref, vt_ref = refs[:6]
-    refs = refs[6:]
+def attention_kernel(parts, outs, linked, slots_ref, reads_ref, before_ref, start_ref, order_ref, first_ref, *refs):
+    q_ref, do_ref, k_ref, v_ref = refs[:4]
+    refs = refs[4:]
+    if not linked:
+        kt_ref, vt_ref = refs[:2]
+        refs = refs[2:]
     ck_refs, cv_refs, refs = refs[:parts], refs[parts : 2 * parts], refs[2 * parts :]
-    dq_ref, dk_ref, dv_ref, dkt_ref, dvt_ref = refs[:5]
-    refs = refs[5:]
+    if linked:
+        grads_ref = refs[0]
+        refs = refs[1:]
+    else:
+        dq_ref, dk_ref, dv_ref, dkt_ref, dvt_ref = refs[:5]
+        refs = refs[5:]
     gk_refs, gv_refs, refs = refs[:outs], refs[outs : 2 * outs], refs[2 * outs :]
     kx, vx, dkx, dvx = refs[:4]
     if parts > 1:
@@ -201,15 +263,27 @@
     rows = q_ref.shape[0]
     span = WINDOW + TILE
     chunk, chunks = pl.program_id(1), pl.num_programs(1)
-    group = (first_head + pl.program_id(0)) // GROUP_HEADS
+    group = (first_ref[0] + pl.program_id(0)) // GROUP_HEADS
     table = (group * chunks + order_ref[chunk]) * (rows // BLOCK)
 
-    kx[:WINDOW] = kt_ref[...]
+    if linked:
+        for ref in (kx, vx, dkx, dvx):
+            ref[:WINDOW] = ref[WINDOW:]
+
+        @pl.when(chunk == 0)
+        def _():
+            for ref in (kx, vx, dkx, dvx):
+                ref[:WINDOW] = jnp.zeros((WINDOW, HEAD_DIM), ref.dtype)
+
+        dkx[WINDOW:] = jnp.zeros((WINDOW, HEAD_DIM), jnp.float32)
+        dvx[WINDOW:] = jnp.zeros((WINDOW, HEAD_DIM), jnp.float32)
+    else:
+        kx[:WINDOW] = kt_ref[...]
+        vx[:WINDOW] = vt_ref[...]
+        dkx[...] = jnp.zeros_like(dkx)
+        dvx[...] = jnp.zeros_like(dvx)
     kx[WINDOW:] = k_ref[...]
-    vx[:WINDOW] = vt_ref[...]
     vx[WINDOW:] = v_ref[...]
-    dkx[...] = jnp.zeros_like(dkx)
-    dvx[...] = jnp.zeros_like(dvx)
 
     @pl.when(chunk == 0)
     def _():
@@ -275,7 +349,11 @@
         ds_mem = (p_mem * (dp_mem - delta)).astype(jnp.bfloat16)
 
         dq_mem = jnp.where(first_rows, dot(ds_mem, k_mem[0], (0, 0)), dot(ds_mem, k_mem[1], (0, 0)))
-        dq_ref[pl.ds(at, TILE)] = ((dot(ds_loc, k_loc, (0, 0)) + dq_mem) * SCALE).astype(dq_ref.dtype)
+        dq = ((dot(ds_loc, k_loc, (0, 0)) + dq_mem) * SCALE).astype(jnp.bfloat16)
+        if linked:
+            grads_ref[pl.ds(pl.multiple_of(chunk * rows + at, TILE), TILE), :HEAD_DIM] = dq
+        else:
+            dq_ref[pl.ds(at, TILE)] = dq
         dkx[pl.ds(at, span)] += dot(ds_loc, q, (1, 0))
         dvx[pl.ds(at, span)] += dot(w_loc, do, (1, 0))
         zero = jnp.zeros_like(q)
@@ -291,27 +369,45 @@
         return carry
 
     lax.fori_loop(0, rows // TILE, tile, 0, unroll=UNROLL)
-    dkt_ref[...] = dkx[:WINDOW] * SCALE
-    dvt_ref[...] = dvx[:WINDOW]
-    dk_ref[...] = dkx[WINDOW:] * SCALE
-    dv_ref[...] = dvx[WINDOW:]
+    if linked:
+
+        def put(first, low):
+            there = pl.ds(pl.multiple_of(first, WINDOW), WINDOW)
+            here = slice(low, low + WINDOW)
+            grads_ref[there, HEAD_DIM : 2 * HEAD_DIM] = (dkx[here] * SCALE).astype(grads_ref.dtype)
+            grads_ref[there, 2 * HEAD_DIM :] = dvx[here].astype(grads_ref.dtype)
+
+        @pl.when(chunk > 0)
+        def _():
+            put((chunk - 1) * WINDOW, 0)
+
+        @pl.when(chunk == chunks - 1)
+        def _():
+            put(chunk * WINDOW, WINDOW)
+
+    else:
+        dkt_ref[...] = (dkx[:WINDOW] * SCALE).astype(dkt_ref.dtype)
+        dvt_ref[...] = dvx[:WINDOW].astype(dvt_ref.dtype)
+        dk_ref[...] = dkx[WINDOW:] * SCALE
+        dv_ref[...] = dvx[WINDOW:]
     if parts > 1:
 
         @pl.when(chunk == chunks - 1)
         def _():
             out_rows = gk_refs[0].shape[0]
             for p in range(outs):
-                gk_refs[p][...] = gkx[p * out_rows : (p + 1) * out_rows]
-                gv_refs[p][...] = gvx[p * out_rows : (p + 1) * out_rows]
-
-
-def attention(tables, tokens_in, prev, cache, cut, group_width):
+                gk_refs[p][...] = gkx[p * out_rows : (p + 1) * out_rows].astype(gk_refs[p].dtype)
+                gv_refs[p][...] = gvx[p * out_rows : (p + 1) * out_rows].astype(gv_refs[p].dtype)
+
+
+def attention(tables, tokens_in, prev, cache, group_width):
     rows, width = tokens_in.shape[0], tokens_in.shape[1] // 4
-    heads, first_head = width // HEAD_DIM, cut[0] // HEAD_DIM
+    heads = width // HEAD_DIM
     group_heads = group_width // HEAD_DIM
     parts, part_rows = len(cache), cache[0].shape[0]
     outs = min(2, parts)
     out_rows = parts * part_rows // outs
+    linked = prev is None
 
     def chunk_of(offset):
         return pl.BlockSpec((WINDOW, HEAD_DIM), lambda h, j, *_: (j, h + offset))
@@ -319,37 +415,45 @@
     def before(offset):
         return pl.BlockSpec((WINDOW, HEAD_DIM), lambda h, j, slots, reads, at, *_: (at[j], h + offset))
 
-    def column(height, offset):
-        return pl.BlockSpec((height, HEAD_DIM), lambda h, j, *_: (0, h + offset))
+    def column(height):
+        return pl.BlockSpec((height, HEAD_DIM), lambda h, j, *_: (0, h))
+
+    def cached(offset):
+        return pl.BlockSpec((part_rows, HEAD_DIM), lambda h, j, *tables: (0, h + tables[-1][0] + offset))
 
     bf16, f32 = jnp.bfloat16, jnp.float32
     shape = jax.ShapeDtypeStruct
     scratch = [pltpu.VMEM((2 * WINDOW, HEAD_DIM), kind) for kind in (bf16, bf16, f32, f32)]
     if parts > 1:
         scratch += [pltpu.VMEM((parts * part_rows, HEAD_DIM), kind) for kind in (bf16, bf16, f32, f32)]
+    if linked:
+        token_specs = [pl.BlockSpec((rows, 3 * HEAD_DIM), lambda h, j, *_: (0, h))]
+        token_shapes = [shape((rows, 3 * width), bf16)]
+    else:
+        token_specs = [chunk_of(0)] * 5
+        token_shapes = [shape((rows, width), kind) for kind in (bf16, f32, f32, bf16, bf16)]
     pairs = heads * rows * (WINDOW + TILE + 2 * READS * BLOCK)
     results = pl.pallas_call(
-        functools.partial(attention_kernel, parts, outs, first_head),
+        functools.partial(attention_kernel, parts, outs, linked),
         grid_spec=pltpu.PrefetchScalarGridSpec(
-            num_scalar_prefetch=5,
+            num_scalar_prefetch=6,
             grid=(heads, rows // WINDOW),
             in_specs=[chunk_of(n * heads) for n in range(4)]
-            + [before(0), before(heads)]
-            + [column(part_rows, first_head)] * parts
-            + [column(part_rows, first_head + group_heads)] * parts,
-            out_specs=[chunk_of(0)] * 5 + [column(out_rows, 0)] * (2 * outs),
+            + ([] if linked else [before(0), before(heads)])
+            + [cached(0)] * parts
+            + [cached(group_heads)] * parts,
+            out_specs=token_specs + [column(out_rows)] * (2 * outs),
             scratch_shapes=scratch,
         ),
-        out_shape=[shape((rows, width), bf16)]
-        + [shape((rows, width), f32)] * 4
-        + [shape((out_rows, width), f32)] * (2 * outs),
+        out_shape=token_shapes + [shape((out_rows, width), bf16 if linked else f32)] * (2 * outs),
         compiler_params=pltpu.CompilerParams(vmem_limit_bytes=56 * 2**20),
         cost_estimate=pl.CostEstimate(
             flops=10 * pairs * HEAD_DIM, bytes_accessed=heads * part_rows * parts * 3000, transcendentals=pairs
         ),
         name="attention",
-    )(*tables, *[tokens_in] * 4, prev, prev, *cache, *cache)
-    return results[:5], results[5 : 5 + outs], results[5 + outs :]
+    )(*tables, *[tokens_in] * 4, *([] if linked else [prev, prev]), *cache, *cache)
+    count = len(token_specs)
+    return results[:count], results[count : count + outs], results[count + outs :]
 
 
 def per_device(queries, keys_local, values_local, cache_keys, cache_values, block_map, retrieved, out_grad):
@@ -361,25 +465,29 @@
     groups = retrieved.shape[1]
     shared = groups == chips and chips in (2, 4)
     split = chips if shared else 1
-    head_axes = ("chip", "head") if shared else ("head",)
-    peers = split * zs
-    group_width = features // peers
-    low = group_width - group_width // GROUP_HEADS
+    group_width = features // (split * zs)
+    low = 2 * HEAD_DIM
     cuts = ((0, low), (low, group_width))
-    tokens = rows * peers
-    chunks = tokens // WINDOW
+    firsts = [g * group_width for g in range(split)]
+    if shared:
+        axes = (("chip", "core", "head"), ("chip", "head"))
+        plan = (([g + c * HEAD_DIM for g in firsts for c in range(2)], HEAD_DIM), ([g + low for g in firsts], HEAD_DIM))
+    else:
+        axes = (("head",), ("head",))
+        plan = tuple(([g + a for g in firsts], b - a) for a, b in cuts)
     seq_parts = min(8, 2 * chips)
-    numbers = jnp.arange(chunks, dtype=jnp.int32)
-    bf16, f32 = jnp.bfloat16, jnp.float32
-
-    def exchange(array):
-        return lax.all_to_all(array, head_axes, split_axis=0, concat_axis=0, tiled=True)
-
-    def to_heads(packed):
-        return exchange(packed.reshape(peers, rows, packed.shape[3])).reshape(tokens, packed.shape[3])
-
-    def to_tokens(array):
-        return exchange(array.reshape(peers, rows, array.shape[1])).reshape(split, zs, rows, array.shape[1])
+    bf16 = jnp.bfloat16
+
+    def exchange(array, stage):
+        return lax.all_to_all(array, axes[stage], split_axis=0, concat_axis=0, tiled=True)
+
+    def to_heads(packed, stage):
+        places, _, _, width = packed.shape
+        return exchange(packed.reshape(places * zs, rows, width), stage).reshape(places * zs * rows, width)
+
+    def to_tokens(array, stage):
+        places, width = len(plan[stage][0]), array.shape[1]
+        return exchange(array.reshape(places * zs, rows, width), stage).reshape(places, zs, rows, width)
 
     def other_core(array):
         return lax.ppermute(array, "core", [(0, 1), (1, 0)])
@@ -387,36 +495,47 @@
     def other_chip(array, by):
         return lax.ppermute(array, "chip", [(i, i ^ by) for i in range(chips)]) if by else array
 
+    def ints(*arrays):
+        return tuple(a.astype(jnp.int32) for a in arrays)
+
     everyone = ("chip", "core")
     parts = 2 * chips
-    if shared:
-        before, back_at = jnp.maximum(numbers - 1 + core, 0), jnp.minimum(numbers + core, chunks - 1)
-        back_on = (numbers + core < chunks).astype(jnp.int32)
-        start = ((2 * numbers + core) % seq_parts == 0).astype(jnp.int32)
-        order = jnp.arange(chips, dtype=jnp.int32) ^ chip
-        ids = jnp.stack([other_chip(retrieved, k) for k in range(chips)])
-        reads = lax.dynamic_slice_in_dim(ids, chip, 1, 2)
-        reads = reads.reshape(-1)
-    else:
-        before, back_at, back_on = numbers, numbers, numbers + 1
-        start = (lax.axis_index(everyone) % seq_parts == 0).astype(jnp.int32) + numbers
-        order = numbers
-        reads = jnp.transpose(retrieved, (1, 0, 2)).reshape(-1)
     owner, local = block_map // blk_dev, block_map % blk_dev
     if shared:
+        chip_order = jnp.arange(chips, dtype=jnp.int32) ^ chip
+        arrived = [other_chip(retrieved, k) for k in range(chips)]
+        ids = lax.dynamic_slice_in_dim(jnp.stack(arrived), chip, 1, 2)
+        reads = jnp.concatenate([ids.reshape(-1), other_core(ids).reshape(-1)])
         slots = (((owner % 2) ^ core) * chips + ((owner // 2) ^ chip)) * blk_dev + local
-    else:
-        slots = block_map
-    before, back_at, start = (a.astype(jnp.int32) for a in (before, back_at, start))
-    tables = (slots.astype(jnp.int32), reads, before, start, order.astype(jnp.int32))
-
-    packed = pack_tokens([queries, out_grad, keys_local, values_local], split, zs, cuts)
+        mem = jnp.arange(parts, dtype=jnp.int32)
+        start_a = (mem % seq_parts == 0) + 0 * mem
+        order_a = ((mem % 2) ^ core) * chips + ((mem // 2) ^ chip)
+        tables_a = ints(slots, reads, mem, start_a, order_a, core.reshape(1))
+        numbers = jnp.arange(chips, dtype=jnp.int32)
+        before, back_at = jnp.maximum(numbers - 1 + core, 0), jnp.minimum(numbers + core, chips - 1)
+        back_on = numbers + core < chips
+        start_b = (2 * numbers + core) % seq_parts == 0
+        tables_b = ints(slots, reads, before, start_b, chip_order, jnp.full((1,), low // HEAD_DIM))
+        backs = ints(back_at, back_on)
+    else:
+        arrived = []
+        zero = jnp.zeros((1,), jnp.int32)
+        reads = jnp.transpose(retrieved, (1, 0, 2)).reshape(-1)
+        start = (lax.axis_index(everyone) % seq_parts == 0).reshape(1)
+        tables_a = ints(block_map, reads, zero, start, zero, zero)
+        tables_b = ints(block_map, reads, zero, start, zero, zero + low // HEAD_DIM)
+        backs = (zero, zero + 1)
+    tables = (tables_a, tables_b)
+
+    packed = pack_tokens([queries, out_grad, keys_local, values_local], zs, plan)
+    late = []
     if shared:
-        pieces = pack_cache(cache_keys, cache_values, order)
+        pieces = pack_cache(cache_keys, cache_values, chip_order)
         mine = [other_chip(piece, k) for k, piece in enumerate(pieces)]
-        cache = mine + [other_core(piece) for piece in mine]
-    else:
-        cache = [lax.all_gather(jnp.concatenate([cache_keys, cache_values], 1), everyone, tiled=True)]
+        theirs = [other_core(piece) for piece in mine]
+        early, late = mine + theirs[:-1], theirs[-1:]
+    else:
+        early = [lax.all_gather(jnp.concatenate([cache_keys, cache_values], 1), everyone, tiled=True)]
 
     def chunks_before(keys_values):
         if shared:
@@ -428,34 +547,40 @@
             return other_core(grads)
         return lax.ppermute(grads, everyone, [(i + 1, i) for i in range(parts - 1)])
 
-    def run(stage, moved):
-        (low, high), width = cuts[stage], cuts[stage][1] - cuts[stage][0]
+    def by_tokens(stage, moved):
+        width = moved.shape[1] // 4
         prev = chunks_before(moved[:, 2 * width :])
-        (dq, dk, dv, dkt, dvt), gk, gv = attention(tables, moved, prev, cache, cuts[stage], group_width)
-        back_k, back_v = send_back(dkt), send_back(dvt)
-        out = finish_tokens(back_at, back_on, dq, dk, dv, back_k, back_v)
+        (dq, dk, dv, dkt, dvt), gk, gv = attention(tables[stage], moved, prev, cache, group_width)
+        out = finish_tokens(*backs, dq, dk, dv, send_back(dkt), send_back(dvt))
         if not shared:
-            sums = [lax.psum_scatter(g[0], everyone, scatter_dimension=0, tiled=True).astype(bf16) for g in (gk, gv)]
-            return out, sums
+            return out, [lax.psum_scatter(g[0], everyone, scatter_dimension=0, tiled=True).astype(bf16) for g in (gk, gv)]
         return out, sum_cores(gk[0], gv[0], other_core(gk[1]), other_core(gv[1]), chips)
 
-    moved_a = to_heads(packed[0])
-    moved_a, second, cache, tables = after((moved_a, packed[1], cache, tables), ())
-    moved_b = to_heads(second)
-    out_a, sums_a = run(0, moved_a)
+    def by_heads(stage, moved):
+        (out,), gk, gv = attention(tables[stage], moved, None, cache, group_width)
+        return out, (gk, gv)
+
+    moved_a = to_heads(after(packed[0], arrived), 0)
+    moved_a, second, early, tables = after((moved_a, packed[1], early, tables), ())
+    cache = early + late
+    moved_b = to_heads(second, 1)
+    out_a, sums_a = (by_heads if shared else by_tokens)(0, moved_a)
     out_a, moved_b = after((out_a, moved_b), ())
-    out_a = to_tokens(out_a)
-    out_b, sums_b = run(1, moved_b)
+    out_a = to_tokens(out_a, 0)
+    out_b, sums_b = by_tokens(1, moved_b)
     if shared:
+        gk, gv = sums_a
+        sums_a = merge_cores(tables_a[5], gk[0], gv[0], other_core(gk[1]), other_core(gv[1]), chips)
         sums_a = [other_chip(s, k) for k, s in enumerate(sums_a)]
-    out_b, out_a, sums_a = after((out_b, out_a, sums_a), ())
+    out_b, out_a, sums_a, sums_b = after((out_b, out_a, sums_a, sums_b), ())
     if shared:
         sums_b = [other_chip(s, k) for k, s in enumerate(sums_b)]
-        grad_cache = place_cache([sums_a, sums_b], order.astype(jnp.int32), cuts)
+        grad_cache = place_cache([sums_a, sums_b], chip_order, cuts)
     else:
         grad_cache = [jnp.concatenate([a, b], 1) for a, b in zip(sums_a, sums_b)]
-    out_b = to_tokens(out_b)
-    return (*unpack_tokens([out_a, out_b], cuts, 3), *grad_cache)
+    grads = unpack_tokens(out_a, *plan[0], features, 3)
+    out_b = to_tokens(out_b, 1)
+    return (*add_tokens(out_b, *plan[1], grads), *grad_cache)
 
 
 def solution(mesh):

time: 311 us -> 291 us (0.936)
  waiting for transfers between devices: 175 us -> 162 us
  local copies, waits for them, and re-layouts: 13.6 us -> 6.38 us
    ppermute x14 -> x12, waiting for transfers between devices: 17.4 us -> 6.16 us  [other_core(): return lax.ppermute(array, 'core', [(0, 1), (1, 0)])]
    slice x2 -> x1, local copies, waits for them, and re-layouts: 4.43 us -> 0.07 us  [by_tokens(): prev = chunks_before(moved[:, 2 * width:])]
    ppermute x12, waiting for transfers between devices: 129 us -> 125 us  [other_chip(): lax.ppermute(array, 'chip', [(i, i ^ by) for i in range(chips)])]
    all_to_all x4, starting transfers between devices: 26.4 us -> 22.7 us  [exchange(): lax.all_to_all(array, axes[stage], split_axis=0, concat_axis=0, tiled=True)]
    ppermute x12, starting transfers between devices: 12.5 us -> 16.1 us  [other_chip(): lax.ppermute(array, 'chip', [(i, i ^ by) for i in range(chips)])]
    unnamed x48 -> x42, local copies, waits for them, and re-layouts: 8.44 us -> 5.4 us
    pallas_call x3 -> x5, Pallas kernels: 58.5 us -> 61.2 us  [the longest x2 53.1 us: attention(): pl.pallas_call(functools.partial(attention_kernel, parts, outs, linked),...]
  transfers between devices with their start and end apart: 30 -> 28, of which waited for: 18 -> 15; matrix products, arithmetic and copies ran while one was open for 1% -> 1% of each run, Pallas kernels for 21% -> 25%
where the time goes in v4:
time: 291 us; the launch traced here: 290 us
  waiting for transfers between devices  162 us (56%)
  Pallas kernels  76.2 us (26%)
  starting transfers between devices  41.2 us (14%)
  local copies, waits for them, and re-layouts  6.38 us (2%)
  other arithmetic  3.29 us (1%)
    ppermute x12, waiting for transfers between devices, other_chip(): lax.ppermute(array, 'chip', [(i, i ^ by) for i in range(chips)])  125 us
    pallas_call x2, Pallas kernels, attention(): pl.pallas_call(functools.partial(attention_kernel, parts, outs, linked),...  53.1 us
    all_to_all x4, waiting for transfers between devices, exchange(): lax.all_to_all(array, axes[stage], split_axis=0, concat_axis=0, tiled=True)  31.1 us
    all_to_all x4, starting transfers between devices, exchange(): lax.all_to_all(array, axes[stage], split_axis=0, concat_axis=0, tiled=True)  22.7 us
    ppermute x12, starting transfers between devices, other_chip(): lax.ppermute(array, 'chip', [(i, i ^ by) for i in range(chips)])  16.1 us
    ppermute x12, waiting for transfers between devices, other_core(): return lax.ppermute(array, 'core', [(0, 1), (1, 0)])  6.16 us
    pallas_call x1, Pallas kernels, pack_tokens(): pl.pallas_call(body, grid=(zs,), in_specs=[pl.BlockSpec((rows, features /...  6.15 us
  transfers between devices with their start and end apart: 28, of which 15 were waited for; matrix products, arithmetic and copies ran while one was open for 1% of the time, Pallas kernels for 25%

profile of v4, /device:TPU:0, one launch (start us, length us, event | category | flops | bytes accessed | tf_op | source)
XLA Modules:
  0.0 290.4 jit_solution(16078294657119528351)
XLA Ops:
  0.6 3.0 %collective-permute-start = (s32[8,4,4]{0,2,1:T(4,128)}, s32[8,4,4]{0,2,1:T(4,128)S(1)}, u32[]{:S(2)}, u32[]{:S(2)}) collective-permute-start(s32[8,4,4]{0,2,1:T(4,128)} %param.14), channel_id=1, source_target_pairs={{0,8},{8,0},{16,24},{24,16},{1,9},{9,1},{17,25},{25,17},{2,10},{10... | collective-permute-start | bytes 1544 | tf_op jit(solution)/shard_map/ppermute | solution.py:496
  3.6 1.5 collective-permute-start.1
  5.2 6.1 %pack_tokens.1 = (bf16[8,4,128,512]{3,2,1,0:T(8,128)(2,1)}, bf16[4,4,128,512]{3,2,1,0:T(8,128)(2,1)}) custom-call(bf16[128,6144]{1,0:T(8,128)(2,1)} %refs_0_.1, bf16[128,6144]{1,0:T(8,128)(2,1)} %refs_1_.1, bf16[128,6144]{1,0:T(8,128)(2,1)} %refs_2_.1, bf16[128,6144]{1,0:T(8,128)(2,1)} %refs_3_.1), custom_call_target="tpu_custom_call" | custom-call | bytes 12582912 | tf_op jit(solution)/shard_map/pack_tokens/pallas_call | solution.py:45
  11.4 6.4 %all-to-all-start = ((bf16[32,128,512]{2,1,0:T(8,128)(2,1)}), bf16[32,128,512]{2,1,0:T(8,128)(2,1)}, u32[]{:S(2)}, u32[]{:S(2)}) async-start(bf16[32,128,512]{2,1,0:T(8,128)(2,1)} %bitcast.26), calls=%async_computation | async-start | bytes 8388608 | tf_op jit(solution)/shard_map/all_to_all | solution.py:482
  17.8 1.4 copy-done.2
  19.3 2.5 pack_cache.1
  21.7 1.7 collective-permute-start.3
  23.4 1.5 collective-permute-start.4
  24.9 0.3 collective-permute-start.5
  25.2 52.3 %collective-permute-done.3.refs_5_.refs_13_.refs_7_.refs_15_ = bf16[512,768]{1,0:T(8,128)(2,1)S(1)} collective-permute-done((bf16[512,768]{1,0:T(8,128)(2,1)}, bf16[512,768]{1,0:T(8,128)(2,1)S(1)}, u32[]{:S(2)}, u32[]{:S(2)}) %collective-permute-start.3) | collective-permute-done | bytes 786464 | tf_op jit(solution)/shard_map/ppermute | solution.py:496
  77.5 0.5 collective-permute-start.8
  78.0 0.5 fusion.9.order_ref
  78.5 0.5 add_maximum_fusion.before_ref
  79.0 0.6 compare_convert_fusion.start_ref
  79.6 0.5 fusion.3.slots_ref
  80.2 0.2 collective-permute-start.9
  80.4 0.5 compare_convert_fusion.1.start_ref
  80.9 0.1 copy.18
  81.0 0.1 reshape.45
  81.1 0.3 collective-permute-done.9
  81.4 0.1 copy.19
  81.5 0.1 reshape.46
  81.6 0.6 pad_add_fusion.reads_ref
  82.2 23.4 %collective-permute-done.5.refs_7_.refs_15_.refs_9_.refs_17_ = bf16[512,768]{1,0:T(8,128)(2,1)} collective-permute-done((bf16[512,768]{1,0:T(8,128)(2,1)S(1)}, bf16[512,768]{1,0:T(8,128)(2,1)}, u32[]{:S(2)}, u32[]{:S(2)}) %collective-permute-start.5) | collective-permute-done | bytes 786464 | tf_op jit(solution)/shard_map/ppermute | solution.py:496
  105.6 6.3 %all-to-all-done = bf16[32,128,512]{2,1,0:T(8,128)(2,1)} async-done(((bf16[32,128,512]{2,1,0:T(8,128)(2,1)}), bf16[32,128,512]{2,1,0:T(8,128)(2,1)}, u32[]{:S(2)}, u32[]{:S(2)}) %all-to-all-start) | async-done | bytes 4194336 | tf_op jit(solution)/shard_map/all_to_all | solution.py:482
  111.9 0.5 iota.21.before_ref
  112.5 6.5 %all-to-all-start.1 = ((bf16[16,128,512]{2,1,0:T(8,128)(2,1)}), bf16[16,128,512]{2,1,0:T(8,128)(2,1)S(1)}, u32[]{:S(2)}, u32[]{:S(2)}) async-start(bf16[16,128,512]{2,1,0:T(8,128)(2,1)} %bitcast.28), calls=%async_computation.1 | async-start | bytes 4194304 | tf_op jit(solution)/shard_map/all_to_all | solution.py:482
  119.1 2.5 collective-permute-done.10.refs_11_.refs_19_.refs_13_.refs_21_
  121.6 0.9 copy-done.15
  122.5 33.4 %attention.2 = (bf16[4096,384]{1,0:T(8,128)(2,1)}, bf16[2048,128]{1,0:T(8,128)(2,1)}, bf16[2048,128]{1,0:T(8,128)(2,1)}, bf16[2048,128]{1,0:T(8,128)(2,1)}, bf16[2048,128]{1,0:T(8,128)(2,1)}) custom-call(s32[64]{0:T(128)} %fusion.3.slots_ref, s32[256]{0:T(256)} %pad_add_fusion.reads_ref, s32[8]{0:T(128)} %iota.21.before_ref, ...), custom_call_target="tpu_custom_call" | custom-call | flops 6039797760 | bytes 12288000 | tf_op jit(solution)/shard_map/attention/pallas_call | solution.py:436
  155.9 12.6 %all-to-all-done.1 = bf16[16,128,512]{2,1,0:T(8,128)(2,1)S(1)} async-done(((bf16[16,128,512]{2,1,0:T(8,128)(2,1)}), bf16[16,128,512]{2,1,0:T(8,128)(2,1)S(1)}, u32[]{:S(2)}, u32[]{:S(2)}) %all-to-all-start.1) | async-done | bytes 2097184 | tf_op jit(solution)/shard_map/all_to_all | solution.py:482
  168.5 3.8 %all-to-all-start.2 = ((bf16[32,128,384]{2,1,0:T(8,128)(2,1)}), bf16[32,128,384]{2,1,0:T(8,128)(2,1)}, u32[]{:S(2)}, u32[]{:S(2)}) async-start(bf16[32,128,384]{2,1,0:T(8,128)(2,1)} %bitcast.27), calls=%async_computation.2 | async-start | bytes 6291456 | tf_op jit(solution)/shard_map/all_to_all | solution.py:482
  172.5 0.9 copy-done.20
  173.4 0.2 copy-done.19
  173.6 0.4 collective-permute-start.15
  173.9 1.3 collective-permute-done.11.refs_4_.refs_5_
  175.2 1.0 copy-done.16
  176.1 19.7 %attention.3 = (bf16[2048,128]{1,0:T(8,128)(2,1)}, f32[2048,128]{1,0:T(8,128)}, f32[2048,128]{1,0:T(8,128)}, bf16[2048,128]{1,0:T(8,128)(2,1)}, bf16[2048,128]{1...) custom-call(s32[64]{0:T(128)} %fusion.3.slots_ref, ...), custom_call_target="tpu_custom_call" | custom-call | flops 3019898880 | bytes 12288000 | tf_op jit(solution)/shard_map/attention/pallas_call | solution.py:436
  195.9 0.2 collective-permute-start.19
  196.1 0.4 collective-permute-start.20
  196.4 0.1 collective-permute-start.12
  196.6 0.4 collective-permute-start.13
  197.0 0.5 merge_cores.1
  197.5 1.5 collective-permute-start.16
  198.9 2.1 collective-permute-done.12.back_k_ref
  201.0 1.4 collective-permute-start.17
  202.5 1.7 collective-permute-start.18
  204.2 1.0 copy-done.9
  205.2 2.4 finish_tokens.1
  207.7 1.1 sum_cores.1
  208.8 9.8 %collective-permute-done.16.refs_1_ = bf16[512,512]{1,0:T(8,128)(2,1)S(1)} collective-permute-done((bf16[512,512]{1,0:T(8,128)(2,1)S(1)}, bf16[512,512]{1,0:T(8,128)(2,1)S(1)}, u32[]{:S(2)}, u32[]{:S(2)}) %collective-permute-start.16) | collective-permute-done | bytes 524320 | tf_op jit(solution)/shard_map/ppermute | solution.py:496
  218.6 8.2 %collective-permute-done.17.refs_2_ = bf16[512,512]{1,0:T(8,128)(2,1)S(1)} collective-permute-done((bf16[512,512]{1,0:T(8,128)(2,1)S(1)}, bf16[512,512]{1,0:T(8,128)(2,1)S(1)}, u32[]{:S(2)}, u32[]{:S(2)}) %collective-permute-start.17) | collective-permute-done | bytes 524320 | tf_op jit(solution)/shard_map/ppermute | solution.py:496
  226.8 10.2 %collective-permute-done.18.refs_3_ = bf16[512,512]{1,0:T(8,128)(2,1)S(1)} collective-permute-done((bf16[512,512]{1,0:T(8,128)(2,1)S(1)}, bf16[512,512]{1,0:T(8,128)(2,1)S(1)}, u32[]{:S(2)}, u32[]{:S(2)}) %collective-permute-start.18) | collective-permute-done | bytes 524320 | tf_op jit(solution)/shard_map/ppermute | solution.py:496
  237.0 6.0 %all-to-all-done.2 = bf16[32,128,384]{2,1,0:T(8,128)(2,1)} async-done(((bf16[32,128,384]{2,1,0:T(8,128)(2,1)}), bf16[32,128,384]{2,1,0:T(8,128)(2,1)}, u32[]{:S(2)}, u32[]{:S(2)}) %all-to-all-start.2) | async-done | bytes 3145760 | tf_op jit(solution)/shard_map/all_to_all | solution.py:482
  243.0 5.9 %all-to-all-start.3 = ((bf16[16,128,384]{2,1,0:T(8,128)(2,1)}), bf16[16,128,384]{2,1,0:T(8,128)(2,1)}, u32[]{:S(2)}, u32[]{:S(2)}) async-start(bf16[16,128,384]{2,1,0:T(8,128)(2,1)} %bitcast.11), calls=%async_computation.3 | async-start | bytes 3145728 | tf_op jit(solution)/shard_map/all_to_all | solution.py:482
  248.9 1.9 collective-permute-start.21
  250.9 1.5 collective-permute-start.22
  252.3 0.1 collective-permute-start.23
  252.5 4.7 %unpack_tokens.1 = (bf16[128,6144]{1,0:T(8,128)(2,1)}, bf16[128,6144]{1,0:T(8,128)(2,1)}, bf16[128,6144]{1,0:T(8,128)(2,1)}) custom-call(bf16[8,4,128,384]{3,2,1,0:T(8,128)(2,1)} %bitcast.10.moved_ref), custom_call_target="tpu_custom_call" | custom-call | bytes 9437184 | tf_op jit(solution)/shard_map/unpack_tokens/pallas_call | solution.py:65
  257.2 16.2 %collective-permute-done.21.refs_5_ = bf16[512,256]{1,0:T(8,128)(2,1)S(1)} collective-permute-done((bf16[512,256]{1,0:T(8,128)(2,1)}, bf16[512,256]{1,0:T(8,128)(2,1)S(1)}, u32[]{:S(2)}, u32[]{:S(2)}) %collective-permute-start.21) | collective-permute-done | bytes 262176 | tf_op jit(solution)/shard_map/ppermute | solution.py:496
  273.4 4.9 %collective-permute-done.23.refs_7_ = bf16[512,256]{1,0:T(8,128)(2,1)S(1)} collective-permute-done((bf16[512,256]{1,0:T(8,128)(2,1)S(1)}, bf16[512,256]{1,0:T(8,128)(2,1)S(1)}, u32[]{:S(2)}, u32[]{:S(2)}) %collective-permute-start.23) | collective-permute-done | bytes 262176 | tf_op jit(solution)/shard_map/ppermute | solution.py:496
  278.3 2.8 place_cache.1
  281.0 6.2 %all-to-all-done.3 = bf16[16,128,384]{2,1,0:T(8,128)(2,1)} async-done(((bf16[16,128,384]{2,1,0:T(8,128)(2,1)}), bf16[16,128,384]{2,1,0:T(8,128)(2,1)}, u32[]{:S(2)}, u32[]{:S(2)}) %all-to-all-start.3) | async-done | bytes 1572896 | tf_op jit(solution)/shard_map/all_to_all | solution.py:482
  287.3 2.9 %add_tokens.1 = (bf16[128,6144]{1,0:T(8,128)(2,1)}, bf16[128,6144]{1,0:T(8,128)(2,1)}, bf16[128,6144]{1,0:T(8,128)(2,1)}) custom-call(bf16[4,4,128,384]{3,2,1,0:T(8,128)(2,1)} %bitcast.12.moved_ref, bf16[128,6144]{1,0:T(8,128)(2,1)} %get-tuple-element.129.refs_0_, ...), custom_call_target="tpu_custom_call", output_to_operand_aliasing={{0}: (1, {}), {1}: (2, {}), {2}: (3, {})} | custom-call | bytes 3145728 | tf_op jit(solution)/shard_map/add_tokens/pallas_call | solution.py:95
  (60 shorter events, 0.4 us)
Async XLA Ops:
  0.6 10.7 %collective-permute-start = (s32[8,4,4]{0,2,1:T(4,128)}, s32[8,4,4]{0,2,1:T(4,128)S(1)}, u32[]{:S(2)}, u32[]{:S(2)}) collective-permute-start(s32[8,4,4]{0,2,1:T(4,128)} %param.14), channel_id=1, source_target_pairs={{0,8},{8,0},{16,24},{24,16},{1,9},{9,1},{17,25},{25,17},{2,10},{10... | collective-permute-start | bytes 1544 | tf_op jit(solution)/shard_map/ppermute | solution.py:496
  3.6 7.7 %collective-permute-start.1 = (s32[8,4,4]{0,2,1:T(4,128)}, s32[8,4,4]{0,2,1:T(4,128)S(1)}, u32[]{:S(2)}, u32[]{:S(2)}) collective-permute-start(s32[8,4,4]{0,2,1:T(4,128)} %param.14), channel_id=1, source_target_pairs={{0,16},{8,24},{16,0},{24,8},{1,17},{9,25},{17,1},{25,9},{2,18},{10... | collective-permute-start | bytes 1544 | tf_op jit(solution)/shard_map/ppermute | solution.py:496
  5.2 6.2 %collective-permute-start.2 = (s32[8,4,4]{0,2,1:T(4,128)}, s32[8,4,4]{0,2,1:T(4,128)S(1)}, u32[]{:S(2)}, u32[]{:S(2)}) collective-permute-start(s32[8,4,4]{0,2,1:T(4,128)} %param.14), channel_id=1, source_target_pairs={{0,24},{8,16},{16,8},{24,0},{1,25},{9,17},{17,9},{25,1},{2,26},{10... | collective-permute-start | bytes 1544 | tf_op jit(solution)/shard_map/ppermute | solution.py:496
  11.3 6.5 %copy-start.1 = (bf16[512,1536]{1,0:T(8,128)(2,1)S(1)}, bf16[512,1536]{1,0:T(8,128)(2,1)}, u32[]{:S(2)}) copy-start(bf16[512,1536]{1,0:T(8,128)(2,1)} %k_ref.1) | copy-start | bytes 4718596
  11.4 100.6 %all-to-all-start = ((bf16[32,128,512]{2,1,0:T(8,128)(2,1)}), bf16[32,128,512]{2,1,0:T(8,128)(2,1)}, u32[]{:S(2)}, u32[]{:S(2)}) async-start(bf16[32,128,512]{2,1,0:T(8,128)(2,1)} %bitcast.26), calls=%async_computation | async-start | bytes 8388608 | tf_op jit(solution)/shard_map/all_to_all | solution.py:482
  17.8 1.4 copy-start.2
  19.2 2.5 copy-start.10
  19.2 60.4 %copy-start.18 = (s32[64]{0:T(128)S(1)}, s32[64]{0:T(128)}, u32[]{:S(2)}) copy-start(s32[64]{0:T(128)} %param.13) | copy-start | bytes 772
  19.2 60.9 %copy-start.17 = (s32[8,4,4]{0,2,1:T(4,128)S(1)}, s32[8,4,4]{0,2,1:T(4,128)}, u32[]{:S(2)}) copy-start(s32[8,4,4]{0,2,1:T(4,128)} %param.14) | copy-start | bytes 1540
  21.7 90.7 %copy-start = (bf16[512,768]{1,0:T(8,128)(2,1)}, bf16[512,768]{1,0:T(8,128)(2,1)S(1)}, u32[]{:S(2)}) copy-start(bf16[512,768]{1,0:T(8,128)(2,1)S(1)} %get-tuple-element.95.refs_4_.refs_12_.refs_6_.refs_14_) | copy-start | bytes 2359300
  21.7 55.8 %collective-permute-start.3 = (bf16[512,768]{1,0:T(8,128)(2,1)}, bf16[512,768]{1,0:T(8,128)(2,1)S(1)}, u32[]{:S(2)}, u32[]{:S(2)}) collective-permute-start(bf16[512,768]{1,0:T(8,128)(2,1)} %get-tuple-element.79), channel_id=1, source_target_pairs={{0,8},{8,0},{16,24},{24,16},{1,9},{9,1},{17,25},{25,17},{2,10},{10... | collective-permute-start | bytes 2359304 | tf_op jit(solution)/shard_map/ppermute | solution.py:496
  23.4 54.1 %collective-permute-start.4 = (bf16[512,768]{1,0:T(8,128)(2,1)}, bf16[512,768]{1,0:T(8,128)(2,1)S(1)}, u32[]{:S(2)}, u32[]{:S(2)}) collective-permute-start(bf16[512,768]{1,0:T(8,128)(2,1)} %get-tuple-element.80), channel_id=1, source_target_pairs={{0,16},{8,24},{16,0},{24,8},{1,17},{9,25},{17,1},{25,9},{2,18},{10... | collective-permute-start | bytes 2359304 | tf_op jit(solution)/shard_map/ppermute | solution.py:496
  24.9 80.7 %collective-permute-start.5 = (bf16[512,768]{1,0:T(8,128)(2,1)S(1)}, bf16[512,768]{1,0:T(8,128)(2,1)}, u32[]{:S(2)}, u32[]{:S(2)}) collective-permute-start(bf16[512,768]{1,0:T(8,128)(2,1)S(1)} %get-tuple-element.81), channel_id=1, source_target_pairs={{0,24},{8,16},{16,8},{24,0},{1,25},{9,17},{17,9},{25,1},{2,26},{10... | collective-permute-start | bytes 2359304 | tf_op jit(solution)/shard_map/ppermute | solution.py:496
  25.2 80.4 %collective-permute-start.6 = (bf16[512,768]{1,0:T(8,128)(2,1)S(1)}, bf16[512,768]{1,0:T(8,128)(2,1)}, u32[]{:S(2)}, u32[]{:S(2)}) collective-permute-start(bf16[512,768]{1,0:T(8,128)(2,1)S(1)} %get-tuple-element.95.refs_4_.refs_12_.refs_6_.refs_14_), channel_id=1, source_target_pairs={{0,4},{4,0},{1,5},{5,1},{2,6},{6,2},{3,7},{7,3},{8,12},{12,8},{9,1... | collective-permute-start | bytes 2359304 | tf_op jit(solution)/shard_map/ppermute | solution.py:493
  77.5 35.0 %copy-start.13 = (bf16[512,768]{1,0:T(8,128)(2,1)}, bf16[512,768]{1,0:T(8,128)(2,1)S(1)}, u32[]{:S(2)}) copy-start(bf16[512,768]{1,0:T(8,128)(2,1)S(1)} %collective-permute-done.3.refs_5_.refs_13_.refs_7_.refs_15_) | copy-start | bytes 2359300
  77.5 28.1 %collective-permute-start.7 = (bf16[512,768]{1,0:T(8,128)(2,1)S(1)}, bf16[512,768]{1,0:T(8,128)(2,1)}, u32[]{:S(2)}, u32[]{:S(2)}) collective-permute-start(bf16[512,768]{1,0:T(8,128)(2,1)S(1)} %collective-permute-done.3.refs_5_.refs_13_.refs_7_.refs_15_), channel_id=1, source_target_pairs={{0,4},{4,0},{1,5},{5,1},{2,6},{6,2},{3,7},{7,3},{8,12},{12,8},{9,1... | collective-permute-start | bytes 2359304 | tf_op jit(solution)/shard_map/ppermute | solution.py:493
  77.5 35.0 %copy-start.14 = (bf16[512,768]{1,0:T(8,128)(2,1)}, bf16[512,768]{1,0:T(8,128)(2,1)S(1)}, u32[]{:S(2)}) copy-start(bf16[512,768]{1,0:T(8,128)(2,1)S(1)} %collective-permute-done.4.refs_6_.refs_14_.refs_8_.refs_16_) | copy-start | bytes 2359300
  77.5 28.1 %collective-permute-start.8 = (bf16[512,768]{1,0:T(8,128)(2,1)S(1)}, bf16[512,768]{1,0:T(8,128)(2,1)}, u32[]{:S(2)}, u32[]{:S(2)}) collective-permute-start(bf16[512,768]{1,0:T(8,128)(2,1)S(1)} %collective-permute-done.4.refs_6_.refs_14_.refs_8_.refs_16_), channel_id=1, source_target_pairs={{0,4},{4,0},{1,5},{5,1},{2,6},{6,2},{3,7},{7,3},{8,12},{12,8},{9,1... | collective-permute-start | bytes 2359304 | tf_op jit(solution)/shard_map/ppermute | solution.py:493
  80.2 1.2 collective-permute-start.9
  112.5 56.1 %all-to-all-start.1 = ((bf16[16,128,512]{2,1,0:T(8,128)(2,1)}), bf16[16,128,512]{2,1,0:T(8,128)(2,1)S(1)}, u32[]{:S(2)}, u32[]{:S(2)}) async-start(bf16[16,128,512]{2,1,0:T(8,128)(2,1)} %bitcast.28), calls=%async_computation.1 | async-start | bytes 4194304 | tf_op jit(solution)/shard_map/all_to_all | solution.py:482
  119.0 2.6 collective-permute-start.10
  121.6 0.9 copy-start.15
  168.5 3.8 %copy-start.12 = (bf16[16,128,512]{2,1,0:T(8,128)(2,1)}, bf16[16,128,512]{2,1,0:T(8,128)(2,1)S(1)}, u32[]{:S(2)}) copy-start(bf16[16,128,512]{2,1,0:T(8,128)(2,1)S(1)} %all-to-all-done.1) | copy-start | bytes 6291460
  168.5 74.5 %all-to-all-start.2 = ((bf16[32,128,384]{2,1,0:T(8,128)(2,1)}), bf16[32,128,384]{2,1,0:T(8,128)(2,1)}, u32[]{:S(2)}, u32[]{:S(2)}) async-start(bf16[32,128,384]{2,1,0:T(8,128)(2,1)} %bitcast.27), calls=%async_computation.2 | async-start | bytes 6291456 | tf_op jit(solution)/shard_map/all_to_all | solution.py:482
  172.3 1.0 copy-start.20
  172.4 1.2 copy-start.19
  172.4 2.7 collective-permute-start.11
  173.4 23.2 %collective-permute-start.14 = (bf16[2048,128]{1,0:T(8,128)(2,1)S(1)}, bf16[2048,128]{1,0:T(8,128)(2,1)S(1)}, u32[]{:S(2)}, u32[]{:S(2)}) collective-permute-start(bf16[2048,128]{1,0:T(8,128)(2,1)S(1)} %copy-done.20), channel_id=1, source_target_pairs={{0,4},{4,0},{1,5},{5,1},{2,6},{6,2},{3,7},{7,3},{8,12},{12,8},{9,1... | collective-permute-start | bytes 1572872 | tf_op jit(solution)/shard_map/ppermute | solution.py:493
  173.6 23.4 %copy-start.7 = (bf16[2048,128]{1,0:T(8,128)(2,1)S(1)}, bf16[2048,128]{1,0:T(8,128)(2,1)}, u32[]{:S(2)}) copy-start(bf16[2048,128]{1,0:T(8,128)(2,1)} %get-tuple-element.111.mine_k_ref) | copy-start | bytes 1572868
  173.6 23.4 %copy-start.8 = (bf16[2048,128]{1,0:T(8,128)(2,1)S(1)}, bf16[2048,128]{1,0:T(8,128)(2,1)}, u32[]{:S(2)}) copy-start(bf16[2048,128]{1,0:T(8,128)(2,1)} %get-tuple-element.112.mine_v_ref) | copy-start | bytes 1572868
  173.6 23.4 %collective-permute-start.15 = (bf16[2048,128]{1,0:T(8,128)(2,1)S(1)}, bf16[2048,128]{1,0:T(8,128)(2,1)S(1)}, u32[]{:S(2)}, u32[]{:S(2)}) collective-permute-start(bf16[2048,128]{1,0:T(8,128)(2,1)S(1)} %copy-done.19), channel_id=1, source_target_pairs={{0,4},{4,0},{1,5},{5,1},{2,6},{6,2},{3,7},{7,3},{8,12},{12,8},{9,1... | collective-permute-start | bytes 1572872 | tf_op jit(solution)/shard_map/ppermute | solution.py:493
  175.2 1.0 copy-start.16
  195.8 8.3 %copy-start.5 = (f32[2048,128]{1,0:T(8,128)S(1)}, f32[2048,128]{1,0:T(8,128)}, u32[]{:S(2)}) copy-start(f32[2048,128]{1,0:T(8,128)} %get-tuple-element.106.dk_ref) | copy-start | bytes 3145732
  195.8 8.3 %copy-start.6 = (f32[2048,128]{1,0:T(8,128)S(1)}, f32[2048,128]{1,0:T(8,128)}, u32[]{:S(2)}) copy-start(f32[2048,128]{1,0:T(8,128)} %get-tuple-element.107.dv_ref) | copy-start | bytes 3145732
  195.9 11.8 %collective-permute-start.19 = (f32[2048,128]{1,0:T(8,128)}, f32[2048,128]{1,0:T(8,128)S(1)}, u32[]{:S(2)}, u32[]{:S(2)}) collective-permute-start(f32[2048,128]{1,0:T(8,128)} %get-tuple-element.121), channel_id=1, source_target_pairs={{0,4},{4,0},{1,5},{5,1},{2,6},{6,2},{3,7},{7,3},{8,12},{12,8},{9,1... | collective-permute-start | bytes 3145736 | tf_op jit(solution)/shard_map/ppermute | solution.py:493
  196.1 11.6 %collective-permute-start.20 = (f32[2048,128]{1,0:T(8,128)}, f32[2048,128]{1,0:T(8,128)S(1)}, u32[]{:S(2)}, u32[]{:S(2)}) collective-permute-start(f32[2048,128]{1,0:T(8,128)} %get-tuple-element.122), channel_id=1, source_target_pairs={{0,4},{4,0},{1,5},{5,1},{2,6},{6,2},{3,7},{7,3},{8,12},{12,8},{9,1... | collective-permute-start | bytes 3145736 | tf_op jit(solution)/shard_map/ppermute | solution.py:493
  196.4 4.6 %collective-permute-start.12 = (bf16[2048,128]{1,0:T(8,128)(2,1)}, bf16[2048,128]{1,0:T(8,128)(2,1)S(1)}, u32[]{:S(2)}, u32[]{:S(2)}) collective-permute-start(bf16[2048,128]{1,0:T(8,128)(2,1)} %get-tuple-element.108), channel_id=1, source_target_pairs={{0,4},{4,0},{1,5},{5,1},{2,6},{6,2},{3,7},{7,3},{8,12},{12,8},{9,1... | collective-permute-start | bytes 1572872 | tf_op jit(solution)/shard_map/ppermute | solution.py:493
  196.6 5.9 %collective-permute-start.13 = (bf16[2048,128]{1,0:T(8,128)(2,1)}, bf16[2048,128]{1,0:T(8,128)(2,1)S(1)}, u32[]{:S(2)}, u32[]{:S(2)}) collective-permute-start(bf16[2048,128]{1,0:T(8,128)(2,1)} %get-tuple-element.109), channel_id=1, source_target_pairs={{0,4},{4,0},{1,5},{5,1},{2,6},{6,2},{3,7},{7,3},{8,12},{12,8},{9,1... | collective-permute-start | bytes 1572872 | tf_op jit(solution)/shard_map/ppermute | solution.py:493
  197.5 21.2 %collective-permute-start.16 = (bf16[512,512]{1,0:T(8,128)(2,1)S(1)}, bf16[512,512]{1,0:T(8,128)(2,1)S(1)}, u32[]{:S(2)}, u32[]{:S(2)}) collective-permute-start(bf16[512,512]{1,0:T(8,128)(2,1)S(1)} %get-tuple-element.116), channel_id=1, source_target_pairs={{0,8},{8,0},{16,24},{24,16},{1,9},{9,1},{17,25},{25,17},{2,10},{10... | collective-permute-start | bytes 1572872 | tf_op jit(solution)/shard_map/ppermute | solution.py:496
  201.0 25.8 %collective-permute-start.17 = (bf16[512,512]{1,0:T(8,128)(2,1)S(1)}, bf16[512,512]{1,0:T(8,128)(2,1)S(1)}, u32[]{:S(2)}, u32[]{:S(2)}) collective-permute-start(bf16[512,512]{1,0:T(8,128)(2,1)S(1)} %get-tuple-element.117), channel_id=1, source_target_pairs={{0,16},{8,24},{16,0},{24,8},{1,17},{9,25},{17,1},{25,9},{2,18},{10... | collective-permute-start | bytes 1572872 | tf_op jit(solution)/shard_map/ppermute | solution.py:496
  202.5 34.6 %collective-permute-start.18 = (bf16[512,512]{1,0:T(8,128)(2,1)S(1)}, bf16[512,512]{1,0:T(8,128)(2,1)S(1)}, u32[]{:S(2)}, u32[]{:S(2)}) collective-permute-start(bf16[512,512]{1,0:T(8,128)(2,1)S(1)} %get-tuple-element.118), channel_id=1, source_target_pairs={{0,24},{8,16},{16,8},{24,0},{1,25},{9,17},{17,9},{25,1},{2,26},{10... | collective-permute-start | bytes 1572872 | tf_op jit(solution)/shard_map/ppermute | solution.py:496
  204.2 1.0 copy-start.9
  205.2 2.5 copy-start.3
  205.2 2.5 copy-start.4
  243.0 44.3 %all-to-all-start.3 = ((bf16[16,128,384]{2,1,0:T(8,128)(2,1)}), bf16[16,128,384]{2,1,0:T(8,128)(2,1)}, u32[]{:S(2)}, u32[]{:S(2)}) async-start(bf16[16,128,384]{2,1,0:T(8,128)(2,1)} %bitcast.11), calls=%async_computation.3 | async-start | bytes 3145728 | tf_op jit(solution)/shard_map/all_to_all | solution.py:482
  248.9 29.3 %copy-start.11 = (s32[4]{0:T(128)S(1)}, s32[4]{0:T(128)}, u32[]{:S(2)}) copy-start(s32[4]{0:T(128)} %copy-done.10) | copy-start | bytes 52
  248.9 24.4 %collective-permute-start.21 = (bf16[512,256]{1,0:T(8,128)(2,1)}, bf16[512,256]{1,0:T(8,128)(2,1)S(1)}, u32[]{:S(2)}, u32[]{:S(2)}) collective-permute-start(bf16[512,256]{1,0:T(8,128)(2,1)} %get-tuple-element.140), channel_id=1, source_target_pairs={{0,8},{8,0},{16,24},{24,16},{1,9},{9,1},{17,25},{25,17},{2,10},{10... | collective-permute-start | bytes 786440 | tf_op jit(solution)/shard_map/ppermute | solution.py:496
  250.9 22.5 %collective-permute-start.22 = (bf16[512,256]{1,0:T(8,128)(2,1)}, bf16[512,256]{1,0:T(8,128)(2,1)S(1)}, u32[]{:S(2)}, u32[]{:S(2)}) collective-permute-start(bf16[512,256]{1,0:T(8,128)(2,1)} %get-tuple-element.141), channel_id=1, source_target_pairs={{0,16},{8,24},{16,0},{24,8},{1,17},{9,25},{17,1},{25,9},{2,18},{10... | collective-permute-start | bytes 786440 | tf_op jit(solution)/shard_map/ppermute | solution.py:496
  252.3 25.9 %collective-permute-start.23 = (bf16[512,256]{1,0:T(8,128)(2,1)S(1)}, bf16[512,256]{1,0:T(8,128)(2,1)S(1)}, u32[]{:S(2)}, u32[]{:S(2)}) collective-permute-start(bf16[512,256]{1,0:T(8,128)(2,1)S(1)} %get-tuple-element.142), channel_id=1, source_target_pairs={{0,24},{8,16},{16,8},{24,0},{1,25},{9,17},{17,9},{25,1},{2,26},{10... | collective-permute-start | bytes 786440 | tf_op jit(solution)/shard_map/ppermute | solution.py:496

commit v5 on v4

--- a/solution.py
+++ b/solution.py
@@ -104,7 +104,7 @@
     )(moved, *into)
 
 
-def pack_cache(cache_k, cache_v, order):
+def pack_cache(cache_k, cache_v, order, cuts):
     rows, features = cache_k.shape
     parts = order.shape[0]
     group = features // parts
@@ -114,22 +114,25 @@
 
             @pl.when(pl.program_id(0) == p)
             def _(p=p):
-                outs[p][:, :group] = k_ref[...]
-                outs[p][:, group:] = v_ref[...]
-
-    return pl.pallas_call(
+                for s, (low, high) in enumerate(cuts):
+                    outs[s * parts + p][:, : high - low] = k_ref[:, low:high]
+                    outs[s * parts + p][:, high - low :] = v_ref[:, low:high]
+
+    widths = [2 * (high - low) for low, high in cuts for _ in range(parts)]
+    outs = pl.pallas_call(
         body,
         grid_spec=pltpu.PrefetchScalarGridSpec(
             num_scalar_prefetch=1,
             grid=(parts,),
             in_specs=[pl.BlockSpec((rows, group), lambda p, order: (0, order[p]))] * 2,
-            out_specs=[pl.BlockSpec((rows, 2 * group), lambda p, order: (0, 0))] * parts,
+            out_specs=[pl.BlockSpec((rows, w), lambda p, order: (0, 0)) for w in widths],
         ),
-        out_shape=[jax.ShapeDtypeStruct((rows, 2 * group), cache_k.dtype)] * parts,
+        out_shape=[jax.ShapeDtypeStruct((rows, w), cache_k.dtype) for w in widths],
         compiler_params=pltpu.CompilerParams(vmem_limit_bytes=32 * 2**20),
         cost_estimate=moved_bytes(8 * rows * features),
         name="pack_cache",
     )(order, cache_k, cache_v)
+    return [outs[s * parts : (s + 1) * parts] for s in range(len(cuts))]
 
 
 def sum_cores(mine_k, mine_v, recv_k, recv_v, parts):
@@ -400,10 +403,10 @@
                 gv_refs[p][...] = gvx[p * out_rows : (p + 1) * out_rows].astype(gv_refs[p].dtype)
 
 
-def attention(tables, tokens_in, prev, cache, group_width):
+def attention(tables, tokens_in, prev, cache):
     rows, width = tokens_in.shape[0], tokens_in.shape[1] // 4
     heads = width // HEAD_DIM
-    group_heads = group_width // HEAD_DIM
+    cache_heads = cache[0].shape[1] // (2 * HEAD_DIM)
     parts, part_rows = len(cache), cache[0].shape[0]
     outs = min(2, parts)
     out_rows = parts * part_rows // outs
@@ -441,7 +444,7 @@
             in_specs=[chunk_of(n * heads) for n in range(4)]
             + ([] if linked else [before(0), before(heads)])
             + [cached(0)] * parts
-            + [cached(group_heads)] * parts,
+            + [cached(cache_heads)] * parts,
             out_specs=token_specs + [column(out_rows)] * (2 * outs),
             scratch_shapes=scratch,
         ),
@@ -515,10 +518,9 @@
         before, back_at = jnp.maximum(numbers - 1 + core, 0), jnp.minimum(numbers + core, chips - 1)
         back_on = numbers + core < chips
         start_b = (2 * numbers + core) % seq_parts == 0
-        tables_b = ints(slots, reads, before, start_b, chip_order, jnp.full((1,), low // HEAD_DIM))
+        tables_b = ints(slots, reads, before, start_b, chip_order, jnp.zeros((1,)))
         backs = ints(back_at, back_on)
     else:
-        arrived = []
         zero = jnp.zeros((1,), jnp.int32)
         reads = jnp.transpose(retrieved, (1, 0, 2)).reshape(-1)
         start = (lax.axis_index(everyone) % seq_parts == 0).reshape(1)
@@ -527,15 +529,16 @@
         backs = (zero, zero + 1)
     tables = (tables_a, tables_b)
 
-    packed = pack_tokens([queries, out_grad, keys_local, values_local], zs, plan)
-    late = []
+    token_arrays = [queries, out_grad, keys_local, values_local]
+    (packed_a,), (packed_b,) = (pack_tokens(token_arrays, zs, [stage]) for stage in plan)
     if shared:
-        pieces = pack_cache(cache_keys, cache_values, chip_order)
+        pieces = pack_cache(cache_keys, cache_values, chip_order, cuts)
+    else:
+        cache_a = cache_b = [lax.all_gather(jnp.concatenate([cache_keys, cache_values], 1), everyone, tiled=True)]
+
+    def spread(pieces):
         mine = [other_chip(piece, k) for k, piece in enumerate(pieces)]
-        theirs = [other_core(piece) for piece in mine]
-        early, late = mine + theirs[:-1], theirs[-1:]
-    else:
-        early = [lax.all_gather(jnp.concatenate([cache_keys, cache_values], 1), everyone, tiled=True)]
+        return mine + [other_core(piece) for piece in mine], mine
 
     def chunks_before(keys_values):
         if shared:
@@ -547,40 +550,45 @@
             return other_core(grads)
         return lax.ppermute(grads, everyone, [(i + 1, i) for i in range(parts - 1)])
 
-    def by_tokens(stage, moved):
+    def by_tokens(stage, moved, cache):
         width = moved.shape[1] // 4
         prev = chunks_before(moved[:, 2 * width :])
-        (dq, dk, dv, dkt, dvt), gk, gv = attention(tables[stage], moved, prev, cache, group_width)
+        (dq, dk, dv, dkt, dvt), gk, gv = attention(tables[stage], moved, prev, cache)
         out = finish_tokens(*backs, dq, dk, dv, send_back(dkt), send_back(dvt))
         if not shared:
             return out, [lax.psum_scatter(g[0], everyone, scatter_dimension=0, tiled=True).astype(bf16) for g in (gk, gv)]
         return out, sum_cores(gk[0], gv[0], other_core(gk[1]), other_core(gv[1]), chips)
 
-    def by_heads(stage, moved):
-        (out,), gk, gv = attention(tables[stage], moved, None, cache, group_width)
+    def by_heads(stage, moved, cache):
+        (out,), gk, gv = attention(tables[stage], moved, None, cache)
         return out, (gk, gv)
 
-    moved_a = to_heads(after(packed[0], arrived), 0)
-    moved_a, second, early, tables = after((moved_a, packed[1], early, tables), ())
-    cache = early + late
-    moved_b = to_heads(second, 1)
-    out_a, sums_a = (by_heads if shared else by_tokens)(0, moved_a)
-    out_a, moved_b = after((out_a, moved_b), ())
-    out_a = to_tokens(out_a, 0)
-    out_b, sums_b = by_tokens(1, moved_b)
+    moved_b = to_heads(packed_b, 1)
+    early = ()
+    if shared:
+        cache_b, mine = spread(pieces[1])
+        early = (mine, arrived)
+    moved_b, packed_a, early = after((moved_b, packed_a, early), ())
+    if shared:
+        cache_a, _ = spread(after(pieces[0], moved_b))
+    moved_a = to_heads(packed_a, 0)
+    out_b, sums_b = by_tokens(1, moved_b, cache_b)
+    moved_a, out_b, sums_b, tables, cache_a = after((moved_a, out_b, sums_b, tables, cache_a), ())
+    out_b = to_tokens(out_b, 1)
+    out_a, sums_a = (by_heads if shared else by_tokens)(0, moved_a, cache_a)
+    if shared:
+        sums_b = [other_chip(s, k) for k, s in enumerate(sums_b)]
+    out_a, out_b, sums_b = after((out_a, out_b, sums_b), ())
     if shared:
         gk, gv = sums_a
         sums_a = merge_cores(tables_a[5], gk[0], gv[0], other_core(gk[1]), other_core(gv[1]), chips)
         sums_a = [other_chip(s, k) for k, s in enumerate(sums_a)]
-    out_b, out_a, sums_a, sums_b = after((out_b, out_a, sums_a, sums_b), ())
-    if shared:
-        sums_b = [other_chip(s, k) for k, s in enumerate(sums_b)]
         grad_cache = place_cache([sums_a, sums_b], chip_order, cuts)
     else:
         grad_cache = [jnp.concatenate([a, b], 1) for a, b in zip(sums_a, sums_b)]
-    grads = unpack_tokens(out_a, *plan[0], features, 3)
-    out_b = to_tokens(out_b, 1)
-    return (*add_tokens(out_b, *plan[1], grads), *grad_cache)
+    grads = unpack_tokens(out_b, *plan[1], features, 3)
+    out_a = to_tokens(out_a, 0)
+    return (*add_tokens(out_a, *plan[0], grads), *grad_cache)
 
 
 def solution(mesh):

time: 291 us -> 289 us (level)
  waiting for transfers between devices: 162 us -> 143 us
  local copies, waits for them, and re-layouts: 6.38 us -> 13.8 us
  Pallas kernels: 76.2 us -> 81 us
  starting transfers between devices: 41.2 us -> 45.1 us
    ppermute x12 -> x15, waiting for transfers between devices: 125 us -> 107 us  [other_chip(): lax.ppermute(array, 'chip', [(i, i ^ by) for i in range(chips)])]
    unnamed x42 -> x67, local copies, waits for them, and re-layouts: 5.4 us -> 10.4 us
    pallas_call x1 -> x2, Pallas kernels: 6.15 us -> 10 us  [pack_tokens(): pl.pallas_call(body, grid=(zs,), in_specs=[pl.BlockSpec((rows, features /...]
    ppermute x12 -> x16, waiting for transfers between devices: 6.16 us -> 2.28 us  [other_core(): return lax.ppermute(array, 'core', [(0, 1), (1, 0)])]
    all_to_all x4, waiting for transfers between devices: 31.1 us -> 34.3 us  [exchange(): lax.all_to_all(array, axes[stage], split_axis=0, concat_axis=0, tiled=True)]
    ppermute x12 -> x15, starting transfers between devices: 16.1 us -> 17.9 us  [other_chip(): lax.ppermute(array, 'chip', [(i, i ^ by) for i in range(chips)])]
  transfers between devices with their start and end apart: 28 -> 35, of which waited for: 15 -> 12; matrix products, arithmetic and copies ran while one was open for 1% -> 2% of each run, Pallas kernels for 25% -> 25%
where the time goes in v5:
time: 289 us; the launch traced here: 287 us
  waiting for transfers between devices  143 us (49%)
  Pallas kernels  81 us (28%)
  starting transfers between devices  45.1 us (16%)
  local copies, waits for them, and re-layouts  13.8 us (5%)
    ppermute x15, waiting for transfers between devices, other_chip(): lax.ppermute(array, 'chip', [(i, i ^ by) for i in range(chips)])  107 us
    pallas_call x2, Pallas kernels, attention(): pl.pallas_call(functools.partial(attention_kernel, parts, outs, linked),...  53.1 us
    all_to_all x4, waiting for transfers between devices, exchange(): lax.all_to_all(array, axes[stage], split_axis=0, concat_axis=0, tiled=True)  34.3 us
    all_to_all x4, starting transfers between devices, exchange(): lax.all_to_all(array, axes[stage], split_axis=0, concat_axis=0, tiled=True)  23.4 us
    ppermute x15, starting transfers between devices, other_chip(): lax.ppermute(array, 'chip', [(i, i ^ by) for i in range(chips)])  17.9 us
    unnamed x67, local copies, waits for them, and re-layouts  10.4 us
    pallas_call x2, Pallas kernels, pack_tokens(): pl.pallas_call(body, grid=(zs,), in_specs=[pl.BlockSpec((rows, features /...  10 us
  transfers between devices with their start and end apart: 35, of which 12 were waited for; matrix products, arithmetic and copies ran while one was open for 2% of the time, Pallas kernels for 25%

profile of v5, /device:TPU:0, one launch (start us, length us, event | category | flops | bytes accessed | tf_op | source)
XLA Modules:
  0.0 287.3 jit_solution(10635497178448142551)
XLA Ops:
  0.6 4.7 %pack_tokens.2 = bf16[4,4,128,512]{3,2,1,0:T(8,128)(2,1)} custom-call(bf16[128,6144]{1,0:T(8,128)(2,1)} %refs_0_.3, bf16[128,6144]{1,0:T(8,128)(2,1)} %refs_1_.3, bf16[128,6144]{1,0:T(8,128)(2,1)} %refs_2_.3, bf16[128,6144]{1,0:T(8,128)(2,1)} %refs_3_.3), custom_call_target="tpu_custom_call" | custom-call | bytes 12582912 | tf_op jit(solution)/shard_map/pack_tokens/pallas_call | solution.py:45
  5.3 8.5 %all-to-all-start = ((bf16[16,128,512]{2,1,0:T(8,128)(2,1)}), bf16[16,128,512]{2,1,0:T(8,128)(2,1)}, u32[]{:S(2)}, u32[]{:S(2)}) async-start(bf16[16,128,512]{2,1,0:T(8,128)(2,1)} %bitcast.22), calls=%async_computation | async-start | bytes 4194304 | tf_op jit(solution)/shard_map/all_to_all | solution.py:485
  13.8 1.4 copy-done.2
  15.2 2.1 pack_cache.1
  17.3 0.8 copy-done.13
  18.1 0.8 copy-done.15
  18.9 1.9 collective-permute-start
  20.8 1.5 collective-permute-start.1
  22.4 1.9 collective-permute-start.3
  24.3 1.5 collective-permute-start.4
  25.7 23.5 %collective-permute-done.3 = s32[8,4,4]{0,2,1:T(4,128)S(1)} collective-permute-done((s32[8,4,4]{0,2,1:T(4,128)S(1)}, s32[8,4,4]{0,2,1:T(4,128)S(1)}, u32[]{:S(2)}, u32[]{:S(2)}) %collective-permute-start.3) | collective-permute-done | bytes 544 | tf_op jit(solution)/shard_map/ppermute | solution.py:499
  49.2 0.5 collective-permute-start.5
  49.7 5.4 %pack_tokens.3 = bf16[8,4,128,512]{3,2,1,0:T(8,128)(2,1)} custom-call(bf16[128,6144]{1,0:T(8,128)(2,1)} %refs_0_.3, bf16[128,6144]{1,0:T(8,128)(2,1)} %refs_1_.3, bf16[128,6144]{1,0:T(8,128)(2,1)} %refs_2_.3, bf16[128,6144]{1,0:T(8,128)(2,1)} %refs_3_.3), custom_call_target="tpu_custom_call" | custom-call | bytes 12582912 | tf_op jit(solution)/shard_map/pack_tokens/pallas_call | solution.py:45
  55.1 8.7 %all-to-all-done = bf16[16,128,512]{2,1,0:T(8,128)(2,1)} async-done(((bf16[16,128,512]{2,1,0:T(8,128)(2,1)}), bf16[16,128,512]{2,1,0:T(8,128)(2,1)}, u32[]{:S(2)}, u32[]{:S(2)}) %all-to-all-start) | async-done | bytes 2097184 | tf_op jit(solution)/shard_map/all_to_all | solution.py:485
  63.8 3.6 %all-to-all-start.1 = ((bf16[32,128,512]{2,1,0:T(8,128)(2,1)}), bf16[32,128,512]{2,1,0:T(8,128)(2,1)}, u32[]{:S(2)}, u32[]{:S(2)}) async-start(bf16[32,128,512]{2,1,0:T(8,128)(2,1)} %bitcast.21), calls=%async_computation.1 | async-start | bytes 8388608 | tf_op jit(solution)/shard_map/all_to_all | solution.py:485
  67.4 2.3 slice.3
  69.8 0.5 collective-permute-start.8
  70.3 0.6 fusion.3.slots_ref
  70.9 0.6 add_maximum_fusion.before_ref
  71.5 0.5 collective-permute-start.10
  72.1 0.4 collective-permute-start.9
  72.5 0.5 compare_convert_fusion.1.start_ref
  73.5 1.7 collective-permute-start.16
  75.3 1.5 collective-permute-start.17
  76.8 1.0 copy-done.18
  77.8 19.7 %attention.2 = (bf16[2048,128]{1,0:T(8,128)(2,1)}, f32[2048,128]{1,0:T(8,128)}, f32[2048,128]{1,0:T(8,128)}, bf16[2048,128]{1,0:T(8,128)(2,1)}, bf16[2048,128]{1...) custom-call(s32[64]{0:T(128)} %fusion.3.slots_ref, ...), custom_call_target="tpu_custom_call" | custom-call | flops 3019898880 | bytes 12288000 | tf_op jit(solution)/shard_map/attention/pallas_call | solution.py:439
  97.6 0.4 collective-permute-start.18
  98.1 19.9 %collective-permute-done.16.refs_5_.refs_13_ = bf16[512,512]{1,0:T(8,128)(2,1)S(1)} collective-permute-done((bf16[512,512]{1,0:T(8,128)(2,1)S(1)}, bf16[512,512]{1,0:T(8,128)(2,1)S(1)}, u32[]{:S(2)}, u32[]{:S(2)}) %collective-permute-start.16) | collective-permute-done | bytes 524320 | tf_op jit(solution)/shard_map/ppermute | solution.py:499
  118.1 0.5 collective-permute-start.13
  118.6 16.4 %collective-permute-done.18.refs_7_.refs_15_ = bf16[512,512]{1,0:T(8,128)(2,1)S(1)} collective-permute-done((bf16[512,512]{1,0:T(8,128)(2,1)S(1)}, bf16[512,512]{1,0:T(8,128)(2,1)S(1)}, u32[]{:S(2)}, u32[]{:S(2)}) %collective-permute-start.18) | collective-permute-done | bytes 524320 | tf_op jit(solution)/shard_map/ppermute | solution.py:499
  135.0 0.5 collective-permute-start.20
  135.6 0.4 collective-permute-start.22
  136.0 0.5 fusion.9.order_ref
  136.5 0.6 compare_convert_fusion.start_ref
  137.1 1.2 copy-done.6
  138.3 1.2 copy-done.7
  139.6 1.0 copy-done.10
  140.6 2.4 finish_tokens.1
  143.0 0.4 sum_cores.1
  143.5 0.8 copy-done.22
  144.4 0.8 copy-done.24
  145.2 14.6 %all-to-all-done.1 = bf16[32,128,512]{2,1,0:T(8,128)(2,1)} async-done(((bf16[32,128,512]{2,1,0:T(8,128)(2,1)}), bf16[32,128,512]{2,1,0:T(8,128)(2,1)}, u32[]{:S(2)}, u32[]{:S(2)}) %all-to-all-start.1) | async-done | bytes 4194336 | tf_op jit(solution)/shard_map/all_to_all | solution.py:485
  159.8 0.6 iota.23.before_ref
  160.3 7.5 %all-to-all-start.2 = ((bf16[16,128,384]{2,1,0:T(8,128)(2,1)}), bf16[16,128,384]{2,1,0:T(8,128)(2,1)S(1)}, u32[]{:S(2)}, u32[]{:S(2)}) async-start(bf16[16,128,384]{2,1,0:T(8,128)(2,1)} %bitcast.9), calls=%async_computation.2 | async-start | bytes 3145728 | tf_op jit(solution)/shard_map/all_to_all | solution.py:485
  167.8 2.0 collective-permute-start.23
  169.8 1.5 collective-permute-start.24
  171.4 33.4 %attention.3 = (bf16[4096,384]{1,0:T(8,128)(2,1)}, bf16[2048,128]{1,0:T(8,128)(2,1)}, bf16[2048,128]{1,0:T(8,128)(2,1)}, bf16[2048,128]{1,0:T(8,128)(2,1)}, bf16[2048,128]{1,0:T(8,128)(2,1)}) custom-call(s32[64]{0:T(128)} %fusion.3.slots_ref, s32[256]{0:T(256)} %copy-done.29, s32[8]{0:T(128)} %iota.23.before_ref, s32[8]{0:T(128)} %compare_convert_fusion.start_ref, ...), custom_call_target="tpu_custom_call" | custom-call | flops 6039797760 | bytes 12288000 | tf_op jit(solution)/shard_map/attention/pallas_call | solution.py:439
  204.8 2.2 all-to-all-done.2
  207.0 1.1 copy-done.17
  208.1 3.9 %all-to-all-start.3 = ((bf16[32,128,384]{2,1,0:T(8,128)(2,1)}), bf16[32,128,384]{2,1,0:T(8,128)(2,1)}, u32[]{:S(2)}, u32[]{:S(2)}) async-start(bf16[32,128,384]{2,1,0:T(8,128)(2,1)} %bitcast.24), calls=%async_computation.3 | async-start | bytes 6291456 | tf_op jit(solution)/shard_map/all_to_all | solution.py:485
  212.0 0.3 collective-permute-start.26
  212.3 0.3 collective-permute-start.27
  212.6 1.4 collective-permute-done.26.recv_k_ref
  214.0 0.7 collective-permute-done.27.recv_v_ref
  214.8 1.7 merge_cores.1
  216.4 1.7 collective-permute-start.28
  218.1 1.5 collective-permute-start.29
  219.6 0.3 collective-permute-start.30
  219.9 4.2 %unpack_tokens.1 = (bf16[128,6144]{1,0:T(8,128)(2,1)}, bf16[128,6144]{1,0:T(8,128)(2,1)}, bf16[128,6144]{1,0:T(8,128)(2,1)}) custom-call(bf16[4,4,128,384]{3,2,1,0:T(8,128)(2,1)} %bitcast.23), custom_call_target="tpu_custom_call" | custom-call | bytes 9437184 | tf_op jit(solution)/shard_map/unpack_tokens/pallas_call | solution.py:65
  224.1 28.2 %collective-permute-done.28.refs_1_ = bf16[512,512]{1,0:T(8,128)(2,1)S(1)} collective-permute-done((bf16[512,512]{1,0:T(8,128)(2,1)}, bf16[512,512]{1,0:T(8,128)(2,1)S(1)}, u32[]{:S(2)}, u32[]{:S(2)}) %collective-permute-start.28) | collective-permute-done | bytes 524320 | tf_op jit(solution)/shard_map/ppermute | solution.py:499
  252.3 18.9 %collective-permute-done.30.refs_3_ = bf16[512,512]{1,0:T(8,128)(2,1)S(1)} collective-permute-done((bf16[512,512]{1,0:T(8,128)(2,1)}, bf16[512,512]{1,0:T(8,128)(2,1)S(1)}, u32[]{:S(2)}, u32[]{:S(2)}) %collective-permute-start.30) | collective-permute-done | bytes 524320 | tf_op jit(solution)/shard_map/ppermute | solution.py:499
  271.1 2.8 place_cache.1
  273.9 8.9 %all-to-all-done.3 = bf16[32,128,384]{2,1,0:T(8,128)(2,1)} async-done(((bf16[32,128,384]{2,1,0:T(8,128)(2,1)}), bf16[32,128,384]{2,1,0:T(8,128)(2,1)}, u32[]{:S(2)}, u32[]{:S(2)}) %all-to-all-start.3) | async-done | bytes 3145760 | tf_op jit(solution)/shard_map/all_to_all | solution.py:485
  282.8 4.4 %add_tokens.1 = (bf16[128,6144]{1,0:T(8,128)(2,1)}, bf16[128,6144]{1,0:T(8,128)(2,1)}, bf16[128,6144]{1,0:T(8,128)(2,1)}) custom-call(bf16[8,4,128,384]{3,2,1,0:T(8,128)(2,1)} %bitcast.12.moved_ref, bf16[128,6144]{1,0:T(8,128)(2,1)} %get-tuple-element.125.refs_0_, ...), custom_call_target="tpu_custom_call", output_to_operand_aliasing={{0}: (1, {}), {1}: (2, {}), {2}: (3, {})} | custom-call | bytes 6291456 | tf_op jit(solution)/shard_map/add_tokens/pallas_call | solution.py:95
  (101 shorter events, 1.6 us)
Async XLA Ops:
  5.3 8.5 %copy-start.1 = (bf16[512,1536]{1,0:T(8,128)(2,1)S(1)}, bf16[512,1536]{1,0:T(8,128)(2,1)}, u32[]{:S(2)}) copy-start(bf16[512,1536]{1,0:T(8,128)(2,1)} %k_ref.1) | copy-start | bytes 4718596
  5.3 58.5 %all-to-all-start = ((bf16[16,128,512]{2,1,0:T(8,128)(2,1)}), bf16[16,128,512]{2,1,0:T(8,128)(2,1)}, u32[]{:S(2)}, u32[]{:S(2)}) async-start(bf16[16,128,512]{2,1,0:T(8,128)(2,1)} %bitcast.22), calls=%async_computation | async-start | bytes 4194304 | tf_op jit(solution)/shard_map/all_to_all | solution.py:485
  13.8 1.4 copy-start.2
  15.2 2.1 copy-start.11
  15.2 7.2 %copy-start.28 = (s32[8,4,4]{0,2,1:T(4,128)S(1)}, s32[8,4,4]{0,2,1:T(4,128)}, u32[]{:S(2)}) copy-start(s32[8,4,4]{0,2,1:T(4,128)} %param.14) | copy-start | bytes 1540
  18.9 50.9 %copy-start.3 = (bf16[512,256]{1,0:T(8,128)(2,1)}, bf16[512,256]{1,0:T(8,128)(2,1)S(1)}, u32[]{:S(2)}) copy-start(bf16[512,256]{1,0:T(8,128)(2,1)S(1)} %get-tuple-element.75.refs_6_.refs_14_) | copy-start | bytes 786436
  18.9 116.0 %copy-start = (bf16[512,512]{1,0:T(8,128)(2,1)}, bf16[512,512]{1,0:T(8,128)(2,1)S(1)}, u32[]{:S(2)}) copy-start(bf16[512,512]{1,0:T(8,128)(2,1)S(1)} %get-tuple-element.109.refs_4_.refs_12_) | copy-start | bytes 1572868
  18.9 36.1 %collective-permute-start = (bf16[512,256]{1,0:T(8,128)(2,1)}, bf16[512,256]{1,0:T(8,128)(2,1)S(1)}, u32[]{:S(2)}, u32[]{:S(2)}) collective-permute-start(bf16[512,256]{1,0:T(8,128)(2,1)} %get-tuple-element.76), channel_id=1, source_target_pairs={{0,8},{8,0},{16,24},{24,16},{1,9},{9,1},{17,25},{25,17},{2,10},{10... | collective-permute-start | bytes 786440 | tf_op jit(solution)/shard_map/ppermute | solution.py:499
  20.8 34.3 %collective-permute-start.1 = (bf16[512,256]{1,0:T(8,128)(2,1)S(1)}, bf16[512,256]{1,0:T(8,128)(2,1)S(1)}, u32[]{:S(2)}, u32[]{:S(2)}) collective-permute-start(bf16[512,256]{1,0:T(8,128)(2,1)S(1)} %get-tuple-element.77), channel_id=1, source_target_pairs={{0,16},{8,24},{16,0},{24,8},{1,17},{9,25},{17,1},{25,9},{2,18},{10... | collective-permute-start | bytes 786440 | tf_op jit(solution)/shard_map/ppermute | solution.py:499
  22.3 32.8 %collective-permute-start.2 = (bf16[512,256]{1,0:T(8,128)(2,1)S(1)}, bf16[512,256]{1,0:T(8,128)(2,1)S(1)}, u32[]{:S(2)}, u32[]{:S(2)}) collective-permute-start(bf16[512,256]{1,0:T(8,128)(2,1)S(1)} %get-tuple-element.78), channel_id=1, source_target_pairs={{0,24},{8,16},{16,8},{24,0},{1,25},{9,17},{17,9},{25,1},{2,26},{10... | collective-permute-start | bytes 786440 | tf_op jit(solution)/shard_map/ppermute | solution.py:499
  22.4 26.8 %collective-permute-start.3 = (s32[8,4,4]{0,2,1:T(4,128)S(1)}, s32[8,4,4]{0,2,1:T(4,128)S(1)}, u32[]{:S(2)}, u32[]{:S(2)}) collective-permute-start(s32[8,4,4]{0,2,1:T(4,128)S(1)} %copy-done.28), channel_id=1, source_target_pairs={{0,8},{8,0},{16,24},{24,16},{1,9},{9,1},{17,25},{25,17},{2,10},{10... | collective-permute-start | bytes 1544 | tf_op jit(solution)/shard_map/ppermute | solution.py:499
  24.3 30.7 %collective-permute-start.4 = (s32[8,4,4]{0,2,1:T(4,128)S(1)}, s32[8,4,4]{0,2,1:T(4,128)S(1)}, u32[]{:S(2)}, u32[]{:S(2)}) collective-permute-start(s32[8,4,4]{0,2,1:T(4,128)S(1)} %copy-done.28), channel_id=1, source_target_pairs={{0,16},{8,24},{16,0},{24,8},{1,17},{9,25},{17,1},{25,9},{2,18},{10... | collective-permute-start | bytes 1544 | tf_op jit(solution)/shard_map/ppermute | solution.py:499
  49.2 5.8 %collective-permute-start.5 = (s32[8,4,4]{0,2,1:T(4,128)S(1)}, s32[8,4,4]{0,2,1:T(4,128)S(1)}, u32[]{:S(2)}, u32[]{:S(2)}) collective-permute-start(s32[8,4,4]{0,2,1:T(4,128)S(1)} %copy-done.28), channel_id=1, source_target_pairs={{0,24},{8,16},{16,8},{24,0},{1,25},{9,17},{17,9},{25,1},{2,26},{10... | collective-permute-start | bytes 1544 | tf_op jit(solution)/shard_map/ppermute | solution.py:499
  55.0 8.8 %copy-start.25 = (bf16[512,256]{1,0:T(8,128)(2,1)}, bf16[512,256]{1,0:T(8,128)(2,1)S(1)}, u32[]{:S(2)}) copy-start(bf16[512,256]{1,0:T(8,128)(2,1)S(1)} %collective-permute-done.refs_7_.refs_15_) | copy-start | bytes 786436
  55.1 8.7 %copy-start.26 = (bf16[512,256]{1,0:T(8,128)(2,1)}, bf16[512,256]{1,0:T(8,128)(2,1)S(1)}, u32[]{:S(2)}) copy-start(bf16[512,256]{1,0:T(8,128)(2,1)S(1)} %collective-permute-done.1.refs_8_.refs_16_) | copy-start | bytes 786436
  55.1 8.7 %copy-start.27 = (bf16[512,256]{1,0:T(8,128)(2,1)}, bf16[512,256]{1,0:T(8,128)(2,1)S(1)}, u32[]{:S(2)}) copy-start(bf16[512,256]{1,0:T(8,128)(2,1)S(1)} %collective-permute-done.2.refs_9_.refs_17_) | copy-start | bytes 786436
  63.8 95.9 %all-to-all-start.1 = ((bf16[32,128,512]{2,1,0:T(8,128)(2,1)}), bf16[32,128,512]{2,1,0:T(8,128)(2,1)}, u32[]{:S(2)}, u32[]{:S(2)}) async-start(bf16[32,128,512]{2,1,0:T(8,128)(2,1)} %bitcast.21), calls=%async_computation.1 | async-start | bytes 8388608 | tf_op jit(solution)/shard_map/all_to_all | solution.py:485
  67.4 2.9 %copy-start.30 = (s32[64]{0:T(128)S(1)}, s32[64]{0:T(128)}, u32[]{:S(2)}) copy-start(s32[64]{0:T(128)} %param.13) | copy-start | bytes 772
  67.4 6.1 %copy-start.16 = (bf16[512,512]{1,0:T(8,128)(2,1)S(1)}, bf16[512,512]{1,0:T(8,128)(2,1)}, u32[]{:S(2)}) copy-start(bf16[512,512]{1,0:T(8,128)(2,1)} %copy-done.15) | copy-start | bytes 1572868
  67.4 7.9 %copy-start.14 = (bf16[512,512]{1,0:T(8,128)(2,1)S(1)}, bf16[512,512]{1,0:T(8,128)(2,1)}, u32[]{:S(2)}) copy-start(bf16[512,512]{1,0:T(8,128)(2,1)} %copy-done.13) | copy-start | bytes 1572868
  69.8 7.0 %collective-permute-start.7 = (bf16[2048,256]{1,0:T(8,128)(2,1)}, bf16[2048,256]{1,0:T(8,128)(2,1)S(1)}, u32[]{:S(2)}, u32[]{:S(2)}) collective-permute-start(bf16[2048,256]{1,0:T(8,128)(2,1)} %slice.3), channel_id=1, source_target_pairs={{0,4},{4,0},{1,5},{5,1},{2,6},{6,2},{3,7},{7,3},{8,12},{12,8},{9,1... | collective-permute-start | bytes 3145736 | tf_op jit(solution)/shard_map/ppermute | solution.py:496
  69.8 3.7 %collective-permute-start.8 = (bf16[512,256]{1,0:T(8,128)(2,1)S(1)}, bf16[512,256]{1,0:T(8,128)(2,1)}, u32[]{:S(2)}, u32[]{:S(2)}) collective-permute-start(bf16[512,256]{1,0:T(8,128)(2,1)S(1)} %get-tuple-element.75.refs_6_.refs_14_), channel_id=1, source_target_pairs={{0,4},{4,0},{1,5},{5,1},{2,6},{6,2},{3,7},{7,3},{8,12},{12,8},{9,1... | collective-permute-start | bytes 786440 | tf_op jit(solution)/shard_map/ppermute | solution.py:496
  70.9 1.2 collective-permute-start.6
  71.5 3.8 %collective-permute-start.10 = (bf16[512,256]{1,0:T(8,128)(2,1)}, bf16[512,256]{1,0:T(8,128)(2,1)}, u32[]{:S(2)}, u32[]{:S(2)}) collective-permute-start(bf16[512,256]{1,0:T(8,128)(2,1)} %copy-done.26), channel_id=1, source_target_pairs={{0,4},{4,0},{1,5},{5,1},{2,6},{6,2},{3,7},{7,3},{8,12},{12,8},{9,1... | collective-permute-start | bytes 786440 | tf_op jit(solution)/shard_map/ppermute | solution.py:496
  72.0 4.8 %collective-permute-start.11 = (bf16[512,256]{1,0:T(8,128)(2,1)}, bf16[512,256]{1,0:T(8,128)(2,1)}, u32[]{:S(2)}, u32[]{:S(2)}) collective-permute-start(bf16[512,256]{1,0:T(8,128)(2,1)} %copy-done.27), channel_id=1, source_target_pairs={{0,4},{4,0},{1,5},{5,1},{2,6},{6,2},{3,7},{7,3},{8,12},{12,8},{9,1... | collective-permute-start | bytes 786440 | tf_op jit(solution)/shard_map/ppermute | solution.py:496
  72.1 4.7 %collective-permute-start.9 = (bf16[512,256]{1,0:T(8,128)(2,1)}, bf16[512,256]{1,0:T(8,128)(2,1)}, u32[]{:S(2)}, u32[]{:S(2)}) collective-permute-start(bf16[512,256]{1,0:T(8,128)(2,1)} %copy-done.25), channel_id=1, source_target_pairs={{0,4},{4,0},{1,5},{5,1},{2,6},{6,2},{3,7},{7,3},{8,12},{12,8},{9,1... | collective-permute-start | bytes 786440 | tf_op jit(solution)/shard_map/ppermute | solution.py:496
  73.5 3.3 %copy-start.29 = (s32[256]{0:T(256)}, s32[256]{0:T(256)S(1)}, u32[]{:S(2)}) copy-start(s32[256]{0:T(256)S(1)} %constant_dynamic-update-slice_fusion.reads_ref) | copy-start | bytes 3076
  73.5 44.5 %collective-permute-start.16 = (bf16[512,512]{1,0:T(8,128)(2,1)S(1)}, bf16[512,512]{1,0:T(8,128)(2,1)S(1)}, u32[]{:S(2)}, u32[]{:S(2)}) collective-permute-start(bf16[512,512]{1,0:T(8,128)(2,1)S(1)} %copy-done.16), channel_id=1, source_target_pairs={{0,8},{8,0},{16,24},{24,16},{1,9},{9,1},{17,25},{25,17},{2,10},{10... | collective-permute-start | bytes 1572872 | tf_op jit(solution)/shard_map/ppermute | solution.py:499
  75.3 42.8 %collective-permute-start.17 = (bf16[512,512]{1,0:T(8,128)(2,1)S(1)}, bf16[512,512]{1,0:T(8,128)(2,1)S(1)}, u32[]{:S(2)}, u32[]{:S(2)}) collective-permute-start(bf16[512,512]{1,0:T(8,128)(2,1)S(1)} %copy-done.14), channel_id=1, source_target_pairs={{0,16},{8,24},{16,0},{24,8},{1,17},{9,25},{17,1},{25,9},{2,18},{10... | collective-permute-start | bytes 1572872 | tf_op jit(solution)/shard_map/ppermute | solution.py:499
  76.8 1.0 copy-start.18
  97.5 38.1 %collective-permute-start.14 = (f32[2048,128]{1,0:T(8,128)}, f32[2048,128]{1,0:T(8,128)S(1)}, u32[]{:S(2)}, u32[]{:S(2)}) collective-permute-start(f32[2048,128]{1,0:T(8,128)} %get-tuple-element.88), channel_id=1, source_target_pairs={{0,4},{4,0},{1,5},{5,1},{2,6},{6,2},{3,7},{7,3},{8,12},{12,8},{9,1... | collective-permute-start | bytes 3145736 | tf_op jit(solution)/shard_map/ppermute | solution.py:496
  97.6 37.4 %collective-permute-start.18 = (bf16[512,512]{1,0:T(8,128)(2,1)S(1)}, bf16[512,512]{1,0:T(8,128)(2,1)S(1)}, u32[]{:S(2)}, u32[]{:S(2)}) collective-permute-start(bf16[512,512]{1,0:T(8,128)(2,1)S(1)} %get-tuple-element.101), channel_id=1, source_target_pairs={{0,24},{8,16},{16,8},{24,0},{1,25},{9,17},{17,9},{25,1},{2,26},{10... | collective-permute-start | bytes 1572872 | tf_op jit(solution)/shard_map/ppermute | solution.py:499
  98.0 45.0 %collective-permute-start.15 = (f32[2048,128]{1,0:T(8,128)}, f32[2048,128]{1,0:T(8,128)S(1)}, u32[]{:S(2)}, u32[]{:S(2)}) collective-permute-start(f32[2048,128]{1,0:T(8,128)} %get-tuple-element.89), channel_id=1, source_target_pairs={{0,4},{4,0},{1,5},{5,1},{2,6},{6,2},{3,7},{7,3},{8,12},{12,8},{9,1... | collective-permute-start | bytes 3145736 | tf_op jit(solution)/shard_map/ppermute | solution.py:496
  118.0 24.9 %copy-start.19 = (bf16[512,512]{1,0:T(8,128)(2,1)}, bf16[512,512]{1,0:T(8,128)(2,1)S(1)}, u32[]{:S(2)}) copy-start(bf16[512,512]{1,0:T(8,128)(2,1)S(1)} %collective-permute-done.16.refs_5_.refs_13_) | copy-start | bytes 1572868
  118.0 16.9 %collective-permute-start.12 = (bf16[2048,128]{1,0:T(8,128)(2,1)}, bf16[2048,128]{1,0:T(8,128)(2,1)S(1)}, u32[]{:S(2)}, u32[]{:S(2)}) collective-permute-start(bf16[2048,128]{1,0:T(8,128)(2,1)} %get-tuple-element.84), channel_id=1, source_target_pairs={{0,4},{4,0},{1,5},{5,1},{2,6},{6,2},{3,7},{7,3},{8,12},{12,8},{9,1... | collective-permute-start | bytes 1572872 | tf_op jit(solution)/shard_map/ppermute | solution.py:496
  118.1 24.9 %copy-start.20 = (bf16[512,512]{1,0:T(8,128)(2,1)}, bf16[512,512]{1,0:T(8,128)(2,1)S(1)}, u32[]{:S(2)}) copy-start(bf16[512,512]{1,0:T(8,128)(2,1)S(1)} %collective-permute-done.17.refs_6_.refs_14_) | copy-start | bytes 1572868
  118.1 17.4 %collective-permute-start.13 = (bf16[2048,128]{1,0:T(8,128)(2,1)}, bf16[2048,128]{1,0:T(8,128)(2,1)S(1)}, u32[]{:S(2)}, u32[]{:S(2)}) collective-permute-start(bf16[2048,128]{1,0:T(8,128)(2,1)} %get-tuple-element.85), channel_id=1, source_target_pairs={{0,4},{4,0},{1,5},{5,1},{2,6},{6,2},{3,7},{7,3},{8,12},{12,8},{9,1... | collective-permute-start | bytes 1572872 | tf_op jit(solution)/shard_map/ppermute | solution.py:496
  135.0 8.0 %copy-start.21 = (bf16[512,512]{1,0:T(8,128)(2,1)}, bf16[512,512]{1,0:T(8,128)(2,1)S(1)}, u32[]{:S(2)}) copy-start(bf16[512,512]{1,0:T(8,128)(2,1)S(1)} %collective-permute-done.18.refs_7_.refs_15_) | copy-start | bytes 1572868
  135.0 8.5 %collective-permute-start.19 = (bf16[512,512]{1,0:T(8,128)(2,1)S(1)}, bf16[512,512]{1,0:T(8,128)(2,1)S(1)}, u32[]{:S(2)}, u32[]{:S(2)}) collective-permute-start(bf16[512,512]{1,0:T(8,128)(2,1)S(1)} %get-tuple-element.109.refs_4_.refs_12_), channel_id=1, source_target_pairs={{0,4},{4,0},{1,5},{5,1},{2,6},{6,2},{3,7},{7,3},{8,12},{12,8},{9,1... | collective-permute-start | bytes 1572872 | tf_op jit(solution)/shard_map/ppermute | solution.py:496
  135.0 8.5 %collective-permute-start.20 = (bf16[512,512]{1,0:T(8,128)(2,1)S(1)}, bf16[512,512]{1,0:T(8,128)(2,1)S(1)}, u32[]{:S(2)}, u32[]{:S(2)}) collective-permute-start(bf16[512,512]{1,0:T(8,128)(2,1)S(1)} %collective-permute-done.16.refs_5_.refs_13_), channel_id=1, source_target_pairs={{0,4},{4,0},{1,5},{5,1},{2,6},{6,2},{3,7},{7,3},{8,12},{12,8},{9,1... | collective-permute-start | bytes 1572872 | tf_op jit(solution)/shard_map/ppermute | solution.py:496
  135.5 8.0 %collective-permute-start.21 = (bf16[512,512]{1,0:T(8,128)(2,1)S(1)}, bf16[512,512]{1,0:T(8,128)(2,1)S(1)}, u32[]{:S(2)}, u32[]{:S(2)}) collective-permute-start(bf16[512,512]{1,0:T(8,128)(2,1)S(1)} %collective-permute-done.17.refs_6_.refs_14_), channel_id=1, source_target_pairs={{0,4},{4,0},{1,5},{5,1},{2,6},{6,2},{3,7},{7,3},{8,12},{12,8},{9,1... | collective-permute-start | bytes 1572872 | tf_op jit(solution)/shard_map/ppermute | solution.py:496
  135.6 9.6 %collective-permute-start.22 = (bf16[512,512]{1,0:T(8,128)(2,1)S(1)}, bf16[512,512]{1,0:T(8,128)(2,1)}, u32[]{:S(2)}, u32[]{:S(2)}) collective-permute-start(bf16[512,512]{1,0:T(8,128)(2,1)S(1)} %collective-permute-done.18.refs_7_.refs_15_), channel_id=1, source_target_pairs={{0,4},{4,0},{1,5},{5,1},{2,6},{6,2},{3,7},{7,3},{8,12},{12,8},{9,1... | collective-permute-start | bytes 1572872 | tf_op jit(solution)/shard_map/ppermute | solution.py:496
  137.1 1.2 copy-start.6
  138.3 1.2 copy-start.7
  139.6 1.0 copy-start.10
  140.6 2.4 copy-start.4
  140.6 2.4 copy-start.5
  143.5 0.9 copy-start.23
  160.3 46.7 %all-to-all-start.2 = ((bf16[16,128,384]{2,1,0:T(8,128)(2,1)}), bf16[16,128,384]{2,1,0:T(8,128)(2,1)S(1)}, u32[]{:S(2)}, u32[]{:S(2)}) async-start(bf16[16,128,384]{2,1,0:T(8,128)(2,1)} %bitcast.9), calls=%async_computation.2 | async-start | bytes 3145728 | tf_op jit(solution)/shard_map/all_to_all | solution.py:485
  167.8 37.0 %collective-permute-start.23 = (bf16[512,256]{1,0:T(8,128)(2,1)S(1)}, bf16[512,256]{1,0:T(8,128)(2,1)S(1)}, u32[]{:S(2)}, u32[]{:S(2)}) collective-permute-start(bf16[512,256]{1,0:T(8,128)(2,1)S(1)} %get-tuple-element.120), channel_id=1, source_target_pairs={{0,8},{8,0},{16,24},{24,16},{1,9},{9,1},{17,25},{25,17},{2,10},{10... | collective-permute-start | bytes 786440 | tf_op jit(solution)/shard_map/ppermute | solution.py:499
  169.8 35.0 %collective-permute-start.24 = (bf16[512,256]{1,0:T(8,128)(2,1)S(1)}, bf16[512,256]{1,0:T(8,128)(2,1)S(1)}, u32[]{:S(2)}, u32[]{:S(2)}) collective-permute-start(bf16[512,256]{1,0:T(8,128)(2,1)S(1)} %get-tuple-element.121), channel_id=1, source_target_pairs={{0,16},{8,24},{16,0},{24,8},{1,17},{9,25},{17,1},{25,9},{2,18},{10... | collective-permute-start | bytes 786440 | tf_op jit(solution)/shard_map/ppermute | solution.py:499
  171.3 33.5 %collective-permute-start.25 = (bf16[512,256]{1,0:T(8,128)(2,1)S(1)}, bf16[512,256]{1,0:T(8,128)(2,1)S(1)}, u32[]{:S(2)}, u32[]{:S(2)}) collective-permute-start(bf16[512,256]{1,0:T(8,128)(2,1)S(1)} %get-tuple-element.122), channel_id=1, source_target_pairs={{0,24},{8,16},{16,8},{24,0},{1,25},{9,17},{17,9},{25,1},{2,26},{10... | collective-permute-start | bytes 786440 | tf_op jit(solution)/shard_map/ppermute | solution.py:499
  207.0 1.1 copy-start.17
  208.1 3.9 %copy-start.32 = (bf16[2048,128]{1,0:T(8,128)(2,1)S(1)}, bf16[2048,128]{1,0:T(8,128)(2,1)}, u32[]{:S(2)}) copy-start(bf16[2048,128]{1,0:T(8,128)(2,1)} %get-tuple-element.133) | copy-start | bytes 1572868
  208.1 4.1 %copy-start.31 = (bf16[2048,128]{1,0:T(8,128)(2,1)S(1)}, bf16[2048,128]{1,0:T(8,128)(2,1)}, u32[]{:S(2)}) copy-start(bf16[2048,128]{1,0:T(8,128)(2,1)} %get-tuple-element.134) | copy-start | bytes 1572868
  208.1 6.6 %copy-start.8 = (bf16[2048,128]{1,0:T(8,128)(2,1)S(1)}, bf16[2048,128]{1,0:T(8,128)(2,1)}, u32[]{:S(2)}) copy-start(bf16[2048,128]{1,0:T(8,128)(2,1)} %get-tuple-element.131.mine_k_ref) | copy-start | bytes 1572868
  208.1 6.6 %copy-start.9 = (bf16[2048,128]{1,0:T(8,128)(2,1)S(1)}, bf16[2048,128]{1,0:T(8,128)(2,1)}, u32[]{:S(2)}) copy-start(bf16[2048,128]{1,0:T(8,128)(2,1)} %get-tuple-element.132.mine_v_ref) | copy-start | bytes 1572868
  208.1 74.7 %all-to-all-start.3 = ((bf16[32,128,384]{2,1,0:T(8,128)(2,1)}), bf16[32,128,384]{2,1,0:T(8,128)(2,1)}, u32[]{:S(2)}, u32[]{:S(2)}) async-start(bf16[32,128,384]{2,1,0:T(8,128)(2,1)} %bitcast.24), calls=%async_computation.3 | async-start | bytes 6291456 | tf_op jit(solution)/shard_map/all_to_all | solution.py:485
  212.0 2.0 collective-permute-start.26
  212.3 2.5 collective-permute-start.27
  214.8 56.4 %copy-start.12 = (s32[4]{0:T(128)S(1)}, s32[4]{0:T(128)}, u32[]{:S(2)}) copy-start(s32[4]{0:T(128)} %copy-done.11) | copy-start | bytes 52
  216.4 35.9 %collective-permute-start.28 = (bf16[512,512]{1,0:T(8,128)(2,1)}, bf16[512,512]{1,0:T(8,128)(2,1)S(1)}, u32[]{:S(2)}, u32[]{:S(2)}) collective-permute-start(bf16[512,512]{1,0:T(8,128)(2,1)} %get-tuple-element.136), channel_id=1, source_target_pairs={{0,8},{8,0},{16,24},{24,16},{1,9},{9,1},{17,25},{25,17},{2,10},{10... | collective-permute-start | bytes 1572872 | tf_op jit(solution)/shard_map/ppermute | solution.py:499
  218.1 34.2 %collective-permute-start.29 = (bf16[512,512]{1,0:T(8,128)(2,1)}, bf16[512,512]{1,0:T(8,128)(2,1)S(1)}, u32[]{:S(2)}, u32[]{:S(2)}) collective-permute-start(bf16[512,512]{1,0:T(8,128)(2,1)} %get-tuple-element.137), channel_id=1, source_target_pairs={{0,16},{8,24},{16,0},{24,8},{1,17},{9,25},{17,1},{25,9},{2,18},{10... | collective-permute-start | bytes 1572872 | tf_op jit(solution)/shard_map/ppermute | solution.py:499
  219.6 51.6 %collective-permute-start.30 = (bf16[512,512]{1,0:T(8,128)(2,1)}, bf16[512,512]{1,0:T(8,128)(2,1)S(1)}, u32[]{:S(2)}, u32[]{:S(2)}) collective-permute-start(bf16[512,512]{1,0:T(8,128)(2,1)} %get-tuple-element.138), channel_id=1, source_target_pairs={{0,24},{8,16},{16,8},{24,0},{1,25},{9,17},{17,9},{25,1},{2,26},{10... | collective-permute-start | bytes 1572872 | tf_op jit(solution)/shard_map/ppermute | solution.py:499
  (4 other events, 3.2 us)

commit v6 on v5

--- a/solution.py
+++ b/solution.py
@@ -50,6 +50,35 @@
         out_shape=[jax.ShapeDtypeStruct((len(p), zs, rows, count * w), arrays[0].dtype) for p, w in plan],
         cost_estimate=moved_bytes(4 * count * rows * features),
         name="pack_tokens",
+    )(*arrays)
+
+
+def pack_by_copies(arrays, zs, places, width):
+    rows, features = arrays[0].shape
+    count, group = len(arrays), features // zs
+
+    def body(*refs):
+        out, sem = refs[count], refs[count + 1]
+        copies = []
+        for z in range(zs):
+            for p, low in enumerate(places):
+                for n in range(count):
+                    source = refs[n].at[:, pl.ds(z * group + low, width)]
+                    target = out.at[p, z, :, pl.ds(n * width, width)]
+                    copies.append(pltpu.make_async_copy(source, target, sem.at[len(copies)]))
+                    copies[-1].start()
+        for copy in copies:
+            copy.wait()
+
+    return pl.pallas_call(
+        body,
+        in_specs=[pl.BlockSpec(memory_space=pl.ANY)] * count,
+        out_specs=pl.BlockSpec(memory_space=pltpu.VMEM),
+        out_shape=jax.ShapeDtypeStruct((len(places), zs, rows, count * width), arrays[0].dtype),
+        scratch_shapes=[pltpu.SemaphoreType.DMA((zs * len(places) * count,))],
+        compiler_params=pltpu.CompilerParams(vmem_limit_bytes=58 * 2**20),
+        cost_estimate=moved_bytes(4 * count * rows * zs * len(places) * width),
+        name="pack_by_copies",
     )(*arrays)
 
 
@@ -530,7 +559,8 @@
     tables = (tables_a, tables_b)
 
     token_arrays = [queries, out_grad, keys_local, values_local]
-    (packed_a,), (packed_b,) = (pack_tokens(token_arrays, zs, [stage]) for stage in plan)
+    packed_b = pack_by_copies(token_arrays, zs, *plan[1])
+    (packed_a,) = pack_tokens(token_arrays, zs, plan[:1])
     if shared:
         pieces = pack_cache(cache_keys, cache_values, chip_order, cuts)
     else:

time: 289 us -> 287 us (level)
    pallas_call x2 -> x1, Pallas kernels: 10 us -> 5.37 us  [pack_tokens(): pl.pallas_call(body, grid=(zs,), in_specs=[pl.BlockSpec((rows, features /...]
    pallas_call x0 -> x1, Pallas kernels: none -> 3.42 us  [pack_by_copies(): pl.pallas_call(body, in_specs=[pl.BlockSpec(memory_space=pl.ANY)] * count...]
where the time goes in v6:
time: 287 us; the launch traced here: 286 us
  waiting for transfers between devices  143 us (50%)
  Pallas kernels  79.7 us (28%)
  starting transfers between devices  45.2 us (16%)
  local copies, waits for them, and re-layouts  13.8 us (5%)
    ppermute x15, waiting for transfers between devices, other_chip(): lax.ppermute(array, 'chip', [(i, i ^ by) for i in range(chips)])  107 us
    pallas_call x2, Pallas kernels, attention(): pl.pallas_call(functools.partial(attention_kernel, parts, outs, linked),...  53.1 us
    all_to_all x4, waiting for transfers between devices, exchange(): lax.all_to_all(array, axes[stage], split_axis=0, concat_axis=0, tiled=True)  34.3 us
    all_to_all x4, starting transfers between devices, exchange(): lax.all_to_all(array, axes[stage], split_axis=0, concat_axis=0, tiled=True)  23.5 us
    ppermute x15, starting transfers between devices, other_chip(): lax.ppermute(array, 'chip', [(i, i ^ by) for i in range(chips)])  17.9 us
    unnamed x67, local copies, waits for them, and re-layouts  10.4 us
  transfers between devices with their start and end apart: 35, of which 12 were waited for; matrix products, arithmetic and copies ran while one was open for 2% of the time, Pallas kernels for 25%

profile of v6, /device:TPU:0, one launch (start us, length us, event | category | flops | bytes accessed | tf_op | source)
XLA Modules:
  0.0 286.1 jit_solution(955625281632714304)
XLA Ops:
  0.6 3.4 %pack_by_copies.1 = bf16[4,4,128,512]{3,2,1,0:T(8,128)(2,1)} custom-call(bf16[128,6144]{1,0:T(8,128)(2,1)} %refs_0_.3, bf16[128,6144]{1,0:T(8,128)(2,1)} %refs_1_.3, bf16[128,6144]{1,0:T(8,128)(2,1)} %refs_2_.3, bf16[128,6144]{1,0:T(8,128)(2,1)} %refs_3_.3), custom_call_target="tpu_custom_call" | custom-call | bytes 4194304 | tf_op jit(solution)/shard_map/pack_by_copies/pallas_call | solution.py:73
  4.1 8.5 %all-to-all-start = ((bf16[16,128,512]{2,1,0:T(8,128)(2,1)}), bf16[16,128,512]{2,1,0:T(8,128)(2,1)}, u32[]{:S(2)}, u32[]{:S(2)}) async-start(bf16[16,128,512]{2,1,0:T(8,128)(2,1)} %bitcast.22), calls=%async_computation | async-start | bytes 4194304 | tf_op jit(solution)/shard_map/all_to_all | solution.py:514
  12.6 1.4 copy-done.2
  14.0 2.1 pack_cache.1
  16.1 0.8 copy-done.13
  16.9 0.8 copy-done.15
  17.7 1.9 collective-permute-start
  19.6 1.5 collective-permute-start.1
  21.2 1.9 collective-permute-start.3
  23.1 1.5 collective-permute-start.4
  24.5 23.5 %collective-permute-done.3 = s32[8,4,4]{0,2,1:T(4,128)S(1)} collective-permute-done((s32[8,4,4]{0,2,1:T(4,128)S(1)}, s32[8,4,4]{0,2,1:T(4,128)S(1)}, u32[]{:S(2)}, u32[]{:S(2)}) %collective-permute-start.3) | collective-permute-done | bytes 544 | tf_op jit(solution)/shard_map/ppermute | solution.py:528
  48.0 0.5 collective-permute-start.5
  48.4 5.4 %pack_tokens.1 = bf16[8,4,128,512]{3,2,1,0:T(8,128)(2,1)} custom-call(bf16[128,6144]{1,0:T(8,128)(2,1)} %refs_0_.3, bf16[128,6144]{1,0:T(8,128)(2,1)} %refs_1_.3, bf16[128,6144]{1,0:T(8,128)(2,1)} %refs_2_.3, bf16[128,6144]{1,0:T(8,128)(2,1)} %refs_3_.3), custom_call_target="tpu_custom_call" | custom-call | bytes 12582912 | tf_op jit(solution)/shard_map/pack_tokens/pallas_call | solution.py:45
  53.9 8.7 %all-to-all-done = bf16[16,128,512]{2,1,0:T(8,128)(2,1)} async-done(((bf16[16,128,512]{2,1,0:T(8,128)(2,1)}), bf16[16,128,512]{2,1,0:T(8,128)(2,1)}, u32[]{:S(2)}, u32[]{:S(2)}) %all-to-all-start) | async-done | bytes 2097184 | tf_op jit(solution)/shard_map/all_to_all | solution.py:514
  62.6 3.6 %all-to-all-start.1 = ((bf16[32,128,512]{2,1,0:T(8,128)(2,1)}), bf16[32,128,512]{2,1,0:T(8,128)(2,1)}, u32[]{:S(2)}, u32[]{:S(2)}) async-start(bf16[32,128,512]{2,1,0:T(8,128)(2,1)} %bitcast.21), calls=%async_computation.1 | async-start | bytes 8388608 | tf_op jit(solution)/shard_map/all_to_all | solution.py:514
  66.2 2.3 slice.3
  68.6 0.5 collective-permute-start.8
  69.1 0.6 fusion.3.slots_ref
  69.7 0.6 add_maximum_fusion.before_ref
  70.3 0.5 collective-permute-start.10
  70.9 0.4 collective-permute-start.9
  71.3 0.5 compare_convert_fusion.1.start_ref
  72.3 1.7 collective-permute-start.16
  74.1 1.5 collective-permute-start.17
  75.6 1.0 copy-done.18
  76.6 19.7 %attention.2 = (bf16[2048,128]{1,0:T(8,128)(2,1)}, f32[2048,128]{1,0:T(8,128)}, f32[2048,128]{1,0:T(8,128)}, bf16[2048,128]{1,0:T(8,128)(2,1)}, bf16[2048,128]{1...) custom-call(s32[64]{0:T(128)} %fusion.3.slots_ref, ...), custom_call_target="tpu_custom_call" | custom-call | flops 3019898880 | bytes 12288000 | tf_op jit(solution)/shard_map/attention/pallas_call | solution.py:468
  96.4 0.4 collective-permute-start.18
  96.9 19.9 %collective-permute-done.16.refs_5_.refs_13_ = bf16[512,512]{1,0:T(8,128)(2,1)S(1)} collective-permute-done((bf16[512,512]{1,0:T(8,128)(2,1)S(1)}, bf16[512,512]{1,0:T(8,128)(2,1)S(1)}, u32[]{:S(2)}, u32[]{:S(2)}) %collective-permute-start.16) | collective-permute-done | bytes 524320 | tf_op jit(solution)/shard_map/ppermute | solution.py:528
  116.9 0.5 collective-permute-start.13
  117.4 16.4 %collective-permute-done.18.refs_7_.refs_15_ = bf16[512,512]{1,0:T(8,128)(2,1)S(1)} collective-permute-done((bf16[512,512]{1,0:T(8,128)(2,1)S(1)}, bf16[512,512]{1,0:T(8,128)(2,1)S(1)}, u32[]{:S(2)}, u32[]{:S(2)}) %collective-permute-start.18) | collective-permute-done | bytes 524320 | tf_op jit(solution)/shard_map/ppermute | solution.py:528
  133.8 0.5 collective-permute-start.20
  134.3 0.4 collective-permute-start.22
  134.8 0.5 fusion.9.order_ref
  135.3 0.6 compare_convert_fusion.start_ref
  135.9 1.2 copy-done.6
  137.1 1.2 copy-done.7
  138.4 1.0 copy-done.10
  139.4 2.4 finish_tokens.1
  141.8 0.4 sum_cores.1
  142.3 0.8 copy-done.22
  143.2 0.8 copy-done.24
  144.0 14.6 %all-to-all-done.1 = bf16[32,128,512]{2,1,0:T(8,128)(2,1)} async-done(((bf16[32,128,512]{2,1,0:T(8,128)(2,1)}), bf16[32,128,512]{2,1,0:T(8,128)(2,1)}, u32[]{:S(2)}, u32[]{:S(2)}) %all-to-all-start.1) | async-done | bytes 4194336 | tf_op jit(solution)/shard_map/all_to_all | solution.py:514
  158.5 0.6 iota.23.before_ref
  159.1 7.5 %all-to-all-start.2 = ((bf16[16,128,384]{2,1,0:T(8,128)(2,1)}), bf16[16,128,384]{2,1,0:T(8,128)(2,1)S(1)}, u32[]{:S(2)}, u32[]{:S(2)}) async-start(bf16[16,128,384]{2,1,0:T(8,128)(2,1)} %bitcast.9), calls=%async_computation.2 | async-start | bytes 3145728 | tf_op jit(solution)/shard_map/all_to_all | solution.py:514
  166.6 2.0 collective-permute-start.23
  168.6 1.5 collective-permute-start.24
  170.2 33.4 %attention.3 = (bf16[4096,384]{1,0:T(8,128)(2,1)}, bf16[2048,128]{1,0:T(8,128)(2,1)}, bf16[2048,128]{1,0:T(8,128)(2,1)}, bf16[2048,128]{1,0:T(8,128)(2,1)}, bf16[2048,128]{1,0:T(8,128)(2,1)}) custom-call(s32[64]{0:T(128)} %fusion.3.slots_ref, s32[256]{0:T(256)} %copy-done.29, s32[8]{0:T(128)} %iota.23.before_ref, s32[8]{0:T(128)} %compare_convert_fusion.start_ref, ...), custom_call_target="tpu_custom_call" | custom-call | flops 6039797760 | bytes 12288000 | tf_op jit(solution)/shard_map/attention/pallas_call | solution.py:468
  203.6 2.2 all-to-all-done.2
  205.8 1.1 copy-done.17
  206.9 3.9 %all-to-all-start.3 = ((bf16[32,128,384]{2,1,0:T(8,128)(2,1)}), bf16[32,128,384]{2,1,0:T(8,128)(2,1)}, u32[]{:S(2)}, u32[]{:S(2)}) async-start(bf16[32,128,384]{2,1,0:T(8,128)(2,1)} %bitcast.24), calls=%async_computation.3 | async-start | bytes 6291456 | tf_op jit(solution)/shard_map/all_to_all | solution.py:514
  210.8 0.3 collective-permute-start.26
  211.1 0.3 collective-permute-start.27
  211.4 1.4 collective-permute-done.26.recv_k_ref
  212.8 0.7 collective-permute-done.27.recv_v_ref
  213.6 1.7 merge_cores.1
  215.2 1.7 collective-permute-start.28
  216.9 1.5 collective-permute-start.29
  218.4 0.3 collective-permute-start.30
  218.7 4.2 %unpack_tokens.1 = (bf16[128,6144]{1,0:T(8,128)(2,1)}, bf16[128,6144]{1,0:T(8,128)(2,1)}, bf16[128,6144]{1,0:T(8,128)(2,1)}) custom-call(bf16[4,4,128,384]{3,2,1,0:T(8,128)(2,1)} %bitcast.23), custom_call_target="tpu_custom_call" | custom-call | bytes 9437184 | tf_op jit(solution)/shard_map/unpack_tokens/pallas_call | solution.py:94
  222.9 28.2 %collective-permute-done.28.refs_1_ = bf16[512,512]{1,0:T(8,128)(2,1)S(1)} collective-permute-done((bf16[512,512]{1,0:T(8,128)(2,1)}, bf16[512,512]{1,0:T(8,128)(2,1)S(1)}, u32[]{:S(2)}, u32[]{:S(2)}) %collective-permute-start.28) | collective-permute-done | bytes 524320 | tf_op jit(solution)/shard_map/ppermute | solution.py:528
  251.1 18.9 %collective-permute-done.30.refs_3_ = bf16[512,512]{1,0:T(8,128)(2,1)S(1)} collective-permute-done((bf16[512,512]{1,0:T(8,128)(2,1)}, bf16[512,512]{1,0:T(8,128)(2,1)S(1)}, u32[]{:S(2)}, u32[]{:S(2)}) %collective-permute-start.30) | collective-permute-done | bytes 524320 | tf_op jit(solution)/shard_map/ppermute | solution.py:528
  269.9 2.8 place_cache.1
  272.7 8.9 %all-to-all-done.3 = bf16[32,128,384]{2,1,0:T(8,128)(2,1)} async-done(((bf16[32,128,384]{2,1,0:T(8,128)(2,1)}), bf16[32,128,384]{2,1,0:T(8,128)(2,1)}, u32[]{:S(2)}, u32[]{:S(2)}) %all-to-all-start.3) | async-done | bytes 3145760 | tf_op jit(solution)/shard_map/all_to_all | solution.py:514
  281.6 4.4 %add_tokens.1 = (bf16[128,6144]{1,0:T(8,128)(2,1)}, bf16[128,6144]{1,0:T(8,128)(2,1)}, bf16[128,6144]{1,0:T(8,128)(2,1)}) custom-call(bf16[8,4,128,384]{3,2,1,0:T(8,128)(2,1)} %bitcast.12.moved_ref, bf16[128,6144]{1,0:T(8,128)(2,1)} %get-tuple-element.125.refs_0_, ...), custom_call_target="tpu_custom_call", output_to_operand_aliasing={{0}: (1, {}), {1}: (2, {}), {2}: (3, {})} | custom-call | bytes 6291456 | tf_op jit(solution)/shard_map/add_tokens/pallas_call | solution.py:124
  (101 shorter events, 1.6 us)
Async XLA Ops:
  4.1 8.5 %copy-start.1 = (bf16[512,1536]{1,0:T(8,128)(2,1)S(1)}, bf16[512,1536]{1,0:T(8,128)(2,1)}, u32[]{:S(2)}) copy-start(bf16[512,1536]{1,0:T(8,128)(2,1)} %k_ref.1) | copy-start | bytes 4718596
  4.1 58.5 %all-to-all-start = ((bf16[16,128,512]{2,1,0:T(8,128)(2,1)}), bf16[16,128,512]{2,1,0:T(8,128)(2,1)}, u32[]{:S(2)}, u32[]{:S(2)}) async-start(bf16[16,128,512]{2,1,0:T(8,128)(2,1)} %bitcast.22), calls=%async_computation | async-start | bytes 4194304 | tf_op jit(solution)/shard_map/all_to_all | solution.py:514
  12.6 1.4 copy-start.2
  14.0 2.1 copy-start.11
  14.0 7.2 %copy-start.28 = (s32[8,4,4]{0,2,1:T(4,128)S(1)}, s32[8,4,4]{0,2,1:T(4,128)}, u32[]{:S(2)}) copy-start(s32[8,4,4]{0,2,1:T(4,128)} %param.14) | copy-start | bytes 1540
  17.7 50.9 %copy-start.3 = (bf16[512,256]{1,0:T(8,128)(2,1)}, bf16[512,256]{1,0:T(8,128)(2,1)S(1)}, u32[]{:S(2)}) copy-start(bf16[512,256]{1,0:T(8,128)(2,1)S(1)} %get-tuple-element.75.refs_6_.refs_14_) | copy-start | bytes 786436
  17.7 116.0 %copy-start = (bf16[512,512]{1,0:T(8,128)(2,1)}, bf16[512,512]{1,0:T(8,128)(2,1)S(1)}, u32[]{:S(2)}) copy-start(bf16[512,512]{1,0:T(8,128)(2,1)S(1)} %get-tuple-element.109.refs_4_.refs_12_) | copy-start | bytes 1572868
  17.7 36.1 %collective-permute-start = (bf16[512,256]{1,0:T(8,128)(2,1)}, bf16[512,256]{1,0:T(8,128)(2,1)S(1)}, u32[]{:S(2)}, u32[]{:S(2)}) collective-permute-start(bf16[512,256]{1,0:T(8,128)(2,1)} %get-tuple-element.76), channel_id=1, source_target_pairs={{0,8},{8,0},{16,24},{24,16},{1,9},{9,1},{17,25},{25,17},{2,10},{10... | collective-permute-start | bytes 786440 | tf_op jit(solution)/shard_map/ppermute | solution.py:528
  19.6 34.3 %collective-permute-start.1 = (bf16[512,256]{1,0:T(8,128)(2,1)S(1)}, bf16[512,256]{1,0:T(8,128)(2,1)S(1)}, u32[]{:S(2)}, u32[]{:S(2)}) collective-permute-start(bf16[512,256]{1,0:T(8,128)(2,1)S(1)} %get-tuple-element.77), channel_id=1, source_target_pairs={{0,16},{8,24},{16,0},{24,8},{1,17},{9,25},{17,1},{25,9},{2,18},{10... | collective-permute-start | bytes 786440 | tf_op jit(solution)/shard_map/ppermute | solution.py:528
  21.0 32.8 %collective-permute-start.2 = (bf16[512,256]{1,0:T(8,128)(2,1)S(1)}, bf16[512,256]{1,0:T(8,128)(2,1)S(1)}, u32[]{:S(2)}, u32[]{:S(2)}) collective-permute-start(bf16[512,256]{1,0:T(8,128)(2,1)S(1)} %get-tuple-element.78), channel_id=1, source_target_pairs={{0,24},{8,16},{16,8},{24,0},{1,25},{9,17},{17,9},{25,1},{2,26},{10... | collective-permute-start | bytes 786440 | tf_op jit(solution)/shard_map/ppermute | solution.py:528
  21.2 26.8 %collective-permute-start.3 = (s32[8,4,4]{0,2,1:T(4,128)S(1)}, s32[8,4,4]{0,2,1:T(4,128)S(1)}, u32[]{:S(2)}, u32[]{:S(2)}) collective-permute-start(s32[8,4,4]{0,2,1:T(4,128)S(1)} %copy-done.28), channel_id=1, source_target_pairs={{0,8},{8,0},{16,24},{24,16},{1,9},{9,1},{17,25},{25,17},{2,10},{10... | collective-permute-start | bytes 1544 | tf_op jit(solution)/shard_map/ppermute | solution.py:528
  23.1 30.7 %collective-permute-start.4 = (s32[8,4,4]{0,2,1:T(4,128)S(1)}, s32[8,4,4]{0,2,1:T(4,128)S(1)}, u32[]{:S(2)}, u32[]{:S(2)}) collective-permute-start(s32[8,4,4]{0,2,1:T(4,128)S(1)} %copy-done.28), channel_id=1, source_target_pairs={{0,16},{8,24},{16,0},{24,8},{1,17},{9,25},{17,1},{25,9},{2,18},{10... | collective-permute-start | bytes 1544 | tf_op jit(solution)/shard_map/ppermute | solution.py:528
  48.0 5.8 %collective-permute-start.5 = (s32[8,4,4]{0,2,1:T(4,128)S(1)}, s32[8,4,4]{0,2,1:T(4,128)S(1)}, u32[]{:S(2)}, u32[]{:S(2)}) collective-permute-start(s32[8,4,4]{0,2,1:T(4,128)S(1)} %copy-done.28), channel_id=1, source_target_pairs={{0,24},{8,16},{16,8},{24,0},{1,25},{9,17},{17,9},{25,1},{2,26},{10... | collective-permute-start | bytes 1544 | tf_op jit(solution)/shard_map/ppermute | solution.py:528
  53.8 8.8 %copy-start.25 = (bf16[512,256]{1,0:T(8,128)(2,1)}, bf16[512,256]{1,0:T(8,128)(2,1)S(1)}, u32[]{:S(2)}) copy-start(bf16[512,256]{1,0:T(8,128)(2,1)S(1)} %collective-permute-done.refs_7_.refs_15_) | copy-start | bytes 786436
  53.9 8.7 %copy-start.26 = (bf16[512,256]{1,0:T(8,128)(2,1)}, bf16[512,256]{1,0:T(8,128)(2,1)S(1)}, u32[]{:S(2)}) copy-start(bf16[512,256]{1,0:T(8,128)(2,1)S(1)} %collective-permute-done.1.refs_8_.refs_16_) | copy-start | bytes 786436
  53.9 8.7 %copy-start.27 = (bf16[512,256]{1,0:T(8,128)(2,1)}, bf16[512,256]{1,0:T(8,128)(2,1)S(1)}, u32[]{:S(2)}) copy-start(bf16[512,256]{1,0:T(8,128)(2,1)S(1)} %collective-permute-done.2.refs_9_.refs_17_) | copy-start | bytes 786436
  62.6 95.9 %all-to-all-start.1 = ((bf16[32,128,512]{2,1,0:T(8,128)(2,1)}), bf16[32,128,512]{2,1,0:T(8,128)(2,1)}, u32[]{:S(2)}, u32[]{:S(2)}) async-start(bf16[32,128,512]{2,1,0:T(8,128)(2,1)} %bitcast.21), calls=%async_computation.1 | async-start | bytes 8388608 | tf_op jit(solution)/shard_map/all_to_all | solution.py:514
  66.2 2.9 %copy-start.30 = (s32[64]{0:T(128)S(1)}, s32[64]{0:T(128)}, u32[]{:S(2)}) copy-start(s32[64]{0:T(128)} %param.13) | copy-start | bytes 772
  66.2 6.1 %copy-start.16 = (bf16[512,512]{1,0:T(8,128)(2,1)S(1)}, bf16[512,512]{1,0:T(8,128)(2,1)}, u32[]{:S(2)}) copy-start(bf16[512,512]{1,0:T(8,128)(2,1)} %copy-done.15) | copy-start | bytes 1572868
  66.2 7.9 %copy-start.14 = (bf16[512,512]{1,0:T(8,128)(2,1)S(1)}, bf16[512,512]{1,0:T(8,128)(2,1)}, u32[]{:S(2)}) copy-start(bf16[512,512]{1,0:T(8,128)(2,1)} %copy-done.13) | copy-start | bytes 1572868
  68.6 7.0 %collective-permute-start.7 = (bf16[2048,256]{1,0:T(8,128)(2,1)}, bf16[2048,256]{1,0:T(8,128)(2,1)S(1)}, u32[]{:S(2)}, u32[]{:S(2)}) collective-permute-start(bf16[2048,256]{1,0:T(8,128)(2,1)} %slice.3), channel_id=1, source_target_pairs={{0,4},{4,0},{1,5},{5,1},{2,6},{6,2},{3,7},{7,3},{8,12},{12,8},{9,1... | collective-permute-start | bytes 3145736 | tf_op jit(solution)/shard_map/ppermute | solution.py:525
  68.6 3.7 %collective-permute-start.8 = (bf16[512,256]{1,0:T(8,128)(2,1)S(1)}, bf16[512,256]{1,0:T(8,128)(2,1)}, u32[]{:S(2)}, u32[]{:S(2)}) collective-permute-start(bf16[512,256]{1,0:T(8,128)(2,1)S(1)} %get-tuple-element.75.refs_6_.refs_14_), channel_id=1, source_target_pairs={{0,4},{4,0},{1,5},{5,1},{2,6},{6,2},{3,7},{7,3},{8,12},{12,8},{9,1... | collective-permute-start | bytes 786440 | tf_op jit(solution)/shard_map/ppermute | solution.py:525
  69.7 1.2 collective-permute-start.6
  70.3 3.8 %collective-permute-start.10 = (bf16[512,256]{1,0:T(8,128)(2,1)}, bf16[512,256]{1,0:T(8,128)(2,1)}, u32[]{:S(2)}, u32[]{:S(2)}) collective-permute-start(bf16[512,256]{1,0:T(8,128)(2,1)} %copy-done.26), channel_id=1, source_target_pairs={{0,4},{4,0},{1,5},{5,1},{2,6},{6,2},{3,7},{7,3},{8,12},{12,8},{9,1... | collective-permute-start | bytes 786440 | tf_op jit(solution)/shard_map/ppermute | solution.py:525
  70.8 4.8 %collective-permute-start.11 = (bf16[512,256]{1,0:T(8,128)(2,1)}, bf16[512,256]{1,0:T(8,128)(2,1)}, u32[]{:S(2)}, u32[]{:S(2)}) collective-permute-start(bf16[512,256]{1,0:T(8,128)(2,1)} %copy-done.27), channel_id=1, source_target_pairs={{0,4},{4,0},{1,5},{5,1},{2,6},{6,2},{3,7},{7,3},{8,12},{12,8},{9,1... | collective-permute-start | bytes 786440 | tf_op jit(solution)/shard_map/ppermute | solution.py:525
  70.9 4.7 %collective-permute-start.9 = (bf16[512,256]{1,0:T(8,128)(2,1)}, bf16[512,256]{1,0:T(8,128)(2,1)}, u32[]{:S(2)}, u32[]{:S(2)}) collective-permute-start(bf16[512,256]{1,0:T(8,128)(2,1)} %copy-done.25), channel_id=1, source_target_pairs={{0,4},{4,0},{1,5},{5,1},{2,6},{6,2},{3,7},{7,3},{8,12},{12,8},{9,1... | collective-permute-start | bytes 786440 | tf_op jit(solution)/shard_map/ppermute | solution.py:525
  72.3 3.3 %copy-start.29 = (s32[256]{0:T(256)}, s32[256]{0:T(256)S(1)}, u32[]{:S(2)}) copy-start(s32[256]{0:T(256)S(1)} %constant_dynamic-update-slice_fusion.reads_ref) | copy-start | bytes 3076
  72.3 44.5 %collective-permute-start.16 = (bf16[512,512]{1,0:T(8,128)(2,1)S(1)}, bf16[512,512]{1,0:T(8,128)(2,1)S(1)}, u32[]{:S(2)}, u32[]{:S(2)}) collective-permute-start(bf16[512,512]{1,0:T(8,128)(2,1)S(1)} %copy-done.16), channel_id=1, source_target_pairs={{0,8},{8,0},{16,24},{24,16},{1,9},{9,1},{17,25},{25,17},{2,10},{10... | collective-permute-start | bytes 1572872 | tf_op jit(solution)/shard_map/ppermute | solution.py:528
  74.1 42.8 %collective-permute-start.17 = (bf16[512,512]{1,0:T(8,128)(2,1)S(1)}, bf16[512,512]{1,0:T(8,128)(2,1)S(1)}, u32[]{:S(2)}, u32[]{:S(2)}) collective-permute-start(bf16[512,512]{1,0:T(8,128)(2,1)S(1)} %copy-done.14), channel_id=1, source_target_pairs={{0,16},{8,24},{16,0},{24,8},{1,17},{9,25},{17,1},{25,9},{2,18},{10... | collective-permute-start | bytes 1572872 | tf_op jit(solution)/shard_map/ppermute | solution.py:528
  75.6 1.0 copy-start.18
  96.3 38.1 %collective-permute-start.14 = (f32[2048,128]{1,0:T(8,128)}, f32[2048,128]{1,0:T(8,128)S(1)}, u32[]{:S(2)}, u32[]{:S(2)}) collective-permute-start(f32[2048,128]{1,0:T(8,128)} %get-tuple-element.88), channel_id=1, source_target_pairs={{0,4},{4,0},{1,5},{5,1},{2,6},{6,2},{3,7},{7,3},{8,12},{12,8},{9,1... | collective-permute-start | bytes 3145736 | tf_op jit(solution)/shard_map/ppermute | solution.py:525
  96.4 37.4 %collective-permute-start.18 = (bf16[512,512]{1,0:T(8,128)(2,1)S(1)}, bf16[512,512]{1,0:T(8,128)(2,1)S(1)}, u32[]{:S(2)}, u32[]{:S(2)}) collective-permute-start(bf16[512,512]{1,0:T(8,128)(2,1)S(1)} %get-tuple-element.101), channel_id=1, source_target_pairs={{0,24},{8,16},{16,8},{24,0},{1,25},{9,17},{17,9},{25,1},{2,26},{10... | collective-permute-start | bytes 1572872 | tf_op jit(solution)/shard_map/ppermute | solution.py:528
  96.8 45.0 %collective-permute-start.15 = (f32[2048,128]{1,0:T(8,128)}, f32[2048,128]{1,0:T(8,128)S(1)}, u32[]{:S(2)}, u32[]{:S(2)}) collective-permute-start(f32[2048,128]{1,0:T(8,128)} %get-tuple-element.89), channel_id=1, source_target_pairs={{0,4},{4,0},{1,5},{5,1},{2,6},{6,2},{3,7},{7,3},{8,12},{12,8},{9,1... | collective-permute-start | bytes 3145736 | tf_op jit(solution)/shard_map/ppermute | solution.py:525
  116.8 24.9 %copy-start.19 = (bf16[512,512]{1,0:T(8,128)(2,1)}, bf16[512,512]{1,0:T(8,128)(2,1)S(1)}, u32[]{:S(2)}) copy-start(bf16[512,512]{1,0:T(8,128)(2,1)S(1)} %collective-permute-done.16.refs_5_.refs_13_) | copy-start | bytes 1572868
  116.8 16.9 %collective-permute-start.12 = (bf16[2048,128]{1,0:T(8,128)(2,1)}, bf16[2048,128]{1,0:T(8,128)(2,1)S(1)}, u32[]{:S(2)}, u32[]{:S(2)}) collective-permute-start(bf16[2048,128]{1,0:T(8,128)(2,1)} %get-tuple-element.84), channel_id=1, source_target_pairs={{0,4},{4,0},{1,5},{5,1},{2,6},{6,2},{3,7},{7,3},{8,12},{12,8},{9,1... | collective-permute-start | bytes 1572872 | tf_op jit(solution)/shard_map/ppermute | solution.py:525
  116.8 24.9 %copy-start.20 = (bf16[512,512]{1,0:T(8,128)(2,1)}, bf16[512,512]{1,0:T(8,128)(2,1)S(1)}, u32[]{:S(2)}) copy-start(bf16[512,512]{1,0:T(8,128)(2,1)S(1)} %collective-permute-done.17.refs_6_.refs_14_) | copy-start | bytes 1572868
  116.9 17.4 %collective-permute-start.13 = (bf16[2048,128]{1,0:T(8,128)(2,1)}, bf16[2048,128]{1,0:T(8,128)(2,1)S(1)}, u32[]{:S(2)}, u32[]{:S(2)}) collective-permute-start(bf16[2048,128]{1,0:T(8,128)(2,1)} %get-tuple-element.85), channel_id=1, source_target_pairs={{0,4},{4,0},{1,5},{5,1},{2,6},{6,2},{3,7},{7,3},{8,12},{12,8},{9,1... | collective-permute-start | bytes 1572872 | tf_op jit(solution)/shard_map/ppermute | solution.py:525
  133.7 8.0 %copy-start.21 = (bf16[512,512]{1,0:T(8,128)(2,1)}, bf16[512,512]{1,0:T(8,128)(2,1)S(1)}, u32[]{:S(2)}) copy-start(bf16[512,512]{1,0:T(8,128)(2,1)S(1)} %collective-permute-done.18.refs_7_.refs_15_) | copy-start | bytes 1572868
  133.7 8.5 %collective-permute-start.19 = (bf16[512,512]{1,0:T(8,128)(2,1)S(1)}, bf16[512,512]{1,0:T(8,128)(2,1)S(1)}, u32[]{:S(2)}, u32[]{:S(2)}) collective-permute-start(bf16[512,512]{1,0:T(8,128)(2,1)S(1)} %get-tuple-element.109.refs_4_.refs_12_), channel_id=1, source_target_pairs={{0,4},{4,0},{1,5},{5,1},{2,6},{6,2},{3,7},{7,3},{8,12},{12,8},{9,1... | collective-permute-start | bytes 1572872 | tf_op jit(solution)/shard_map/ppermute | solution.py:525
  133.8 8.5 %collective-permute-start.20 = (bf16[512,512]{1,0:T(8,128)(2,1)S(1)}, bf16[512,512]{1,0:T(8,128)(2,1)S(1)}, u32[]{:S(2)}, u32[]{:S(2)}) collective-permute-start(bf16[512,512]{1,0:T(8,128)(2,1)S(1)} %collective-permute-done.16.refs_5_.refs_13_), channel_id=1, source_target_pairs={{0,4},{4,0},{1,5},{5,1},{2,6},{6,2},{3,7},{7,3},{8,12},{12,8},{9,1... | collective-permute-start | bytes 1572872 | tf_op jit(solution)/shard_map/ppermute | solution.py:525
  134.3 8.0 %collective-permute-start.21 = (bf16[512,512]{1,0:T(8,128)(2,1)S(1)}, bf16[512,512]{1,0:T(8,128)(2,1)S(1)}, u32[]{:S(2)}, u32[]{:S(2)}) collective-permute-start(bf16[512,512]{1,0:T(8,128)(2,1)S(1)} %collective-permute-done.17.refs_6_.refs_14_), channel_id=1, source_target_pairs={{0,4},{4,0},{1,5},{5,1},{2,6},{6,2},{3,7},{7,3},{8,12},{12,8},{9,1... | collective-permute-start | bytes 1572872 | tf_op jit(solution)/shard_map/ppermute | solution.py:525
  134.3 9.6 %collective-permute-start.22 = (bf16[512,512]{1,0:T(8,128)(2,1)S(1)}, bf16[512,512]{1,0:T(8,128)(2,1)}, u32[]{:S(2)}, u32[]{:S(2)}) collective-permute-start(bf16[512,512]{1,0:T(8,128)(2,1)S(1)} %collective-permute-done.18.refs_7_.refs_15_), channel_id=1, source_target_pairs={{0,4},{4,0},{1,5},{5,1},{2,6},{6,2},{3,7},{7,3},{8,12},{12,8},{9,1... | collective-permute-start | bytes 1572872 | tf_op jit(solution)/shard_map/ppermute | solution.py:525
  135.9 1.2 copy-start.6
  137.1 1.2 copy-start.7
  138.4 1.0 copy-start.10
  139.4 2.4 copy-start.4
  139.4 2.4 copy-start.5
  142.2 0.9 copy-start.23
  159.1 46.7 %all-to-all-start.2 = ((bf16[16,128,384]{2,1,0:T(8,128)(2,1)}), bf16[16,128,384]{2,1,0:T(8,128)(2,1)S(1)}, u32[]{:S(2)}, u32[]{:S(2)}) async-start(bf16[16,128,384]{2,1,0:T(8,128)(2,1)} %bitcast.9), calls=%async_computation.2 | async-start | bytes 3145728 | tf_op jit(solution)/shard_map/all_to_all | solution.py:514
  166.6 37.0 %collective-permute-start.23 = (bf16[512,256]{1,0:T(8,128)(2,1)S(1)}, bf16[512,256]{1,0:T(8,128)(2,1)S(1)}, u32[]{:S(2)}, u32[]{:S(2)}) collective-permute-start(bf16[512,256]{1,0:T(8,128)(2,1)S(1)} %get-tuple-element.120), channel_id=1, source_target_pairs={{0,8},{8,0},{16,24},{24,16},{1,9},{9,1},{17,25},{25,17},{2,10},{10... | collective-permute-start | bytes 786440 | tf_op jit(solution)/shard_map/ppermute | solution.py:528
  168.6 35.0 %collective-permute-start.24 = (bf16[512,256]{1,0:T(8,128)(2,1)S(1)}, bf16[512,256]{1,0:T(8,128)(2,1)S(1)}, u32[]{:S(2)}, u32[]{:S(2)}) collective-permute-start(bf16[512,256]{1,0:T(8,128)(2,1)S(1)} %get-tuple-element.121), channel_id=1, source_target_pairs={{0,16},{8,24},{16,0},{24,8},{1,17},{9,25},{17,1},{25,9},{2,18},{10... | collective-permute-start | bytes 786440 | tf_op jit(solution)/shard_map/ppermute | solution.py:528
  170.1 33.5 %collective-permute-start.25 = (bf16[512,256]{1,0:T(8,128)(2,1)S(1)}, bf16[512,256]{1,0:T(8,128)(2,1)S(1)}, u32[]{:S(2)}, u32[]{:S(2)}) collective-permute-start(bf16[512,256]{1,0:T(8,128)(2,1)S(1)} %get-tuple-element.122), channel_id=1, source_target_pairs={{0,24},{8,16},{16,8},{24,0},{1,25},{9,17},{17,9},{25,1},{2,26},{10... | collective-permute-start | bytes 786440 | tf_op jit(solution)/shard_map/ppermute | solution.py:528
  205.8 1.1 copy-start.17
  206.9 3.9 %copy-start.32 = (bf16[2048,128]{1,0:T(8,128)(2,1)S(1)}, bf16[2048,128]{1,0:T(8,128)(2,1)}, u32[]{:S(2)}) copy-start(bf16[2048,128]{1,0:T(8,128)(2,1)} %get-tuple-element.133) | copy-start | bytes 1572868
  206.9 4.2 %copy-start.31 = (bf16[2048,128]{1,0:T(8,128)(2,1)S(1)}, bf16[2048,128]{1,0:T(8,128)(2,1)}, u32[]{:S(2)}) copy-start(bf16[2048,128]{1,0:T(8,128)(2,1)} %get-tuple-element.134) | copy-start | bytes 1572868
  206.9 6.6 %copy-start.8 = (bf16[2048,128]{1,0:T(8,128)(2,1)S(1)}, bf16[2048,128]{1,0:T(8,128)(2,1)}, u32[]{:S(2)}) copy-start(bf16[2048,128]{1,0:T(8,128)(2,1)} %get-tuple-element.131.mine_k_ref) | copy-start | bytes 1572868
  206.9 6.6 %copy-start.9 = (bf16[2048,128]{1,0:T(8,128)(2,1)S(1)}, bf16[2048,128]{1,0:T(8,128)(2,1)}, u32[]{:S(2)}) copy-start(bf16[2048,128]{1,0:T(8,128)(2,1)} %get-tuple-element.132.mine_v_ref) | copy-start | bytes 1572868
  206.9 74.7 %all-to-all-start.3 = ((bf16[32,128,384]{2,1,0:T(8,128)(2,1)}), bf16[32,128,384]{2,1,0:T(8,128)(2,1)}, u32[]{:S(2)}, u32[]{:S(2)}) async-start(bf16[32,128,384]{2,1,0:T(8,128)(2,1)} %bitcast.24), calls=%async_computation.3 | async-start | bytes 6291456 | tf_op jit(solution)/shard_map/all_to_all | solution.py:514
  210.8 2.0 collective-permute-start.26
  211.1 2.5 collective-permute-start.27
  213.6 56.4 %copy-start.12 = (s32[4]{0:T(128)S(1)}, s32[4]{0:T(128)}, u32[]{:S(2)}) copy-start(s32[4]{0:T(128)} %copy-done.11) | copy-start | bytes 52
  215.2 35.9 %collective-permute-start.28 = (bf16[512,512]{1,0:T(8,128)(2,1)}, bf16[512,512]{1,0:T(8,128)(2,1)S(1)}, u32[]{:S(2)}, u32[]{:S(2)}) collective-permute-start(bf16[512,512]{1,0:T(8,128)(2,1)} %get-tuple-element.136), channel_id=1, source_target_pairs={{0,8},{8,0},{16,24},{24,16},{1,9},{9,1},{17,25},{25,17},{2,10},{10... | collective-permute-start | bytes 1572872 | tf_op jit(solution)/shard_map/ppermute | solution.py:528
  216.9 34.2 %collective-permute-start.29 = (bf16[512,512]{1,0:T(8,128)(2,1)}, bf16[512,512]{1,0:T(8,128)(2,1)S(1)}, u32[]{:S(2)}, u32[]{:S(2)}) collective-permute-start(bf16[512,512]{1,0:T(8,128)(2,1)} %get-tuple-element.137), channel_id=1, source_target_pairs={{0,16},{8,24},{16,0},{24,8},{1,17},{9,25},{17,1},{25,9},{2,18},{10... | collective-permute-start | bytes 1572872 | tf_op jit(solution)/shard_map/ppermute | solution.py:528
  218.4 51.6 %collective-permute-start.30 = (bf16[512,512]{1,0:T(8,128)(2,1)}, bf16[512,512]{1,0:T(8,128)(2,1)S(1)}, u32[]{:S(2)}, u32[]{:S(2)}) collective-permute-start(bf16[512,512]{1,0:T(8,128)(2,1)} %get-tuple-element.138), channel_id=1, source_target_pairs={{0,24},{8,16},{16,8},{24,0},{1,25},{9,17},{17,9},{25,1},{2,26},{10... | collective-permute-start | bytes 1572872 | tf_op jit(solution)/shard_map/ppermute | solution.py:528
  (4 other events, 3.2 us)
